TPU v7x, 32 devices: a whole 2x2x4 slice. The times are simulated.
32 devices in a mesh: row: 4 (over z), col: 8 (over y, x, core).
Axes of the slice: x: 2, y: 2, z: 4, core: 2. Of those that a mesh axis runs over, the one named last changes fastest.
Arguments:
- query_tokens: bfloat16 [128, 32, 128], P('row'), may hold values from -14 to 14
- query_lengths: int32 [128], P('row'), may hold values from 8 to 32
- passage_tokens: bfloat16 [1024, 176, 128], P(('col', 'row')), may hold values from -8 to 8
- passage_lengths: int32 [1024], P(('col', 'row')), may hold values from 44 to 176
- student_queries: bfloat16 [128, 768], P('row', 'col'), may hold values from -28 to 28
- student_passages: bfloat16 [1024, 768], P('col', 'row'), may hold values from -0.21875 to 0.21875
- positives: int32 [128], P('row'), may hold values from 0 to 1023
Outputs:
- query_grads: float32 [128, 768], P('row', 'col')
- passage_grads: float32 [1024, 768], P('col', 'row')
- loss: float32 [], replicated
All inputs are finite; a program needn't handle non-finite values.
Results may differ from a plain program's by a relative error of at most 0.00045.
Values may be sent and summed in bfloat16 or wider, within the bound.
No kernel may reach another device: no remote copies, remote signals or barrier semaphores. Data moves between devices by JAX's collectives and lax.ppermute only.
A program may use at most 64 MiB of HBM per device.

v0:
```python
import functools

import jax
import jax.numpy as jnp
from jax import lax
from jax.experimental import pallas as pl
from jax.experimental.pallas import tpu as pltpu
from jax.sharding import PartitionSpec as P

NEG = -1e30
SCALE = 4.0
TILE = 16
GROUP = 32
LANES = 128


def params(megabytes):
    return pltpu.CompilerParams(vmem_limit_bytes=megabytes * 1024 * 1024)


def vmem():
    return pl.BlockSpec(memory_space=pltpu.VMEM)


def place():
    return pl.BlockSpec(memory_space=pl.ANY)


def smem():
    return pl.BlockSpec(memory_space=pltpu.SMEM)


def split(x, parts):
    out = []
    for _ in range(parts):
        piece = x.astype(jnp.bfloat16)
        out.append(piece)
        x = x - piece.astype(jnp.float32)
    return out


def mxu(a, b, dims=((1,), (0,))):
    return lax.dot_general(a, b, (dims, ((), ())), preferred_element_type=jnp.float32)


def prepare_kernel(
    slots, per, tokens_ref, lives_ref, lengths_ref, sq_ref, sp_ref, pos_ref, sent_ref, blocks_ref
):
    c = lax.axis_index("col")
    half = tokens_ref.shape[0] // 2
    width = tokens_ref.shape[2]
    slot = lax.broadcasted_iota(jnp.int32, (slots, width), 0)
    some = LANES // slots
    for j in range(half // some):
        values = []
        for q in range(some):
            at = (c % 2) * half + j * some + q
            value = tokens_ref[at].astype(jnp.float32)
            values.append(jnp.where(slot < lives_ref[at], value, 0.0))
        flipped = jnp.concatenate(values, axis=0).T
        sent_ref[j * width : (j + 1) * width, :] = flipped.astype(jnp.bfloat16)
    passages = lengths_ref.shape[0]

    def entries(p, at):
        for b in range(per):
            live = jnp.minimum(lengths_ref[p] - b * TILE, TILE) - 1
            blocks_ref[at + b] = p * TILE * TILE + b * TILE + live
        return at + lax.shift_right_logical(lengths_ref[p] + TILE - 1, 4)

    count = lax.fori_loop(0, passages, entries, 0)
    final = blocks_ref[count - 1]
    for i in range(GROUP):
        blocks_ref[count + i] = final
    blocks_ref[blocks_ref.shape[0] - 1] = count
    block, wide = sq_ref.shape
    base = half // some * width
    depth = sp_ref.shape[0]
    vectors = jnp.concatenate([sq_ref[...].astype(jnp.float32), jnp.zeros((block, LANES - wide), jnp.float32)], axis=1)
    line = lax.broadcasted_iota(jnp.int32, (block, LANES), 0)
    lane = lax.broadcasted_iota(jnp.int32, (block, LANES), 1)
    place = jnp.zeros((block, LANES), jnp.int32)
    for q in range(block):
        place = jnp.where(line == q, pos_ref[q], place)
    high, low = lax.shift_right_logical(place, 6), place & 63
    vectors = jnp.where(lane == wide, high.astype(jnp.float32), vectors)
    vectors = jnp.where(lane == wide + 1, low.astype(jnp.float32), vectors).astype(jnp.bfloat16)
    sent_ref[base : base + depth] = sp_ref[...]
    sent_ref[base + depth :] = vectors


def prepare(tokens, lives, cells, lengths, sq, sp, pos):
    per = cells.shape[0] // lengths.shape[0]
    block, slots, width = tokens.shape
    base = block // 2 * slots // LANES * width
    return pl.pallas_call(
        functools.partial(prepare_kernel, slots, per),
        out_shape=(
            jax.ShapeDtypeStruct((base + sp.shape[0] + block, LANES), jnp.bfloat16),
            jax.ShapeDtypeStruct((cells.shape[0] + TILE + GROUP + 1,), jnp.int32),
        ),
        in_specs=[vmem(), smem(), smem(), vmem(), vmem(), smem()],
        out_specs=(vmem(), smem()),
        compiler_params=params(56),
    )(tokens, lives, lengths, sq, sp, pos)


def teacher_kernel(slots, tasks, shifts, sides, priors, *refs):
    query_refs = dict(zip(shifts, refs))
    refs = refs[len(shifts) :]
    token_refs = dict(zip(sides, refs))
    list_refs = dict(zip(sides, refs[len(sides) :]))
    prior_refs = refs[2 * len(sides) : 2 * len(sides) + priors]
    out_ref, best = refs[-2:]
    passages, lanes = out_ref.shape
    width = token_refs[sides[0]].shape[2]
    r, c = lax.axis_index("row"), lax.axis_index("col")
    rows = lanes // 2 // lax.axis_size("row") * slots
    total = sum([ref[...] for ref in prior_refs], jnp.zeros((passages, lanes), jnp.float32))
    line = lax.broadcasted_iota(jnp.int32, (TILE, width), 0)
    for side, used in tasks:
        tokens_ref, blocks_ref = token_refs[side], list_refs[side]
        per = tokens_ref.shape[0] // passages
        count = blocks_ref[blocks_ref.shape[0] - 1]
        cells = [(query_refs[k], j) for k in used for j in range(rows // LANES)]

        def step(i, carry, tokens_ref=tokens_ref, blocks_ref=blocks_ref, per=per, cells=cells):
            carry = list(carry)
            owner, fresh, values = [], [], []
            for g in range(GROUP):
                entry = blocks_ref[i * GROUP + g]
                p, b = lax.shift_right_logical(entry, 8), lax.shift_right_logical(entry, 4) & (TILE - 1)
                owner.append(pl.multiple_of(p * 8, 8))
                fresh.append(b == 0)
                value = tokens_ref[p * per + b].astype(jnp.float32)
                value = jnp.where(line <= (entry & (TILE - 1)), value, value[0:1, :])
                values.append(value.astype(jnp.bfloat16))
            block = jnp.concatenate(values, axis=0)
            for n in range(0, len(cells), 2):
                pair = [ref[j * width : (j + 1) * width, :] for ref, j in cells[n : n + 2]]
                sims = mxu(block, jnp.concatenate(pair, axis=1))
                for g in range(GROUP):
                    for l in range(2):
                        top = sims[g * TILE : g * TILE + 8, l * LANES : (l + 1) * LANES]
                        low = sims[g * TILE + 8 : g * TILE + 16, l * LANES : (l + 1) * LANES]
                        kept = jnp.where(fresh[g], NEG, carry[n + l])
                        carry[n + l] = jnp.maximum(kept, jnp.maximum(top, low))
                        best[n + l, pl.ds(owner[g], 8), :] = carry[n + l]
            return tuple(carry)

        lax.fori_loop(
            0,
            lax.shift_right_logical(count + GROUP - 1, GROUP.bit_length() - 1),
            step,
            tuple(jnp.full((8, LANES), NEG, jnp.float32) for _ in cells),
        )
        found = []
        for l in range(len(cells)):
            peak = best[l, pl.ds(0, passages, stride=8), :]
            for s in range(1, 8):
                peak = jnp.maximum(peak, best[l, pl.ds(s, passages, stride=8), :])
            found.append(peak)
        parity = c % 2 if side == 0 else 1 - c % 2
        for n, k in enumerate(used):
            some = rows // LANES
            peaks = jnp.concatenate(found[n * some : (n + 1) * some], axis=1)
            start = parity * (lanes // 2) + (r ^ k) * (rows // slots)
            owner = lax.broadcasted_iota(jnp.int32, (rows, lanes), 0) // slots + start
            member = (owner == lax.broadcasted_iota(jnp.int32, (rows, lanes), 1)).astype(jnp.bfloat16)
            for piece in split(peaks, 3):
                total = total + mxu(piece, member)
    out_ref[...] = total


def teacher(slots, tasks, near, tokens, lists, queries, passages, priors=(), after=(), megabytes=16):
    shifts = sorted({k for _, used in tasks for k in used})
    sides = sorted({side for side, _ in tasks})
    operands = [near[k] for k in shifts] + [tokens[i] for i in sides] + [lists[i] for i in sides]
    specs = [vmem()] * (len(shifts) + len(sides)) + [smem()] * len(sides)
    operands += list(priors) + list(after)
    specs += [vmem()] * len(priors)
    specs += [place()] * len(after)
    most = max(len(used) for _, used in tasks)
    size = tokens[0].size
    rows = queries // 2 // lax.axis_size("row") * slots
    return pl.pallas_call(
        functools.partial(teacher_kernel, slots, tasks, shifts, sides, len(priors)),
        out_shape=jax.ShapeDtypeStruct((passages, queries), jnp.float32),
        in_specs=specs,
        out_specs=vmem(),
        scratch_shapes=[pltpu.VMEM((most * rows // LANES, passages * 8, LANES), jnp.float32)],
        compiler_params=params(megabytes),
        cost_estimate=pl.CostEstimate(
            flops=sum(4 * rows * len(used) * size for _, used in tasks),
            bytes_accessed=2 * size * len(sides),
            transcendentals=0,
        ),
    )(*operands)


def pack_kernel(axis, first, count, pieces, *refs):
    out_ref, token_ref = refs[-2:]
    me = lax.axis_index("row") if axis == "row" else lax.axis_index("col") // 2
    for k, ref in enumerate(refs[:pieces]):
        out_ref[me ^ k] = ref[first : first + count]
    token_ref[...] = jnp.zeros(token_ref.shape, jnp.float32)


def pack(axis, pieces, first, count, after):
    shape = (len(pieces), count) + pieces[0].shape[1:]
    return pl.pallas_call(
        functools.partial(pack_kernel, axis, first, count, len(pieces)),
        out_shape=(jax.ShapeDtypeStruct(shape, pieces[0].dtype), jax.ShapeDtypeStruct((8, LANES), jnp.float32)),
        in_specs=[vmem()] * len(pieces) + [place()] * len(after),
        out_specs=(vmem(), vmem()),
        compiler_params=params(24),
    )(*pieces, *after)


def loop(count, body, init):
    if count > 4:
        return lax.fori_loop(0, count, body, init)
    for i in range(count):
        init = body(i, init)
    return init


def student_kernel(
    wide, mine_ref, other_ref, after_ref, score_ref, slope_ref, vectors_ref, stats_ref, held, flat
):
    pairs, R, rows, span = mine_ref.shape
    C = 2 * pairs
    r, c = lax.axis_index("row"), lax.axis_index("col")
    queries = score_ref.shape[2]
    block = queries // R
    half = block // 2
    depth = rows - block
    per = depth // wide
    sides = ((mine_ref, c % 2), (other_ref, 1 - c % 2))
    for j in range(pairs):
        for ref, odd in sides:
            for i in range(R):
                for x in range(2):
                    held[2 * j + odd, x, i] = ref[j, i, depth + x * half : depth + (x + 1) * half]

    def columns(index):
        return held[index].reshape(queries, span).astype(jnp.float32)

    for i in range(R):
        pieces = [columns(i * per + h)[:, :wide] for h in range(per)]
        flat[i] = jnp.concatenate(pieces, axis=1).astype(jnp.bfloat16)
    vectors_ref[...] = flat[r]
    meta = columns(c)
    where = meta[:, wide : wide + 1] * 64.0 + meta[:, wide + 1 : wide + 2]
    diag = lax.broadcasted_iota(jnp.int32, (queries, queries), 0) == lax.broadcasted_iota(
        jnp.int32, (queries, queries), 1
    )
    spot = jnp.sum(jnp.where(diag, where, 0.0), axis=0, keepdims=True).astype(jnp.int32)
    index = lax.broadcasted_iota(jnp.int32, (span, queries), 0)

    def scores(j, carry):
        peak, score = carry
        for ref, odd in sides:
            total = jnp.zeros((queries, span), jnp.float32)
            for k in range(R):
                total = total + mxu(flat[k], ref[j, k, :depth])
            s = (SCALE * total).T
            i = 2 * j + odd
            score_ref[i] = s
            hot = index + i * span == spot
            peak, score = jnp.maximum(peak, s), score + jnp.where(hot, s, 0.0)
        return peak, score

    low = jnp.full((span, queries), -jnp.inf, jnp.float32)
    zero = jnp.zeros((span, queries), jnp.float32)
    peak, score = loop(pairs, scores, (low, zero))
    peak = jnp.max(peak, axis=0, keepdims=True)
    score = jnp.sum(score, axis=0, keepdims=True)

    def powers(j, total):
        for i in (2 * j, 2 * j + 1):
            power = jnp.exp(score_ref[i] - peak)
            slope_ref[i] = power
            total = total + power
        return total

    total = jnp.sum(loop(pairs, powers, zero), axis=0, keepdims=True)
    stats_ref[0:1, :] = peak + jnp.log(total)
    stats_ref[1:2, :] = score
    stats_ref[2:8, :] = jnp.zeros((6, queries), jnp.float32)
    factor = SCALE / queries
    scale = 2.0 * factor / total

    def slopes(j, carry):
        for i in (2 * j, 2 * j + 1):
            hot = index + i * span == spot
            slope_ref[i] = slope_ref[i] * scale - jnp.where(hot, factor, 0.0)
        return carry

    loop(pairs, slopes, 0)


def student_scores(mine, other, after, queries, wide):
    pairs, R, rows, span = mine.shape
    depth = rows - queries // R
    C = 2 * pairs
    return pl.pallas_call(
        functools.partial(student_kernel, wide),
        out_shape=(
            jax.ShapeDtypeStruct((C, span, queries), jnp.float32),
            jax.ShapeDtypeStruct((C, span, queries), jnp.float32),
            jax.ShapeDtypeStruct((queries, depth), jnp.bfloat16),
            jax.ShapeDtypeStruct((8, queries), jnp.float32),
        ),
        in_specs=[vmem(), vmem(), place()],
        out_specs=(vmem(),) * 4,
        scratch_shapes=[
            pltpu.VMEM((C, 2, R, queries // R // 2, span), jnp.bfloat16),
            pltpu.VMEM((R, queries, depth), jnp.bfloat16),
        ],
        compiler_params=params(40),
    )(mine, other, after)


def finish_kernel(
    wide,
    t_mine,
    t_other,
    s_ref,
    slope_ref,
    mine_ref,
    other_ref,
    vectors_ref,
    stats_ref,
    query_ref,
    passage_ref,
    loss_ref,
    teach,
):
    pairs, R, rows, span = mine_ref.shape
    r, c = lax.axis_index("row"), lax.axis_index("col")
    queries = vectors_ref.shape[0]
    depth = vectors_ref.shape[1]
    per = depth // wide
    block = queries // R
    half = queries // 2
    shape = (span, queries)
    odd = c % 2
    s_lse, score = stats_ref[0:1, :], stats_ref[1:2, :]

    def peak(j, t_max):
        a, b = t_mine[j].reshape(shape), t_other[j].reshape(shape)
        pair = [jnp.where(odd == 0, a, b), jnp.where(odd == 0, b, a)]
        for x in range(2):
            t = jnp.concatenate([v[:, x * half : (x + 1) * half] for v in pair], axis=1)
            teach[2 * j + x] = t
            t_max = jnp.maximum(t_max, t)
        return t_max

    t_max = loop(pairs, peak, jnp.full(shape, -jnp.inf, jnp.float32))
    t_max = jnp.max(t_max, axis=0, keepdims=True)

    def totals(j, carry):
        t_sum, cross = carry
        for i in (2 * j, 2 * j + 1):
            t = teach[i]
            t_exp = jnp.exp(t - t_max)
            teach[i] = t_exp
            t_sum, cross = t_sum + t_exp, cross + t_exp * (t - s_ref[i])
        return t_sum, cross

    zero = jnp.zeros(shape, jnp.float32)
    t_sum, cross = loop(pairs, totals, (zero, zero))
    t_sum = jnp.sum(t_sum, axis=0, keepdims=True)
    cross = jnp.sum(cross, axis=0, keepdims=True)
    each = cross / t_sum - (t_max + jnp.log(t_sum)) + 2.0 * s_lse - score
    loss_ref[...] = jnp.sum(each, axis=1, keepdims=True) / queries
    t_factor = SCALE / queries / t_sum

    def slope(i):
        return split(slope_ref[i] - teach[i] * t_factor, 2)

    def gradient(j, total):
        for ref, side in ((mine_ref, odd), (other_ref, 1 - odd)):
            vectors = ref[j, c // per, :depth]
            for piece in slope(2 * j + side):
                total = total + mxu(vectors, piece)
        return total

    flat = loop(pairs, gradient, jnp.zeros((depth, queries), jnp.float32)).T
    sub = block // 2
    for h in range(2):
        lines = functools.reduce(
            jnp.add,
            [jnp.where(r == i, flat[h * half + i * sub : h * half + (i + 1) * sub], 0.0) for i in range(R)],
        )
        query_ref[h * sub : (h + 1) * sub, :] = functools.reduce(
            jnp.add, [jnp.where(c % per == i, lines[:, i * wide : (i + 1) * wide], 0.0) for i in range(per)]
        )
    grads = sum(mxu(piece, vectors_ref[...]) for piece in slope(c))
    passage_ref[...] = grads.T


def finish(t_mine, t_other, s, slope, mine, other, vectors, stats, wide):
    pairs, R, rows, span = mine.shape
    queries, depth = vectors.shape
    return pl.pallas_call(
        functools.partial(finish_kernel, wide),
        out_shape=(
            jax.ShapeDtypeStruct((queries // R, wide), jnp.float32),
            jax.ShapeDtypeStruct((depth, span), jnp.float32),
            jax.ShapeDtypeStruct((1, 1), jnp.float32),
        ),
        in_specs=[vmem()] * 8,
        out_specs=(vmem(),) * 3,
        scratch_shapes=[pltpu.VMEM((2 * pairs, span, queries), jnp.float32)],
        compiler_params=params(48),
    )(t_mine, t_other, s, slope, mine, other, vectors, stats)


def shards(query_tokens, query_lengths, passage_tokens, passage_lengths, student_queries, student_passages, positives):
    R, C = lax.axis_size("row"), lax.axis_size("col")
    block, slots, width = query_tokens.shape
    queries = block * R
    local, count = passage_tokens.shape[:2]
    wide = student_queries.shape[1]

    def over_row(x, k):
        return lax.ppermute(x, "row", [(i, i ^ k) for i in range(R)])

    def over_col(x, k):
        return lax.ppermute(x, "col", [(i, i ^ k) for i in range(C)])

    def spread(stack, after):
        parts = [stack] + [over_col(stack, k) for k in range(2, C, 2)]
        mine, _ = pack("col", parts, 0, stack.shape[0], after)
        return mine, over_col(mine, 1)

    cells = passage_tokens.reshape(local * count // TILE, TILE, width)
    tokens = [cells, over_col(cells, 1)]
    sent, blocks = prepare(
        query_tokens, query_lengths, cells, passage_lengths, student_queries, student_passages.T, positives
    )
    lists = [blocks, over_col(blocks, 1)]
    near = [sent] + [over_row(sent, k) for k in range(1, R)]
    common = dict(near=near, tokens=tokens, lists=lists, queries=queries, passages=local)
    score = teacher(slots, ((0, (0,)),), **common)
    score = teacher(slots, ((1, (0, 1)), (0, (1,))), priors=(score,), **common)
    for k in range(2, R - 2, 2):
        score = teacher(slots, ((0, (k, k + 1)), (1, (k, k + 1))), priors=(score,), **common)
    score = teacher(slots, ((0, (R - 2,)), (1, (R - 2,))), priors=(score,), **common)
    base = sent.shape[0] - student_passages.shape[1] - block
    vectors, token = pack("row", near, base, sent.shape[0] - base, (score,))
    score = teacher(slots, ((0, (R - 1,)), (1, (R - 1,))), priors=(score,), after=(token,), **common)
    scores = [score] + [over_row(score, k) for k in range(1, R)]
    mine, other = spread(vectors, (scores[1],))
    stack, token = pack("row", scores, 0, local, ())
    s, slope, vectors, stats = student_scores(mine, other, token, queries, wide)
    t_mine, t_other = spread(stack, ())
    query_grads, passage_grads, loss = finish(t_mine, t_other, s, slope, mine, other, vectors, stats, wide)
    return (query_grads, passage_grads.T, loss[0, 0])


def solution(mesh):
    return jax.shard_map(
        shards,
        mesh=mesh,
        in_specs=(
            P("row", None, None),
            P("row"),
            P(("col", "row"), None, None),
            P(("col", "row")),
            P("row", "col"),
            P("col", "row"),
            P("row"),
        ),
        out_specs=(P("row", "col"), P("col", "row"), P()),
        check_vma=False,
    )
```

profile of v0, /device:TPU:0, one launch (start us, length us, event | category | flops | bytes accessed | tf_op | source)
XLA Modules:
  0.0 63.7 jit_solution(1216513827639737817)
XLA Ops:
  0.6 0.5 collective-permute-start.1
  1.1 2.8 %shard_map.94 = (bf16[736,128]{1,0:T(8,128)(2,1)}, s32[401]{0:T(512)}) custom-call(bf16[32,32,128]{2,1,0:T(8,128)(2,1)} %tokens_ref.1, s32[32]{0:T(128)} %lives_ref.1, s32[32]{0:T(128)} %lengths_ref.1, bf16[32,96]{1,0:T(8,128)(2,1)} %sq_ref.1, bf16[192,128]{1,0:T(8,128)(2,1)} %bitcast.9, s32[32]{0:T(128)} %pos_ref.1), custom_call_target="tpu_custom_call" | custom-call | tf_op jit(solution)/shard_map/pallas_call | solution.py:95
  4.0 2.7 %collective-permute-start.4 = (bf16[736,128]{1,0:T(8,128)(2,1)}, bf16[736,128]{1,0:T(8,128)(2,1)S(1)}, u32[]{:S(2)}, u32[]{:S(2)}) collective-permute-start(bf16[736,128]{1,0:T(8,128)(2,1)} %get-tuple-element.18.refs_0_), channel_id=1, source_target_pairs={{0,8},{8,0},{16,24},{24,16},{1,9},{9,1},{17,25},{25,17},{2,10},{10... | collective-permute-start | bytes 565256 | tf_op jit(solution)/shard_map/ppermute | solution.py:428
  6.6 2.6 %collective-permute-start.3 = (bf16[736,128]{1,0:T(8,128)(2,1)}, bf16[736,128]{1,0:T(8,128)(2,1)S(1)}, u32[]{:S(2)}, u32[]{:S(2)}) collective-permute-start(bf16[736,128]{1,0:T(8,128)(2,1)} %get-tuple-element.18.refs_0_), channel_id=1, source_target_pairs={{0,16},{8,24},{16,0},{24,8},{1,17},{9,25},{17,1},{25,9},{2,18},{10... | collective-permute-start | bytes 565256 | tf_op jit(solution)/shard_map/ppermute | solution.py:428
  9.2 0.0 collective-permute-start
  9.2 0.0 collective-permute-start.2
  9.2 1.0 %copy-done = bf16[736,128]{1,0:T(8,128)(2,1)S(1)} copy-done((bf16[736,128]{1,0:T(8,128)(2,1)S(1)}, bf16[736,128]{1,0:T(8,128)(2,1)}, u32[]{:S(2)}) %copy-start) | copy-done | bytes 188440
  10.2 1.4 %copy-done.2 = bf16[32,176,128]{2,1,0:T(8,128)(2,1)S(1)} copy-done((bf16[32,176,128]{2,1,0:T(8,128)(2,1)S(1)}, bf16[32,176,128]{2,1,0:T(8,128)(2,1)}, u32[]{:S(2)}) %copy-start.2) | copy-done | bytes 1441816
  11.6 0.7 %copy-done.4 = s32[401]{0:T(512)S(1)} copy-done((s32[401]{0:T(512)S(1)}, s32[401]{0:T(512)}, u32[]{:S(2)}) %copy-start.4) | copy-done | bytes 1628
  12.2 3.4 %shard_map.95.refs_6_ = f32[32,128]{1,0:T(8,128)S(1)} custom-call(bf16[736,128]{1,0:T(8,128)(2,1)S(1)} %copy-done, bf16[352,16,128]{2,1,0:T(8,128)(2,1)S(1)} %bitcast.5, s32[401]{0:T(512)S(1)} %copy-done.4), custom_call_target="tpu_custom_call" | custom-call | flops 1476395008 | bytes 1441792 | tf_op jit(solution)/shard_map/pallas_call | solution.py:185
  15.6 0.0 copy-start.3
  15.6 0.0 collective-permute-done.2.refs_5_.refs_4_
  15.7 0.2 collective-permute-done.4.refs_1_
  15.8 0.0 collective-permute-done.1.refs_3_.refs_2_
  15.8 7.5 %shard_map.96.refs_5_ = f32[32,128]{1,0:T(8,128)S(1)} custom-call(bf16[736,128]{1,0:T(8,128)(2,1)S(1)} %copy-done, bf16[736,128]{1,0:T(8,128)(2,1)S(1)} %collective-permute-done.4.refs_1_, bf16[352,16,128]{2,1,0:T(8,128)(2,1)S(1)} %bitcast.6, bf16[352,16,128]{2,1,0:T(8,128)(2,1)S(1)} %collective-permute-done.1.refs_3_.refs_2_, s32[401]{0:T(512)S(1)} %copy-done.4, ...), custom_call_target="tpu_custom_call" | custom-call | flops 4429185024 | bytes 2883584 | tf_op jit(solution)/shard_map/pallas_call | solution.py:185
  23.4 0.0 copy-start.1
  23.4 0.0 copy-start.5
  23.4 0.0 collective-permute-done.3.refs_0_.refs_2_
  23.4 0.0 copy-done.3
  23.4 6.2 %shard_map.97.refs_4_.refs_5_ = f32[32,128]{1,0:T(8,128)S(1)} custom-call(bf16[736,128]{1,0:T(8,128)(2,1)S(1)} %collective-permute-done.3.refs_0_.refs_2_, bf16[352,16,128]{2,1,0:T(8,128)(2,1)S(1)} %bitcast.7, bf16[352,16,128]{2,1,0:T(8,128)(2,1)S(1)} %collective-permute-done.1.refs_3_.refs_2_, s32[401]{0:T(512)S(1)} %copy-done.4, ...), custom_call_target="tpu_custom_call" | custom-call | flops 2952790016 | bytes 2883584 | tf_op jit(solution)/shard_map/pallas_call | solution.py:185
  29.6 0.0 collective-permute-done.refs_3_.refs_0_
  29.7 2.7 %collective-permute-start.14 = (bf16[4,224,128]{2,1,0:T(8,128)(2,1)S(1)}, bf16[4,224,128]{2,1,0:T(8,128)(2,1)S(1)}, u32[]{:S(2)}, u32[]{:S(2)}) collective-permute-start(bf16[4,224,128]{2,1,0:T(8,128)(2,1)S(1)} %get-tuple-element.23.refs_0_), channel_id=1, source_target_pairs={{0,6},{1,7},{2,4},{3,5},{4,2},{5,3},{6,0},{7,1},{8,14},{9,15},{10,... | collective-permute-start | bytes 688136 | tf_op jit(solution)/shard_map/ppermute | solution.py:431
  32.4 0.5 collective-permute-start.13
  32.9 0.4 collective-permute-start.12
  33.3 6.2 %shard_map.99.refs_0_ = f32[32,128]{1,0:T(8,128)S(1)} custom-call(bf16[736,128]{1,0:T(8,128)(2,1)S(1)} %collective-permute-done.refs_3_.refs_0_, bf16[352,16,128]{2,1,0:T(8,128)(2,1)S(1)} %bitcast.8, bf16[352,16,128]{2,1,0:T(8,128)(2,1)S(1)} %collective-permute-done.1.refs_3_.refs_2_, s32[401]{0:T(512)S(1)} %copy-done.5, ...), custom_call_target="tpu_custom_call" | custom-call | flops 2952790016 | bytes 2883584 | tf_op jit(solution)/shard_map/pallas_call | solution.py:185
  39.5 1.2 %collective-permute-start.5 = (f32[32,128]{1,0:T(8,128)S(1)}, f32[32,128]{1,0:T(8,128)S(1)}, u32[]{:S(2)}, u32[]{:S(2)}) collective-permute-start(f32[32,128]{1,0:T(8,128)S(1)} %shard_map.99.refs_0_), channel_id=1, source_target_pairs={{0,8},{8,0},{16,24},{24,16},{1,9},{9,1},{17,25},{25,17},{2,10},{10... | collective-permute-start | bytes 49160 | tf_op jit(solution)/shard_map/ppermute | solution.py:428
  40.7 2.6 %collective-permute-done.5.refs_1_.refs_4_ = f32[32,128]{1,0:T(8,128)S(1)} collective-permute-done((f32[32,128]{1,0:T(8,128)S(1)}, f32[32,128]{1,0:T(8,128)S(1)}, u32[]{:S(2)}, u32[]{:S(2)}) %collective-permute-start.5) | collective-permute-done | bytes 16416 | tf_op jit(solution)/shard_map/ppermute | solution.py:428
  43.3 0.0 collective-permute-done.14.refs_3_
  43.3 0.1 collective-permute-done.13.refs_2_
  43.4 0.3 collective-permute-done.12.refs_1_
  43.7 0.7 %shard_map.102 = (bf16[4,4,224,128]{3,2,1,0:T(8,128)(2,1)S(1)}, f32[8,128]{1,0:T(8,128)}) custom-call(bf16[4,224,128]{2,1,0:T(8,128)(2,1)S(1)} %get-tuple-element.23.refs_0_, bf16[4,224,128]{2,1,0:T(8,128)(2,1)S(1)} %collective-permute-done.12.refs_1_, bf16[4,224,128]{2,1,0:T(8,128)(2,1)S(1)} %collective-permute-done.13.refs_2_, ...), custom_call_target="tpu_custom_call" | custom-call | tf_op jit(solution)/shard_map/pallas_call | solution.py:210
  44.4 0.0 collective-permute-start.15
  44.4 4.5 %collective-permute-start.7 = (f32[32,128]{1,0:T(8,128)S(1)}, f32[32,128]{1,0:T(8,128)S(1)}, u32[]{:S(2)}, u32[]{:S(2)}) collective-permute-start(f32[32,128]{1,0:T(8,128)S(1)} %shard_map.99.refs_0_), channel_id=1, source_target_pairs={{0,24},{8,16},{16,8},{24,0},{1,25},{9,17},{17,9},{25,1},{2,26},{10... | collective-permute-start | bytes 49160 | tf_op jit(solution)/shard_map/ppermute | solution.py:428
  48.9 0.0 collective-permute-start.6
  48.9 1.7 %collective-permute-done.7.refs_3_ = f32[32,128]{1,0:T(8,128)S(1)} collective-permute-done((f32[32,128]{1,0:T(8,128)S(1)}, f32[32,128]{1,0:T(8,128)S(1)}, u32[]{:S(2)}, u32[]{:S(2)}) %collective-permute-start.7) | collective-permute-done | bytes 16416 | tf_op jit(solution)/shard_map/ppermute | solution.py:428
  50.6 2.9 %collective-permute-done.6.refs_2_ = f32[32,128]{1,0:T(8,128)S(1)} collective-permute-done((f32[32,128]{1,0:T(8,128)S(1)}, f32[32,128]{1,0:T(8,128)S(1)}, u32[]{:S(2)}, u32[]{:S(2)}) %collective-permute-start.6) | collective-permute-done | bytes 16416 | tf_op jit(solution)/shard_map/ppermute | solution.py:428
  53.5 1.6 %collective-permute-start.10 = (f32[4,32,128]{2,1,0:T(8,128)S(1)}, f32[4,32,128]{2,1,0:T(8,128)S(1)}, u32[]{:S(2)}, u32[]{:S(2)}) collective-permute-start(f32[4,32,128]{2,1,0:T(8,128)S(1)} %get-tuple-element.21.refs_0_), channel_id=1, source_target_pairs={{0,6},{1,7},{2,4},{3,5},{4,2},{5,3},{6,0},{7,1},{8,14},{9,15},{10,... | collective-permute-start | bytes 196616 | tf_op jit(solution)/shard_map/ppermute | solution.py:431
  55.1 0.6 collective-permute-start.9
  55.6 1.4 %collective-permute-start.8 = (f32[4,32,128]{2,1,0:T(8,128)S(1)}, f32[4,32,128]{2,1,0:T(8,128)S(1)}, u32[]{:S(2)}, u32[]{:S(2)}) collective-permute-start(f32[4,32,128]{2,1,0:T(8,128)S(1)} %get-tuple-element.21.refs_0_), channel_id=1, source_target_pairs={{0,2},{1,3},{2,0},{3,1},{4,6},{5,7},{6,4},{7,5},{8,10},{9,11},{10,... | collective-permute-start | bytes 196616 | tf_op jit(solution)/shard_map/ppermute | solution.py:431
  57.1 2.0 %collective-permute-done.10.refs_3_ = f32[4,32,128]{2,1,0:T(8,128)S(1)} collective-permute-done((f32[4,32,128]{2,1,0:T(8,128)S(1)}, f32[4,32,128]{2,1,0:T(8,128)S(1)}, u32[]{:S(2)}, u32[]{:S(2)}) %collective-permute-start.10) | collective-permute-done | bytes 65568 | tf_op jit(solution)/shard_map/ppermute | solution.py:431
  59.0 0.7 %collective-permute-done.9.refs_2_ = f32[4,32,128]{2,1,0:T(8,128)S(1)} collective-permute-done((f32[4,32,128]{2,1,0:T(8,128)S(1)}, f32[4,32,128]{2,1,0:T(8,128)S(1)}, u32[]{:S(2)}, u32[]{:S(2)}) %collective-permute-start.9) | collective-permute-done | bytes 65568 | tf_op jit(solution)/shard_map/ppermute | solution.py:431
  59.7 0.2 collective-permute-done.8.refs_1_
  59.9 0.6 shard_map.101
  60.5 0.0 collective-permute-start.11
  60.5 0.0 collective-permute-done.15.other_ref
  60.5 1.1 %shard_map.103 = (f32[8,128,128]{2,1,0:T(8,128)S(1)}, f32[8,128,128]{2,1,0:T(8,128)S(1)}, bf16[128,192]{1,0:T(8,128)(2,1)S(1)}, f32[8,128]{1,0:T(8,128)S(1)}) custom-call(bf16[4,4,224,128]{3,2,1,0:T(8,128)(2,1)S(1)} %get-tuple-element.24.mine_ref, bf16[4,4,224,128]{3,2,1,0:T(8,128)(2,1)S(1)} %collective-permute-done.15.other_ref, ...), custom_call_target="tpu_custom_call" | custom-call | tf_op jit(solution)/shard_map/pallas_call | solution.py:306
  61.6 0.5 collective-permute-done.11.t_other
  62.0 1.6 %shard_map.104 = (f32[32,96]{1,0:T(8,128)}, f32[192,128]{1,0:T(8,128)}, f32[1,1]{1,0:T(1,128)}) custom-call(f32[4,4,32,128]{3,2,1,0:T(8,128)S(1)} %get-tuple-element.22.t_mine, f32[4,4,32,128]{3,2,1,0:T(8,128)S(1)} %collective-permute-done.11.t_other, f32[8,128,128]{2,1,0:T(8,128)S(1)} %get-tuple-element.26.s_ref, ...), custom_call_target="tpu_custom_call" | custom-call | tf_op jit(solution)/shard_map/pallas_call | solution.py:406
  (7 shorter events, 0.0 us)
Async XLA Ops:
  0.6 15.2 %collective-permute-start.1 = (bf16[352,16,128]{2,1,0:T(8,128)(2,1)}, bf16[352,16,128]{2,1,0:T(8,128)(2,1)S(1)}, u32[]{:S(2)}, u32[]{:S(2)}) collective-permute-start(bf16[352,16,128]{2,1,0:T(8,128)(2,1)} %bitcast.4), channel_id=1, source_target_pairs={{0,1},{1,0},{2,3},{3,2},{4,5},{5,4},{6,7},{7,6},{8,9},{9,8},{10,11... | collective-permute-start | bytes 4325384 | tf_op jit(solution)/shard_map/ppermute | solution.py:431
  4.0 11.9 %collective-permute-start.4 = (bf16[736,128]{1,0:T(8,128)(2,1)}, bf16[736,128]{1,0:T(8,128)(2,1)S(1)}, u32[]{:S(2)}, u32[]{:S(2)}) collective-permute-start(bf16[736,128]{1,0:T(8,128)(2,1)} %get-tuple-element.18.refs_0_), channel_id=1, source_target_pairs={{0,8},{8,0},{16,24},{24,16},{1,9},{9,1},{17,25},{25,17},{2,10},{10... | collective-permute-start | bytes 565256 | tf_op jit(solution)/shard_map/ppermute | solution.py:428
  6.6 16.8 %collective-permute-start.3 = (bf16[736,128]{1,0:T(8,128)(2,1)}, bf16[736,128]{1,0:T(8,128)(2,1)S(1)}, u32[]{:S(2)}, u32[]{:S(2)}) collective-permute-start(bf16[736,128]{1,0:T(8,128)(2,1)} %get-tuple-element.18.refs_0_), channel_id=1, source_target_pairs={{0,16},{8,24},{16,0},{24,8},{1,17},{9,25},{17,1},{25,9},{2,18},{10... | collective-permute-start | bytes 565256 | tf_op jit(solution)/shard_map/ppermute | solution.py:428
  9.2 20.4 %collective-permute-start = (bf16[736,128]{1,0:T(8,128)(2,1)}, bf16[736,128]{1,0:T(8,128)(2,1)S(1)}, u32[]{:S(2)}, u32[]{:S(2)}) collective-permute-start(bf16[736,128]{1,0:T(8,128)(2,1)} %get-tuple-element.18.refs_0_), channel_id=1, source_target_pairs={{0,24},{8,16},{16,8},{24,0},{1,25},{9,17},{17,9},{25,1},{2,26},{10... | collective-permute-start | bytes 565256 | tf_op jit(solution)/shard_map/ppermute | solution.py:428
  9.2 6.4 %collective-permute-start.2 = (s32[401]{0:T(512)}, s32[401]{0:T(512)S(1)}, u32[]{:S(2)}, u32[]{:S(2)}) collective-permute-start(s32[401]{0:T(512)} %get-tuple-element.19.refs_2_.refs_4_.refs_3_), channel_id=1, source_target_pairs={{0,1},{1,0},{2,3},{3,2},{4,5},{5,4},{6,7},{7,6},{8,9},{9,8},{10,11... | collective-permute-start | bytes 4820 | tf_op jit(solution)/shard_map/ppermute | solution.py:431
  9.2 1.0 %copy-start = (bf16[736,128]{1,0:T(8,128)(2,1)S(1)}, bf16[736,128]{1,0:T(8,128)(2,1)}, u32[]{:S(2)}) copy-start(bf16[736,128]{1,0:T(8,128)(2,1)} %get-tuple-element.18.refs_0_) | copy-start | bytes 565252
  10.2 1.4 %copy-start.2 = (bf16[32,176,128]{2,1,0:T(8,128)(2,1)S(1)}, bf16[32,176,128]{2,1,0:T(8,128)(2,1)}, u32[]{:S(2)}) copy-start(bf16[32,176,128]{2,1,0:T(8,128)(2,1)} %param.9) | copy-start | bytes 4325380
  11.6 0.7 %copy-start.4 = (s32[401]{0:T(512)S(1)}, s32[401]{0:T(512)}, u32[]{:S(2)}) copy-start(s32[401]{0:T(512)} %get-tuple-element.19.refs_2_.refs_4_.refs_3_) | copy-start | bytes 4816
  15.6 7.8 %copy-start.3 = (bf16[32,176,128]{2,1,0:T(8,128)(2,1)S(1)}, bf16[32,176,128]{2,1,0:T(8,128)(2,1)}, u32[]{:S(2)}) copy-start(bf16[32,176,128]{2,1,0:T(8,128)(2,1)} %param.9) | copy-start | bytes 4325380
  23.4 6.3 %copy-start.1 = (bf16[736,128]{1,0:T(8,128)(2,1)S(1)}, bf16[736,128]{1,0:T(8,128)(2,1)}, u32[]{:S(2)}) copy-start(bf16[736,128]{1,0:T(8,128)(2,1)} %get-tuple-element.18.refs_0_) | copy-start | bytes 565252
  23.4 9.9 %copy-start.5 = (s32[401]{0:T(512)S(1)}, s32[401]{0:T(512)}, u32[]{:S(2)}) copy-start(s32[401]{0:T(512)} %get-tuple-element.19.refs_2_.refs_4_.refs_3_) | copy-start | bytes 4816
  29.7 13.6 %collective-permute-start.14 = (bf16[4,224,128]{2,1,0:T(8,128)(2,1)S(1)}, bf16[4,224,128]{2,1,0:T(8,128)(2,1)S(1)}, u32[]{:S(2)}, u32[]{:S(2)}) collective-permute-start(bf16[4,224,128]{2,1,0:T(8,128)(2,1)S(1)} %get-tuple-element.23.refs_0_), channel_id=1, source_target_pairs={{0,6},{1,7},{2,4},{3,5},{4,2},{5,3},{6,0},{7,1},{8,14},{9,15},{10,... | collective-permute-start | bytes 688136 | tf_op jit(solution)/shard_map/ppermute | solution.py:431
  32.4 11.0 %collective-permute-start.13 = (bf16[4,224,128]{2,1,0:T(8,128)(2,1)S(1)}, bf16[4,224,128]{2,1,0:T(8,128)(2,1)S(1)}, u32[]{:S(2)}, u32[]{:S(2)}) collective-permute-start(bf16[4,224,128]{2,1,0:T(8,128)(2,1)S(1)} %get-tuple-element.23.refs_0_), channel_id=1, source_target_pairs={{0,4},{1,5},{2,6},{3,7},{4,0},{5,1},{6,2},{7,3},{8,12},{9,13},{10,... | collective-permute-start | bytes 688136 | tf_op jit(solution)/shard_map/ppermute | solution.py:431
  32.9 10.9 %collective-permute-start.12 = (bf16[4,224,128]{2,1,0:T(8,128)(2,1)S(1)}, bf16[4,224,128]{2,1,0:T(8,128)(2,1)S(1)}, u32[]{:S(2)}, u32[]{:S(2)}) collective-permute-start(bf16[4,224,128]{2,1,0:T(8,128)(2,1)S(1)} %get-tuple-element.23.refs_0_), channel_id=1, source_target_pairs={{0,2},{1,3},{2,0},{3,1},{4,6},{5,7},{6,4},{7,5},{8,10},{9,11},{10,... | collective-permute-start | bytes 688136 | tf_op jit(solution)/shard_map/ppermute | solution.py:431
  39.5 3.8 %collective-permute-start.5 = (f32[32,128]{1,0:T(8,128)S(1)}, f32[32,128]{1,0:T(8,128)S(1)}, u32[]{:S(2)}, u32[]{:S(2)}) collective-permute-start(f32[32,128]{1,0:T(8,128)S(1)} %shard_map.99.refs_0_), channel_id=1, source_target_pairs={{0,8},{8,0},{16,24},{24,16},{1,9},{9,1},{17,25},{25,17},{2,10},{10... | collective-permute-start | bytes 49160 | tf_op jit(solution)/shard_map/ppermute | solution.py:428
  44.4 16.1 %collective-permute-start.15 = (bf16[4,4,224,128]{3,2,1,0:T(8,128)(2,1)S(1)}, bf16[4,4,224,128]{3,2,1,0:T(8,128)(2,1)S(1)}, u32[]{:S(2)}, u32[]{:S(2)}) collective-permute-start(bf16[4,4,224,128]{3,2,1,0:T(8,128)(2,1)S(1)} %get-tuple-element.24.mine_ref), channel_id=1, source_target_pairs={{0,1},{1,0},{2,3},{3,2},{4,5},{5,4},{6,7},{7,6},{8,9},{9,8},{10,11... | collective-permute-start | bytes 2752520 | tf_op jit(solution)/shard_map/ppermute | solution.py:431
  44.4 6.2 %collective-permute-start.7 = (f32[32,128]{1,0:T(8,128)S(1)}, f32[32,128]{1,0:T(8,128)S(1)}, u32[]{:S(2)}, u32[]{:S(2)}) collective-permute-start(f32[32,128]{1,0:T(8,128)S(1)} %shard_map.99.refs_0_), channel_id=1, source_target_pairs={{0,24},{8,16},{16,8},{24,0},{1,25},{9,17},{17,9},{25,1},{2,26},{10... | collective-permute-start | bytes 49160 | tf_op jit(solution)/shard_map/ppermute | solution.py:428
  48.9 4.6 %collective-permute-start.6 = (f32[32,128]{1,0:T(8,128)S(1)}, f32[32,128]{1,0:T(8,128)S(1)}, u32[]{:S(2)}, u32[]{:S(2)}) collective-permute-start(f32[32,128]{1,0:T(8,128)S(1)} %shard_map.99.refs_0_), channel_id=1, source_target_pairs={{0,16},{8,24},{16,0},{24,8},{1,17},{9,25},{17,1},{25,9},{2,18},{10... | collective-permute-start | bytes 49160 | tf_op jit(solution)/shard_map/ppermute | solution.py:428
  53.5 5.5 %collective-permute-start.10 = (f32[4,32,128]{2,1,0:T(8,128)S(1)}, f32[4,32,128]{2,1,0:T(8,128)S(1)}, u32[]{:S(2)}, u32[]{:S(2)}) collective-permute-start(f32[4,32,128]{2,1,0:T(8,128)S(1)} %get-tuple-element.21.refs_0_), channel_id=1, source_target_pairs={{0,6},{1,7},{2,4},{3,5},{4,2},{5,3},{6,0},{7,1},{8,14},{9,15},{10,... | collective-permute-start | bytes 196616 | tf_op jit(solution)/shard_map/ppermute | solution.py:431
  55.1 4.6 %collective-permute-start.9 = (f32[4,32,128]{2,1,0:T(8,128)S(1)}, f32[4,32,128]{2,1,0:T(8,128)S(1)}, u32[]{:S(2)}, u32[]{:S(2)}) collective-permute-start(f32[4,32,128]{2,1,0:T(8,128)S(1)} %get-tuple-element.21.refs_0_), channel_id=1, source_target_pairs={{0,4},{1,5},{2,6},{3,7},{4,0},{5,1},{6,2},{7,3},{8,12},{9,13},{10,... | collective-permute-start | bytes 196616 | tf_op jit(solution)/shard_map/ppermute | solution.py:431
  55.6 4.3 %collective-permute-start.8 = (f32[4,32,128]{2,1,0:T(8,128)S(1)}, f32[4,32,128]{2,1,0:T(8,128)S(1)}, u32[]{:S(2)}, u32[]{:S(2)}) collective-permute-start(f32[4,32,128]{2,1,0:T(8,128)S(1)} %get-tuple-element.21.refs_0_), channel_id=1, source_target_pairs={{0,2},{1,3},{2,0},{3,1},{4,6},{5,7},{6,4},{7,5},{8,10},{9,11},{10,... | collective-permute-start | bytes 196616 | tf_op jit(solution)/shard_map/ppermute | solution.py:431
  60.5 1.5 %collective-permute-start.11 = (f32[4,4,32,128]{3,2,1,0:T(8,128)S(1)}, f32[4,4,32,128]{3,2,1,0:T(8,128)S(1)}, u32[]{:S(2)}, u32[]{:S(2)}) collective-permute-start(f32[4,4,32,128]{3,2,1,0:T(8,128)S(1)} %get-tuple-element.22.t_mine), channel_id=1, source_target_pairs={{0,1},{1,0},{2,3},{3,2},{4,5},{5,4},{6,7},{7,6},{8,9},{9,8},{10,11... | collective-permute-start | bytes 786440 | tf_op jit(solution)/shard_map/ppermute | solution.py:431
where the time goes:
time: 63.9 us; the launch traced here: 63.7 us
  Pallas kernels  30.2 us (47%)
  starting transfers between devices  18.6 us (29%)
  waiting for transfers between devices  11.1 us (17%)
  local copies, waits for them, and re-layouts  3.04 us (5%)
  between operations  0.76 us (1%)
    pallas_call x4, Pallas kernels, teacher(): pl.pallas_call(functools.partial(teacher_kernel, slots, tasks, shifts, si...  23.4 us
    ppermute x6, starting transfers between devices, over_row(): return lax.ppermute(x, 'row', [(i, i ^ k) for i in range(R)])  11 us
    ppermute x10, starting transfers between devices, over_col(): return lax.ppermute(x, 'col', [(i, i ^ k) for i in range(C)])  7.63 us
    ppermute x6, waiting for transfers between devices, over_row(): return lax.ppermute(x, 'row', [(i, i ^ k) for i in range(R)])  7.37 us
    ppermute x10, waiting for transfers between devices, over_col(): return lax.ppermute(x, 'col', [(i, i ^ k) for i in range(C)])  3.7 us
    unnamed x12, local copies, waits for them, and re-layouts  3.04 us
    pallas_call x1, Pallas kernels, prepare(): pl.pallas_call(functools.partial(prepare_kernel, slots, per), out_shape=(...  2.8 us
    pallas_call x1, Pallas kernels, finish(): pl.pallas_call(functools.partial(finish_kernel, wide), out_shape=(jax.Sha...  1.63 us
  transfers between devices with their start and end apart: 16, of which 10 were waited for; matrix products, arithmetic and copies ran while one was open for 0% of the time, Pallas kernels for 44%

commit v1 on v0

--- a/solution.py
+++ b/solution.py
@@ -147,12 +147,11 @@
                         best[n + l, pl.ds(owner[g], 8), :] = carry[n + l]
             return tuple(carry)
 
-        lax.fori_loop(
-            0,
-            lax.shift_right_logical(count + GROUP - 1, GROUP.bit_length() - 1),
-            step,
-            tuple(jnp.full((8, LANES), NEG, jnp.float32) for _ in cells),
-        )
+        steps = lax.shift_right_logical(count + GROUP - 1, GROUP.bit_length() - 1)
+        twice = lax.shift_right_logical(steps, 1)
+        begin = tuple(jnp.full((8, LANES), NEG, jnp.float32) for _ in cells)
+        begin = lax.fori_loop(0, twice, lambda i, x, step=step: step(2 * i + 1, step(2 * i, x)), begin)
+        lax.fori_loop(2 * twice, steps, step, begin)
         found = []
         for l in range(len(cells)):
             peak = best[l, pl.ds(0, passages, stride=8), :]
@@ -443,17 +442,17 @@
     lists = [blocks, over_col(blocks, 1)]
     near = [sent] + [over_row(sent, k) for k in range(1, R)]
     common = dict(near=near, tokens=tokens, lists=lists, queries=queries, passages=local)
-    score = teacher(slots, ((0, (0,)),), **common)
-    score = teacher(slots, ((1, (0, 1)), (0, (1,))), priors=(score,), **common)
-    for k in range(2, R - 2, 2):
-        score = teacher(slots, ((0, (k, k + 1)), (1, (k, k + 1))), priors=(score,), **common)
-    score = teacher(slots, ((0, (R - 2,)), (1, (R - 2,))), priors=(score,), **common)
+    begun = teacher(slots, ((0, (0,)),), megabytes=56, **common)
+    score = teacher(slots, ((1, (0, 1)), (0, (1,))), after=(begun,), **common)
     base = sent.shape[0] - student_passages.shape[1] - block
     vectors, token = pack("row", near, base, sent.shape[0] - base, (score,))
-    score = teacher(slots, ((0, (R - 1,)), (1, (R - 1,))), priors=(score,), after=(token,), **common)
+    priors = (score, begun)
+    for k in range(2, R, 2):
+        score = teacher(slots, ((0, (k, k + 1)), (1, (k, k + 1))), priors=priors, after=(token,), **common)
+        priors = (score,)
     scores = [score] + [over_row(score, k) for k in range(1, R)]
-    mine, other = spread(vectors, (scores[1],))
     stack, token = pack("row", scores, 0, local, ())
+    mine, other = spread(vectors, (token,))
     s, slope, vectors, stats = student_scores(mine, other, token, queries, wide)
     t_mine, t_other = spread(stack, ())
     query_grads, passage_grads, loss = finish(t_mine, t_other, s, slope, mine, other, vectors, stats, wide)

time: 63.9 us -> 58.8 us (0.920)
  Pallas kernels: 30.2 us -> 24.2 us
  waiting for transfers between devices: 11.1 us -> 16.9 us
  starting transfers between devices: 18.6 us -> 15.8 us
  local copies, waits for them, and re-layouts: 3.04 us -> 0.73 us
    pallas_call x4 -> x3, Pallas kernels: 23.4 us -> 17.4 us  [teacher(): pl.pallas_call(functools.partial(teacher_kernel, slots, tasks, shifts, si...]
    ppermute x6, waiting for transfers between devices: 7.37 us -> 12.7 us  [over_row(): return lax.ppermute(x, 'row', [(i, i ^ k) for i in range(R)])]
    ppermute x6, starting transfers between devices: 11 us -> 8.23 us  [over_row(): return lax.ppermute(x, 'row', [(i, i ^ k) for i in range(R)])]
    unnamed x12 -> x10, local copies, waits for them, and re-layouts: 3.04 us -> 0.73 us
  transfers between devices with their start and end apart: 16 -> 16, of which waited for: 10 -> 8; matrix products, arithmetic and copies ran while one was open for 0% -> 0% of each run, Pallas kernels for 44% -> 37%
where the time goes in v1:
time: 58.8 us; the launch traced here: 58.4 us
  Pallas kernels  24.2 us (41%)
  waiting for transfers between devices  16.9 us (29%)
  starting transfers between devices  15.8 us (27%)
  between operations  0.76 us (1%)
  local copies, waits for them, and re-layouts  0.73 us (1%)
    pallas_call x3, Pallas kernels, teacher(): pl.pallas_call(functools.partial(teacher_kernel, slots, tasks, shifts, si...  17.4 us
    ppermute x6, waiting for transfers between devices, over_row(): return lax.ppermute(x, 'row', [(i, i ^ k) for i in range(R)])  12.7 us
    ppermute x6, starting transfers between devices, over_row(): return lax.ppermute(x, 'row', [(i, i ^ k) for i in range(R)])  8.23 us
    ppermute x10, starting transfers between devices, over_col(): return lax.ppermute(x, 'col', [(i, i ^ k) for i in range(C)])  7.57 us
    ppermute x10, waiting for transfers between devices, over_col(): return lax.ppermute(x, 'col', [(i, i ^ k) for i in range(C)])  4.2 us
    pallas_call x1, Pallas kernels, prepare(): pl.pallas_call(functools.partial(prepare_kernel, slots, per), out_shape=(...  2.8 us
    pallas_call x1, Pallas kernels, finish(): pl.pallas_call(functools.partial(finish_kernel, wide), out_shape=(jax.Sha...  1.63 us
    pallas_call x4, Pallas kernels, pack(): pl.pallas_call(functools.partial(pack_kernel, axis, first, count, len(pie...  1.3 us
  transfers between devices with their start and end apart: 16, of which 8 were waited for; matrix products, arithmetic and copies ran while one was open for 0% of the time, Pallas kernels for 37%

profile of v1, /device:TPU:0, one launch (start us, length us, event | category | flops | bytes accessed | tf_op | source)
XLA Modules:
  0.0 58.4 jit_solution(330578338770717137)
XLA Ops:
  0.6 0.5 collective-permute-start.2
  1.1 2.8 %shard_map.94 = (bf16[736,128]{1,0:T(8,128)(2,1)}, s32[401]{0:T(512)}) custom-call(bf16[32,32,128]{2,1,0:T(8,128)(2,1)} %tokens_ref.1, s32[32]{0:T(128)} %lives_ref.1, s32[32]{0:T(128)} %lengths_ref.1, bf16[32,96]{1,0:T(8,128)(2,1)} %sq_ref.1, bf16[192,128]{1,0:T(8,128)(2,1)} %bitcast.8, s32[32]{0:T(128)} %pos_ref.1), custom_call_target="tpu_custom_call" | custom-call | tf_op jit(solution)/shard_map/pallas_call | solution.py:95
  4.0 2.7 %collective-permute-start.4 = (bf16[736,128]{1,0:T(8,128)(2,1)}, bf16[736,128]{1,0:T(8,128)(2,1)S(1)}, u32[]{:S(2)}, u32[]{:S(2)}) collective-permute-start(bf16[736,128]{1,0:T(8,128)(2,1)} %get-tuple-element.18.refs_0_), channel_id=1, source_target_pairs={{0,8},{8,0},{16,24},{24,16},{1,9},{9,1},{17,25},{25,17},{2,10},{10... | collective-permute-start | bytes 565256 | tf_op jit(solution)/shard_map/ppermute | solution.py:427
  6.6 2.5 %collective-permute-start.1 = (bf16[736,128]{1,0:T(8,128)(2,1)}, bf16[736,128]{1,0:T(8,128)(2,1)S(1)}, u32[]{:S(2)}, u32[]{:S(2)}) collective-permute-start(bf16[736,128]{1,0:T(8,128)(2,1)} %get-tuple-element.18.refs_0_), channel_id=1, source_target_pairs={{0,24},{8,16},{16,8},{24,0},{1,25},{9,17},{17,9},{25,1},{2,26},{10... | collective-permute-start | bytes 565256 | tf_op jit(solution)/shard_map/ppermute | solution.py:427
  9.1 0.1 collective-permute-start
  9.2 0.0 copy-start
  9.2 0.0 copy-start.1
  9.2 0.0 collective-permute-start.3
  9.2 4.4 %shard_map.95.refs_6_.refs_7_ = f32[32,128]{1,0:T(8,128)} custom-call(bf16[736,128]{1,0:T(8,128)(2,1)} %get-tuple-element.18.refs_0_, bf16[352,16,128]{2,1,0:T(8,128)(2,1)} %bitcast.5, s32[401]{0:T(512)} %get-tuple-element.19.refs_2_.refs_4_), custom_call_target="tpu_custom_call" | custom-call | flops 1476395008 | bytes 1441792 | tf_op jit(solution)/shard_map/pallas_call | solution.py:184
  13.6 0.0 collective-permute-done.3.refs_5_
  13.6 0.0 collective-permute-done.4.refs_1_
  13.6 0.0 collective-permute-done.2.refs_3_
  13.6 0.0 copy-done
  13.6 0.0 copy-done.1
  13.7 0.0 copy-done.2
  13.7 0.0 copy-start.3
  13.7 0.7 %copy-done.3 = f32[32,128]{1,0:T(8,128)S(1)} copy-done((f32[32,128]{1,0:T(8,128)S(1)}, f32[32,128]{1,0:T(8,128)}, u32[]{:S(2)}) %copy-start.3) | copy-done | bytes 16408
  14.4 5.9 %shard_map.96.refs_4_.refs_6_ = f32[32,128]{1,0:T(8,128)S(1)} custom-call(bf16[736,128]{1,0:T(8,128)(2,1)S(1)} %copy-done, bf16[736,128]{1,0:T(8,128)(2,1)S(1)} %collective-permute-done.4.refs_1_, bf16[352,16,128]{2,1,0:T(8,128)(2,1)S(1)} %bitcast.6, bf16[352,16,128]{2,1,0:T(8,128)(2,1)S(1)} %collective-permute-done.2.refs_3_, s32[401]{0:T(512)S(1)} %copy-done.2, ...), custom_call_target="tpu_custom_call" | custom-call | flops 4429185024 | bytes 2883584 | tf_op jit(solution)/shard_map/pallas_call | solution.py:184
  20.3 0.0 collective-permute-done.1.refs_3_.refs_1_
  20.3 6.3 %collective-permute-done.refs_2_.refs_0_ = bf16[736,128]{1,0:T(8,128)(2,1)S(1)} collective-permute-done((bf16[736,128]{1,0:T(8,128)(2,1)}, bf16[736,128]{1,0:T(8,128)(2,1)S(1)}, u32[]{:S(2)}, u32[]{:S(2)}) %collective-permute-start) | collective-permute-done | bytes 188448 | tf_op jit(solution)/shard_map/ppermute | solution.py:427
  26.7 2.5 %collective-permute-start.14 = (bf16[4,224,128]{2,1,0:T(8,128)(2,1)S(1)}, bf16[4,224,128]{2,1,0:T(8,128)(2,1)S(1)}, u32[]{:S(2)}, u32[]{:S(2)}) collective-permute-start(bf16[4,224,128]{2,1,0:T(8,128)(2,1)S(1)} %get-tuple-element.23.refs_0_), channel_id=1, source_target_pairs={{0,6},{1,7},{2,4},{3,5},{4,2},{5,3},{6,0},{7,1},{8,14},{9,15},{10,... | collective-permute-start | bytes 688136 | tf_op jit(solution)/shard_map/ppermute | solution.py:430
  29.2 0.5 collective-permute-start.13
  29.7 0.5 collective-permute-start.12
  30.2 0.0 copy-done.4
  30.2 7.1 %shard_map.98.refs_0_ = f32[32,128]{1,0:T(8,128)S(1)} custom-call(bf16[736,128]{1,0:T(8,128)(2,1)S(1)} %collective-permute-done.refs_2_.refs_0_, bf16[736,128]{1,0:T(8,128)(2,1)S(1)} %collective-permute-done.1.refs_3_.refs_1_, bf16[352,16,128]{2,1,0:T(8,128)(2,1)S(1)} %bitcast.7, bf16[352,16,128]{2,1,0:T(8,128)(2,1)S(1)} %collective-permute-done.2.refs_3_, ...), custom_call_target="tpu_custom_call" | custom-call | flops 5905580032 | bytes 2883584 | tf_op jit(solution)/shard_map/pallas_call | solution.py:184
  37.3 3.0 %collective-permute-start.7 = (f32[32,128]{1,0:T(8,128)S(1)}, f32[32,128]{1,0:T(8,128)S(1)}, u32[]{:S(2)}, u32[]{:S(2)}) collective-permute-start(f32[32,128]{1,0:T(8,128)S(1)} %shard_map.98.refs_0_), channel_id=1, source_target_pairs={{0,24},{8,16},{16,8},{24,0},{1,25},{9,17},{17,9},{25,1},{2,26},{10... | collective-permute-start | bytes 49160 | tf_op jit(solution)/shard_map/ppermute | solution.py:427
  40.3 0.0 collective-permute-start.6
  40.3 2.6 %collective-permute-done.7.refs_3_ = f32[32,128]{1,0:T(8,128)S(1)} collective-permute-done((f32[32,128]{1,0:T(8,128)S(1)}, f32[32,128]{1,0:T(8,128)S(1)}, u32[]{:S(2)}, u32[]{:S(2)}) %collective-permute-start.7) | collective-permute-done | bytes 16416 | tf_op jit(solution)/shard_map/ppermute | solution.py:427
  42.9 0.0 collective-permute-start.5
  43.0 2.0 %collective-permute-done.6.refs_2_ = f32[32,128]{1,0:T(8,128)S(1)} collective-permute-done((f32[32,128]{1,0:T(8,128)S(1)}, f32[32,128]{1,0:T(8,128)S(1)}, u32[]{:S(2)}, u32[]{:S(2)}) %collective-permute-start.6) | collective-permute-done | bytes 16416 | tf_op jit(solution)/shard_map/ppermute | solution.py:427
  45.0 1.7 %collective-permute-done.5.refs_1_ = f32[32,128]{1,0:T(8,128)S(1)} collective-permute-done((f32[32,128]{1,0:T(8,128)S(1)}, f32[32,128]{1,0:T(8,128)S(1)}, u32[]{:S(2)}, u32[]{:S(2)}) %collective-permute-start.5) | collective-permute-done | bytes 16416 | tf_op jit(solution)/shard_map/ppermute | solution.py:427
  46.7 0.0 collective-permute-done.14.refs_3_
  46.7 0.0 collective-permute-done.13.refs_2_
  46.7 0.0 collective-permute-done.12.refs_1_
  46.7 0.7 %shard_map.101 = (bf16[4,4,224,128]{3,2,1,0:T(8,128)(2,1)S(1)}, f32[8,128]{1,0:T(8,128)}) custom-call(bf16[4,224,128]{2,1,0:T(8,128)(2,1)S(1)} %get-tuple-element.23.refs_0_, bf16[4,224,128]{2,1,0:T(8,128)(2,1)S(1)} %collective-permute-done.12.refs_1_, bf16[4,224,128]{2,1,0:T(8,128)(2,1)S(1)} %collective-permute-done.13.refs_2_, ...), custom_call_target="tpu_custom_call" | custom-call | tf_op jit(solution)/shard_map/pallas_call | solution.py:209
  47.4 0.0 collective-permute-start.15
  47.4 2.4 %collective-permute-start.10 = (f32[4,32,128]{2,1,0:T(8,128)S(1)}, f32[4,32,128]{2,1,0:T(8,128)S(1)}, u32[]{:S(2)}, u32[]{:S(2)}) collective-permute-start(f32[4,32,128]{2,1,0:T(8,128)S(1)} %get-tuple-element.21.refs_0_), channel_id=1, source_target_pairs={{0,6},{1,7},{2,4},{3,5},{4,2},{5,3},{6,0},{7,1},{8,14},{9,15},{10,... | collective-permute-start | bytes 196616 | tf_op jit(solution)/shard_map/ppermute | solution.py:430
  49.9 0.5 collective-permute-start.9
  50.4 0.5 collective-permute-start.8
  50.9 1.9 %collective-permute-done.10.refs_3_ = f32[4,32,128]{2,1,0:T(8,128)S(1)} collective-permute-done((f32[4,32,128]{2,1,0:T(8,128)S(1)}, f32[4,32,128]{2,1,0:T(8,128)S(1)}, u32[]{:S(2)}, u32[]{:S(2)}) %collective-permute-start.10) | collective-permute-done | bytes 65568 | tf_op jit(solution)/shard_map/ppermute | solution.py:430
  52.8 1.4 %collective-permute-done.9.refs_2_ = f32[4,32,128]{2,1,0:T(8,128)S(1)} collective-permute-done((f32[4,32,128]{2,1,0:T(8,128)S(1)}, f32[4,32,128]{2,1,0:T(8,128)S(1)}, u32[]{:S(2)}, u32[]{:S(2)}) %collective-permute-start.9) | collective-permute-done | bytes 65568 | tf_op jit(solution)/shard_map/ppermute | solution.py:430
  54.2 0.4 collective-permute-done.8.refs_1_
  54.6 0.6 %shard_map.100 = (f32[4,4,32,128]{3,2,1,0:T(8,128)S(1)}, f32[8,128]{1,0:T(8,128)}) custom-call(f32[4,32,128]{2,1,0:T(8,128)S(1)} %get-tuple-element.21.refs_0_, f32[4,32,128]{2,1,0:T(8,128)S(1)} %collective-permute-done.8.refs_1_, f32[4,32,128]{2,1,0:T(8,128)S(1)} %collective-permute-done.9.refs_2_, f32[4,32,128]{2,1,0:T(8,128)S(1)} %collective-permute-done.10.refs_3_), custom_call_target="tpu_custom_call" | custom-call | tf_op jit(solution)/shard_map/pallas_call | solution.py:209
  55.2 0.0 collective-permute-start.11
  55.2 0.0 collective-permute-done.15.other_ref
  55.2 1.1 %shard_map.102 = (f32[8,128,128]{2,1,0:T(8,128)S(1)}, f32[8,128,128]{2,1,0:T(8,128)S(1)}, bf16[128,192]{1,0:T(8,128)(2,1)S(1)}, f32[8,128]{1,0:T(8,128)S(1)}) custom-call(bf16[4,4,224,128]{3,2,1,0:T(8,128)(2,1)S(1)} %get-tuple-element.25.mine_ref, bf16[4,4,224,128]{3,2,1,0:T(8,128)(2,1)S(1)} %collective-permute-done.15.other_ref, ...), custom_call_target="tpu_custom_call" | custom-call | tf_op jit(solution)/shard_map/pallas_call | solution.py:305
  56.3 0.5 collective-permute-done.11.t_other
  56.8 1.6 %shard_map.103 = (f32[32,96]{1,0:T(8,128)}, f32[192,128]{1,0:T(8,128)}, f32[1,1]{1,0:T(1,128)}) custom-call(f32[4,4,32,128]{3,2,1,0:T(8,128)S(1)} %get-tuple-element.22.t_mine, f32[4,4,32,128]{3,2,1,0:T(8,128)S(1)} %collective-permute-done.11.t_other, f32[8,128,128]{2,1,0:T(8,128)S(1)} %get-tuple-element.26.s_ref, ...), custom_call_target="tpu_custom_call" | custom-call | tf_op jit(solution)/shard_map/pallas_call | solution.py:405
  (4 shorter events, 0.0 us)
Async XLA Ops:
  0.6 13.0 %collective-permute-start.2 = (bf16[352,16,128]{2,1,0:T(8,128)(2,1)}, bf16[352,16,128]{2,1,0:T(8,128)(2,1)S(1)}, u32[]{:S(2)}, u32[]{:S(2)}) collective-permute-start(bf16[352,16,128]{2,1,0:T(8,128)(2,1)} %bitcast.4), channel_id=1, source_target_pairs={{0,1},{1,0},{2,3},{3,2},{4,5},{5,4},{6,7},{7,6},{8,9},{9,8},{10,11... | collective-permute-start | bytes 4325384 | tf_op jit(solution)/shard_map/ppermute | solution.py:430
  4.0 9.7 %collective-permute-start.4 = (bf16[736,128]{1,0:T(8,128)(2,1)}, bf16[736,128]{1,0:T(8,128)(2,1)S(1)}, u32[]{:S(2)}, u32[]{:S(2)}) collective-permute-start(bf16[736,128]{1,0:T(8,128)(2,1)} %get-tuple-element.18.refs_0_), channel_id=1, source_target_pairs={{0,8},{8,0},{16,24},{24,16},{1,9},{9,1},{17,25},{25,17},{2,10},{10... | collective-permute-start | bytes 565256 | tf_op jit(solution)/shard_map/ppermute | solution.py:427
  6.6 13.7 %collective-permute-start.1 = (bf16[736,128]{1,0:T(8,128)(2,1)}, bf16[736,128]{1,0:T(8,128)(2,1)S(1)}, u32[]{:S(2)}, u32[]{:S(2)}) collective-permute-start(bf16[736,128]{1,0:T(8,128)(2,1)} %get-tuple-element.18.refs_0_), channel_id=1, source_target_pairs={{0,24},{8,16},{16,8},{24,0},{1,25},{9,17},{17,9},{25,1},{2,26},{10... | collective-permute-start | bytes 565256 | tf_op jit(solution)/shard_map/ppermute | solution.py:427
  9.1 17.6 %collective-permute-start = (bf16[736,128]{1,0:T(8,128)(2,1)}, bf16[736,128]{1,0:T(8,128)(2,1)S(1)}, u32[]{:S(2)}, u32[]{:S(2)}) collective-permute-start(bf16[736,128]{1,0:T(8,128)(2,1)} %get-tuple-element.18.refs_0_), channel_id=1, source_target_pairs={{0,16},{8,24},{16,0},{24,8},{1,17},{9,25},{17,1},{25,9},{2,18},{10... | collective-permute-start | bytes 565256 | tf_op jit(solution)/shard_map/ppermute | solution.py:427
  9.2 4.4 %copy-start = (bf16[736,128]{1,0:T(8,128)(2,1)S(1)}, bf16[736,128]{1,0:T(8,128)(2,1)}, u32[]{:S(2)}) copy-start(bf16[736,128]{1,0:T(8,128)(2,1)} %get-tuple-element.18.refs_0_) | copy-start | bytes 565252
  9.2 4.4 %copy-start.1 = (bf16[32,176,128]{2,1,0:T(8,128)(2,1)S(1)}, bf16[32,176,128]{2,1,0:T(8,128)(2,1)}, u32[]{:S(2)}) copy-start(bf16[32,176,128]{2,1,0:T(8,128)(2,1)} %param.9) | copy-start | bytes 4325380
  9.2 4.5 %copy-start.2 = (s32[401]{0:T(512)S(1)}, s32[401]{0:T(512)}, u32[]{:S(2)}) copy-start(s32[401]{0:T(512)} %get-tuple-element.19.refs_2_.refs_4_) | copy-start | bytes 4816
  9.2 4.4 %collective-permute-start.3 = (s32[401]{0:T(512)}, s32[401]{0:T(512)S(1)}, u32[]{:S(2)}, u32[]{:S(2)}) collective-permute-start(s32[401]{0:T(512)} %get-tuple-element.19.refs_2_.refs_4_), channel_id=1, source_target_pairs={{0,1},{1,0},{2,3},{3,2},{4,5},{5,4},{6,7},{7,6},{8,9},{9,8},{10,11... | collective-permute-start | bytes 4820 | tf_op jit(solution)/shard_map/ppermute | solution.py:430
  13.7 0.7 %copy-start.3 = (f32[32,128]{1,0:T(8,128)S(1)}, f32[32,128]{1,0:T(8,128)}, u32[]{:S(2)}) copy-start(f32[32,128]{1,0:T(8,128)} %shard_map.95.refs_6_.refs_7_) | copy-start | bytes 49156
  14.4 15.9 %copy-start.4 = (f32[32,128]{1,0:T(8,128)S(1)}, f32[32,128]{1,0:T(8,128)}, u32[]{:S(2)}) copy-start(f32[32,128]{1,0:T(8,128)} %shard_map.95.refs_6_.refs_7_) | copy-start | bytes 49156
  26.7 20.0 %collective-permute-start.14 = (bf16[4,224,128]{2,1,0:T(8,128)(2,1)S(1)}, bf16[4,224,128]{2,1,0:T(8,128)(2,1)S(1)}, u32[]{:S(2)}, u32[]{:S(2)}) collective-permute-start(bf16[4,224,128]{2,1,0:T(8,128)(2,1)S(1)} %get-tuple-element.23.refs_0_), channel_id=1, source_target_pairs={{0,6},{1,7},{2,4},{3,5},{4,2},{5,3},{6,0},{7,1},{8,14},{9,15},{10,... | collective-permute-start | bytes 688136 | tf_op jit(solution)/shard_map/ppermute | solution.py:430
  29.2 17.5 %collective-permute-start.13 = (bf16[4,224,128]{2,1,0:T(8,128)(2,1)S(1)}, bf16[4,224,128]{2,1,0:T(8,128)(2,1)S(1)}, u32[]{:S(2)}, u32[]{:S(2)}) collective-permute-start(bf16[4,224,128]{2,1,0:T(8,128)(2,1)S(1)} %get-tuple-element.23.refs_0_), channel_id=1, source_target_pairs={{0,4},{1,5},{2,6},{3,7},{4,0},{5,1},{6,2},{7,3},{8,12},{9,13},{10,... | collective-permute-start | bytes 688136 | tf_op jit(solution)/shard_map/ppermute | solution.py:430
  29.7 17.0 %collective-permute-start.12 = (bf16[4,224,128]{2,1,0:T(8,128)(2,1)S(1)}, bf16[4,224,128]{2,1,0:T(8,128)(2,1)S(1)}, u32[]{:S(2)}, u32[]{:S(2)}) collective-permute-start(bf16[4,224,128]{2,1,0:T(8,128)(2,1)S(1)} %get-tuple-element.23.refs_0_), channel_id=1, source_target_pairs={{0,2},{1,3},{2,0},{3,1},{4,6},{5,7},{6,4},{7,5},{8,10},{9,11},{10,... | collective-permute-start | bytes 688136 | tf_op jit(solution)/shard_map/ppermute | solution.py:430
  37.3 5.6 %collective-permute-start.7 = (f32[32,128]{1,0:T(8,128)S(1)}, f32[32,128]{1,0:T(8,128)S(1)}, u32[]{:S(2)}, u32[]{:S(2)}) collective-permute-start(f32[32,128]{1,0:T(8,128)S(1)} %shard_map.98.refs_0_), channel_id=1, source_target_pairs={{0,24},{8,16},{16,8},{24,0},{1,25},{9,17},{17,9},{25,1},{2,26},{10... | collective-permute-start | bytes 49160 | tf_op jit(solution)/shard_map/ppermute | solution.py:427
  40.3 4.6 %collective-permute-start.6 = (f32[32,128]{1,0:T(8,128)S(1)}, f32[32,128]{1,0:T(8,128)S(1)}, u32[]{:S(2)}, u32[]{:S(2)}) collective-permute-start(f32[32,128]{1,0:T(8,128)S(1)} %shard_map.98.refs_0_), channel_id=1, source_target_pairs={{0,16},{8,24},{16,0},{24,8},{1,17},{9,25},{17,1},{25,9},{2,18},{10... | collective-permute-start | bytes 49160 | tf_op jit(solution)/shard_map/ppermute | solution.py:427
  42.9 3.7 %collective-permute-start.5 = (f32[32,128]{1,0:T(8,128)S(1)}, f32[32,128]{1,0:T(8,128)S(1)}, u32[]{:S(2)}, u32[]{:S(2)}) collective-permute-start(f32[32,128]{1,0:T(8,128)S(1)} %shard_map.98.refs_0_), channel_id=1, source_target_pairs={{0,8},{8,0},{16,24},{24,16},{1,9},{9,1},{17,25},{25,17},{2,10},{10... | collective-permute-start | bytes 49160 | tf_op jit(solution)/shard_map/ppermute | solution.py:427
  47.4 7.8 %collective-permute-start.15 = (bf16[4,4,224,128]{3,2,1,0:T(8,128)(2,1)S(1)}, bf16[4,4,224,128]{3,2,1,0:T(8,128)(2,1)S(1)}, u32[]{:S(2)}, u32[]{:S(2)}) collective-permute-start(bf16[4,4,224,128]{3,2,1,0:T(8,128)(2,1)S(1)} %get-tuple-element.25.mine_ref), channel_id=1, source_target_pairs={{0,1},{1,0},{2,3},{3,2},{4,5},{5,4},{6,7},{7,6},{8,9},{9,8},{10,11... | collective-permute-start | bytes 2752520 | tf_op jit(solution)/shard_map/ppermute | solution.py:430
  47.4 5.4 %collective-permute-start.10 = (f32[4,32,128]{2,1,0:T(8,128)S(1)}, f32[4,32,128]{2,1,0:T(8,128)S(1)}, u32[]{:S(2)}, u32[]{:S(2)}) collective-permute-start(f32[4,32,128]{2,1,0:T(8,128)S(1)} %get-tuple-element.21.refs_0_), channel_id=1, source_target_pairs={{0,6},{1,7},{2,4},{3,5},{4,2},{5,3},{6,0},{7,1},{8,14},{9,15},{10,... | collective-permute-start | bytes 196616 | tf_op jit(solution)/shard_map/ppermute | solution.py:430
  49.9 4.4 %collective-permute-start.9 = (f32[4,32,128]{2,1,0:T(8,128)S(1)}, f32[4,32,128]{2,1,0:T(8,128)S(1)}, u32[]{:S(2)}, u32[]{:S(2)}) collective-permute-start(f32[4,32,128]{2,1,0:T(8,128)S(1)} %get-tuple-element.21.refs_0_), channel_id=1, source_target_pairs={{0,4},{1,5},{2,6},{3,7},{4,0},{5,1},{6,2},{7,3},{8,12},{9,13},{10,... | collective-permute-start | bytes 196616 | tf_op jit(solution)/shard_map/ppermute | solution.py:430
  50.4 4.3 %collective-permute-start.8 = (f32[4,32,128]{2,1,0:T(8,128)S(1)}, f32[4,32,128]{2,1,0:T(8,128)S(1)}, u32[]{:S(2)}, u32[]{:S(2)}) collective-permute-start(f32[4,32,128]{2,1,0:T(8,128)S(1)} %get-tuple-element.21.refs_0_), channel_id=1, source_target_pairs={{0,2},{1,3},{2,0},{3,1},{4,6},{5,7},{6,4},{7,5},{8,10},{9,11},{10,... | collective-permute-start | bytes 196616 | tf_op jit(solution)/shard_map/ppermute | solution.py:430
  55.2 1.5 %collective-permute-start.11 = (f32[4,4,32,128]{3,2,1,0:T(8,128)S(1)}, f32[4,4,32,128]{3,2,1,0:T(8,128)S(1)}, u32[]{:S(2)}, u32[]{:S(2)}) collective-permute-start(f32[4,4,32,128]{3,2,1,0:T(8,128)S(1)} %get-tuple-element.22.t_mine), channel_id=1, source_target_pairs={{0,1},{1,0},{2,3},{3,2},{4,5},{5,4},{6,7},{7,6},{8,9},{9,8},{10,11... | collective-permute-start | bytes 786440 | tf_op jit(solution)/shard_map/ppermute | solution.py:430

commit v2 on v1

--- a/solution.py
+++ b/solution.py
@@ -104,14 +104,14 @@
     )(tokens, lives, lengths, sq, sp, pos)
 
 
-def teacher_kernel(slots, tasks, shifts, sides, priors, *refs):
+def teacher_kernel(slots, tasks, shifts, sides, priors, copies, *refs):
     query_refs = dict(zip(shifts, refs))
     refs = refs[len(shifts) :]
     token_refs = dict(zip(sides, refs))
     list_refs = dict(zip(sides, refs[len(sides) :]))
     prior_refs = refs[2 * len(sides) : 2 * len(sides) + priors]
     out_ref, best = refs[-2:]
-    passages, lanes = out_ref.shape
+    passages, lanes = out_ref.shape[-2:]
     width = token_refs[sides[0]].shape[2]
     r, c = lax.axis_index("row"), lax.axis_index("col")
     rows = lanes // 2 // lax.axis_size("row") * slots
@@ -167,10 +167,14 @@
             member = (owner == lax.broadcasted_iota(jnp.int32, (rows, lanes), 1)).astype(jnp.bfloat16)
             for piece in split(peaks, 3):
                 total = total + mxu(piece, member)
-    out_ref[...] = total
-
-
-def teacher(slots, tasks, near, tokens, lists, queries, passages, priors=(), after=(), megabytes=16):
+    if copies:
+        for i in range(copies):
+            out_ref[i] = total
+    else:
+        out_ref[...] = total
+
+
+def teacher(slots, tasks, near, tokens, lists, queries, passages, priors=(), after=(), megabytes=16, copies=0):
     shifts = sorted({k for _, used in tasks for k in used})
     sides = sorted({side for side, _ in tasks})
     operands = [near[k] for k in shifts] + [tokens[i] for i in sides] + [lists[i] for i in sides]
@@ -182,8 +186,8 @@
     size = tokens[0].size
     rows = queries // 2 // lax.axis_size("row") * slots
     return pl.pallas_call(
-        functools.partial(teacher_kernel, slots, tasks, shifts, sides, len(priors)),
-        out_shape=jax.ShapeDtypeStruct((passages, queries), jnp.float32),
+        functools.partial(teacher_kernel, slots, tasks, shifts, sides, len(priors), copies),
+        out_shape=jax.ShapeDtypeStruct((copies, passages, queries)[0 if copies else 1 :], jnp.float32),
         in_specs=specs,
         out_specs=vmem(),
         scratch_shapes=[pltpu.VMEM((most * rows // LANES, passages * 8, LANES), jnp.float32)],
@@ -200,12 +204,13 @@
     out_ref, token_ref = refs[-2:]
     me = lax.axis_index("row") if axis == "row" else lax.axis_index("col") // 2
     for k, ref in enumerate(refs[:pieces]):
-        out_ref[me ^ k] = ref[first : first + count]
+        for i in range(out_ref.shape[0]):
+            out_ref[i, me ^ k] = ref[first : first + count]
     token_ref[...] = jnp.zeros(token_ref.shape, jnp.float32)
 
 
-def pack(axis, pieces, first, count, after):
-    shape = (len(pieces), count) + pieces[0].shape[1:]
+def pack(axis, pieces, first, count, after, copies=1):
+    shape = (copies, len(pieces), count) + pieces[0].shape[1:]
     return pl.pallas_call(
         functools.partial(pack_kernel, axis, first, count, len(pieces)),
         out_shape=(jax.ShapeDtypeStruct(shape, pieces[0].dtype), jax.ShapeDtypeStruct((8, LANES), jnp.float32)),
@@ -429,11 +434,6 @@
     def over_col(x, k):
         return lax.ppermute(x, "col", [(i, i ^ k) for i in range(C)])
 
-    def spread(stack, after):
-        parts = [stack] + [over_col(stack, k) for k in range(2, C, 2)]
-        mine, _ = pack("col", parts, 0, stack.shape[0], after)
-        return mine, over_col(mine, 1)
-
     cells = passage_tokens.reshape(local * count // TILE, TILE, width)
     tokens = [cells, over_col(cells, 1)]
     sent, blocks = prepare(
@@ -445,16 +445,24 @@
     begun = teacher(slots, ((0, (0,)),), megabytes=56, **common)
     score = teacher(slots, ((1, (0, 1)), (0, (1,))), after=(begun,), **common)
     base = sent.shape[0] - student_passages.shape[1] - block
-    vectors, token = pack("row", near, base, sent.shape[0] - base, (score,))
+    same = [[i for i in range(C) if i % 2 == odd] for odd in range(2)]
+    vectors, token = pack("row", near, base, sent.shape[0] - base, (score,), C // 2)
+    mine = lax.all_to_all(vectors, "col", 0, 0, axis_index_groups=same, tiled=True)
     priors = (score, begun)
     for k in range(2, R, 2):
-        score = teacher(slots, ((0, (k, k + 1)), (1, (k, k + 1))), priors=priors, after=(token,), **common)
+        copies = R if k == R - 2 else 0
+        score = teacher(
+            slots, ((0, (k, k + 1)), (1, (k, k + 1))), priors=priors, after=(token,), copies=copies, **common
+        )
         priors = (score,)
-    scores = [score] + [over_row(score, k) for k in range(1, R)]
-    stack, token = pack("row", scores, 0, local, ())
-    mine, other = spread(vectors, (token,))
+    stack = lax.all_to_all(score, "row", 0, 0, tiled=True)
+    mine, stack = lax.optimization_barrier((mine, stack))
+    other = over_col(mine, 1)
+    parts = [stack] + [over_col(stack, k) for k in range(2, C, 2)]
+    t_mine, token = pack("col", parts, 0, R, ())
+    t_mine = t_mine[0]
+    t_other = over_col(t_mine, 1)
     s, slope, vectors, stats = student_scores(mine, other, token, queries, wide)
-    t_mine, t_other = spread(stack, ())
     query_grads, passage_grads, loss = finish(t_mine, t_other, s, slope, mine, other, vectors, stats, wide)
     return (query_grads, passage_grads.T, loss[0, 0])
 

time: 58.8 us -> 68.1 us (1.16)
  blocking collectives: 0 us -> 23.8 us
  waiting for transfers between devices: 16.9 us -> 9.98 us
  starting transfers between devices: 15.8 us -> 9.33 us
  Pallas kernels: 24.2 us -> 23 us
    all_to_all x0 -> x2, blocking collectives: none -> 23.8 us  [the longest x1 13.6 us: shards(): lax.all_to_all(vectors, 'col', 0, 0, axis_index_groups=same, tiled=True)]
    ppermute x6 -> x3, waiting for transfers between devices: 12.7 us -> 6.38 us  [over_row(): return lax.ppermute(x, 'row', [(i, i ^ k) for i in range(R)])]
    ppermute x10 -> x7, starting transfers between devices: 7.57 us -> 4.08 us  [over_col(): return lax.ppermute(x, 'col', [(i, i ^ k) for i in range(C)])]
    ppermute x6 -> x3, starting transfers between devices: 8.23 us -> 5.25 us  [over_row(): return lax.ppermute(x, 'row', [(i, i ^ k) for i in range(R)])]
    pallas_call x4 -> x2, Pallas kernels: 1.3 us -> 0.16 us  [pack(): pl.pallas_call(functools.partial(pack_kernel, axis, first, count, len(pie...]
    ppermute x10 -> x7, waiting for transfers between devices: 4.2 us -> 3.6 us  [over_col(): return lax.ppermute(x, 'col', [(i, i ^ k) for i in range(C)])]
  transfers between devices with their start and end apart: 16 -> 10, of which waited for: 8 -> 5; matrix products, arithmetic and copies ran while one was open for 0% -> 0% of each run, Pallas kernels for 37% -> 21%
where the time goes in v2:
time: 68.1 us; the launch traced here: 67.6 us
  blocking collectives  23.8 us (35%)
  Pallas kernels  23 us (34%)
  waiting for transfers between devices  9.98 us (15%)
  starting transfers between devices  9.33 us (14%)
  between operations  0.76 us (1%)
  local copies, waits for them, and re-layouts  0.73 us (1%)
    pallas_call x3, Pallas kernels, teacher(): pl.pallas_call(functools.partial(teacher_kernel, slots, tasks, shifts, si...  17.4 us
    all_to_all x1, blocking collectives, shards(): lax.all_to_all(vectors, 'col', 0, 0, axis_index_groups=same, tiled=True)  13.6 us
    all_to_all x1, blocking collectives, shards(): stack = lax.all_to_all(score, 'row', 0, 0, tiled=True)  10.2 us
    ppermute x3, waiting for transfers between devices, over_row(): return lax.ppermute(x, 'row', [(i, i ^ k) for i in range(R)])  6.38 us
    ppermute x3, starting transfers between devices, over_row(): return lax.ppermute(x, 'row', [(i, i ^ k) for i in range(R)])  5.25 us
    ppermute x7, starting transfers between devices, over_col(): return lax.ppermute(x, 'col', [(i, i ^ k) for i in range(C)])  4.08 us
    ppermute x7, waiting for transfers between devices, over_col(): return lax.ppermute(x, 'col', [(i, i ^ k) for i in range(C)])  3.6 us
    pallas_call x1, Pallas kernels, prepare(): pl.pallas_call(functools.partial(prepare_kernel, slots, per), out_shape=(...  2.79 us
  transfers between devices with their start and end apart: 10, of which 5 were waited for; matrix products, arithmetic and copies ran while one was open for 0% of the time, Pallas kernels for 21%

profile of v2, /device:TPU:0, one launch (start us, length us, event | category | flops | bytes accessed | tf_op | source)
XLA Modules:
  0.0 67.6 jit_solution(11193475067187747092)
XLA Ops:
  0.6 0.5 collective-permute-start.3
  1.1 2.8 %shard_map.94 = (bf16[736,128]{1,0:T(8,128)(2,1)}, s32[401]{0:T(512)}) custom-call(bf16[32,32,128]{2,1,0:T(8,128)(2,1)} %tokens_ref.1, s32[32]{0:T(128)} %lives_ref.1, s32[32]{0:T(128)} %lengths_ref.1, bf16[32,96]{1,0:T(8,128)(2,1)} %sq_ref.1, bf16[192,128]{1,0:T(8,128)(2,1)} %bitcast.11, s32[32]{0:T(128)} %pos_ref.1), custom_call_target="tpu_custom_call" | custom-call | tf_op jit(solution)/shard_map/pallas_call | solution.py:95
  4.0 2.7 %collective-permute-start = (bf16[736,128]{1,0:T(8,128)(2,1)}, bf16[736,128]{1,0:T(8,128)(2,1)S(1)}, u32[]{:S(2)}, u32[]{:S(2)}) collective-permute-start(bf16[736,128]{1,0:T(8,128)(2,1)} %get-tuple-element.18.refs_0_), channel_id=1, source_target_pairs={{0,8},{8,0},{16,24},{24,16},{1,9},{9,1},{17,25},{25,17},{2,10},{10... | collective-permute-start | bytes 565256 | tf_op jit(solution)/shard_map/ppermute | solution.py:432
  6.6 2.5 %collective-permute-start.2 = (bf16[736,128]{1,0:T(8,128)(2,1)}, bf16[736,128]{1,0:T(8,128)(2,1)S(1)}, u32[]{:S(2)}, u32[]{:S(2)}) collective-permute-start(bf16[736,128]{1,0:T(8,128)(2,1)} %get-tuple-element.18.refs_0_), channel_id=1, source_target_pairs={{0,24},{8,16},{16,8},{24,0},{1,25},{9,17},{17,9},{25,1},{2,26},{10... | collective-permute-start | bytes 565256 | tf_op jit(solution)/shard_map/ppermute | solution.py:432
  9.1 0.1 collective-permute-start.1
  9.2 0.0 copy-start
  9.2 0.0 copy-start.1
  9.2 0.0 copy-start.2
  9.2 0.0 collective-permute-start.4
  9.2 4.2 %shard_map.95.refs_6_.refs_7_ = f32[32,128]{1,0:T(8,128)} custom-call(bf16[736,128]{1,0:T(8,128)(2,1)} %get-tuple-element.18.refs_0_, bf16[352,16,128]{2,1,0:T(8,128)(2,1)} %bitcast.8, s32[401]{0:T(512)} %get-tuple-element.19.refs_2_.refs_4_), custom_call_target="tpu_custom_call" | custom-call | flops 1476395008 | bytes 1441792 | tf_op jit(solution)/shard_map/pallas_call | solution.py:188
  13.5 0.0 collective-permute-done.4.refs_5_
  13.5 0.0 collective-permute-done.refs_1_
  13.5 0.0 collective-permute-done.3.refs_3_
  13.5 0.0 copy-done
  13.5 0.0 copy-done.1
  13.5 0.0 copy-done.2
  13.5 0.0 copy-start.3
  13.5 0.7 %copy-done.3 = f32[32,128]{1,0:T(8,128)S(1)} copy-done((f32[32,128]{1,0:T(8,128)S(1)}, f32[32,128]{1,0:T(8,128)}, u32[]{:S(2)}) %copy-start.3) | copy-done | bytes 16408
  14.2 0.0 copy-start.4
  14.2 6.0 %shard_map.96.refs_4_.refs_6_ = f32[32,128]{1,0:T(8,128)S(1)} custom-call(bf16[736,128]{1,0:T(8,128)(2,1)S(1)} %copy-done, bf16[736,128]{1,0:T(8,128)(2,1)S(1)} %collective-permute-done.refs_1_, bf16[352,16,128]{2,1,0:T(8,128)(2,1)S(1)} %bitcast.9, bf16[352,16,128]{2,1,0:T(8,128)(2,1)S(1)} %collective-permute-done.3.refs_3_, s32[401]{0:T(512)S(1)} %copy-done.2, ...), custom_call_target="tpu_custom_call" | custom-call | flops 4429185024 | bytes 2883584 | tf_op jit(solution)/shard_map/pallas_call | solution.py:188
  20.3 0.0 collective-permute-done.2.refs_3_.refs_1_
  20.3 6.4 %collective-permute-done.1.refs_2_.refs_0_ = bf16[736,128]{1,0:T(8,128)(2,1)S(1)} collective-permute-done((bf16[736,128]{1,0:T(8,128)(2,1)}, bf16[736,128]{1,0:T(8,128)(2,1)S(1)}, u32[]{:S(2)}, u32[]{:S(2)}) %collective-permute-start.1) | collective-permute-done | bytes 188448 | tf_op jit(solution)/shard_map/ppermute | solution.py:432
  26.7 0.1 shard_map.97
  26.8 0.0 copy-done.4
  26.8 7.1 %shard_map.98 = f32[4,32,128]{2,1,0:T(8,128)S(1)} custom-call(bf16[736,128]{1,0:T(8,128)(2,1)S(1)} %collective-permute-done.1.refs_2_.refs_0_, bf16[736,128]{1,0:T(8,128)(2,1)S(1)} %collective-permute-done.2.refs_3_.refs_1_, bf16[352,16,128]{2,1,0:T(8,128)(2,1)S(1)} %bitcast.10, bf16[352,16,128]{2,1,0:T(8,128)(2,1)S(1)} %collective-permute-done.3.refs_3_, ...), custom_call_target="tpu_custom_call" | custom-call | flops 5905580032 | bytes 2883584 | tf_op jit(solution)/shard_map/pallas_call | solution.py:188
  33.9 10.2 %all_to_all.10.refs_0_ = f32[4,32,128]{2,1,0:T(8,128)S(1)} all-to-all(f32[4,32,128]{2,1,0:T(8,128)S(1)} %shard_map.98), channel_id=1, replica_groups=mesh['row'=4,'col'=8] {'row'}, dimensions={0} | all-to-all | bytes 131072 | tf_op jit(solution)/shard_map/all_to_all | solution.py:458
  44.1 13.6 %all_to_all.11.mine_ref = bf16[4,4,224,128]{3,2,1,0:T(8,128)(2,1)S(1)} all-to-all(bf16[4,4,224,128]{3,2,1,0:T(8,128)(2,1)S(1)} %get-tuple-element.20), channel_id=1, replica_groups={{0,2,4,6},{1,3,5,7},{8,10,12,14},{9,11,13,15},{16,18,20,22},{17,19,21,2..., dimensions={0} | all-to-all | bytes 1835008 | tf_op jit(solution)/shard_map/all_to_all | solution.py:450
  57.7 0.0 collective-permute-start.9
  57.7 0.9 %collective-permute-start.7 = (f32[4,32,128]{2,1,0:T(8,128)S(1)}, f32[4,32,128]{2,1,0:T(8,128)S(1)}, u32[]{:S(2)}, u32[]{:S(2)}) collective-permute-start(f32[4,32,128]{2,1,0:T(8,128)S(1)} %all_to_all.10.refs_0_), channel_id=1, source_target_pairs={{0,6},{1,7},{2,4},{3,5},{4,2},{5,3},{6,0},{7,1},{8,14},{9,15},{10,... | collective-permute-start | bytes 196616 | tf_op jit(solution)/shard_map/ppermute | solution.py:435
  58.6 1.5 %collective-permute-start.6 = (f32[4,32,128]{2,1,0:T(8,128)S(1)}, f32[4,32,128]{2,1,0:T(8,128)S(1)}, u32[]{:S(2)}, u32[]{:S(2)}) collective-permute-start(f32[4,32,128]{2,1,0:T(8,128)S(1)} %all_to_all.10.refs_0_), channel_id=1, source_target_pairs={{0,4},{1,5},{2,6},{3,7},{4,0},{5,1},{6,2},{7,3},{8,12},{9,13},{10,... | collective-permute-start | bytes 196616 | tf_op jit(solution)/shard_map/ppermute | solution.py:435
  60.1 1.1 %collective-permute-start.5 = (f32[4,32,128]{2,1,0:T(8,128)S(1)}, f32[4,32,128]{2,1,0:T(8,128)S(1)}, u32[]{:S(2)}, u32[]{:S(2)}) collective-permute-start(f32[4,32,128]{2,1,0:T(8,128)S(1)} %all_to_all.10.refs_0_), channel_id=1, source_target_pairs={{0,2},{1,3},{2,0},{3,1},{4,6},{5,7},{6,4},{7,5},{8,10},{9,11},{10,... | collective-permute-start | bytes 196616 | tf_op jit(solution)/shard_map/ppermute | solution.py:435
  61.2 2.3 %collective-permute-done.7.refs_3_ = f32[4,32,128]{2,1,0:T(8,128)S(1)} collective-permute-done((f32[4,32,128]{2,1,0:T(8,128)S(1)}, f32[4,32,128]{2,1,0:T(8,128)S(1)}, u32[]{:S(2)}, u32[]{:S(2)}) %collective-permute-start.7) | collective-permute-done | bytes 65568 | tf_op jit(solution)/shard_map/ppermute | solution.py:435
  63.5 0.7 %collective-permute-done.6.refs_2_ = f32[4,32,128]{2,1,0:T(8,128)S(1)} collective-permute-done((f32[4,32,128]{2,1,0:T(8,128)S(1)}, f32[4,32,128]{2,1,0:T(8,128)S(1)}, u32[]{:S(2)}, u32[]{:S(2)}) %collective-permute-start.6) | collective-permute-done | bytes 65568 | tf_op jit(solution)/shard_map/ppermute | solution.py:435
  64.2 0.1 collective-permute-done.5.refs_1_
  64.4 0.1 collective-permute-start.8
  64.5 0.0 collective-permute-done.9.other_ref
  64.5 1.1 %shard_map.100 = (f32[8,128,128]{2,1,0:T(8,128)S(1)}, f32[8,128,128]{2,1,0:T(8,128)S(1)}, bf16[128,192]{1,0:T(8,128)(2,1)S(1)}, f32[8,128]{1,0:T(8,128)S(1)}) custom-call(bf16[4,4,224,128]{3,2,1,0:T(8,128)(2,1)S(1)} %all_to_all.11.mine_ref, bf16[4,4,224,128]{3,2,1,0:T(8,128)(2,1)S(1)} %collective-permute-done.9.other_ref, ...), custom_call_target="tpu_custom_call" | custom-call | tf_op jit(solution)/shard_map/pallas_call | solution.py:310
  65.5 0.4 collective-permute-done.8.t_other
  66.0 1.6 %shard_map.101 = (f32[32,96]{1,0:T(8,128)}, f32[192,128]{1,0:T(8,128)}, f32[1,1]{1,0:T(1,128)}) custom-call(f32[4,4,32,128]{3,2,1,0:T(8,128)S(1)} %bitcast.6, f32[4,4,32,128]{3,2,1,0:T(8,128)S(1)} %collective-permute-done.8.t_other, f32[8,128,128]{2,1,0:T(8,128)S(1)} %get-tuple-element.26.s_ref, f32[8,128,128]{2,1,0:T(8,128)S(1)} %get-tuple-element.27.slope_ref, ...), custom_call_target="tpu_custom_call" | custom-call | tf_op jit(solution)/shard_map/pallas_call | solution.py:410
  (1 shorter events, 0.0 us)
Async XLA Ops:
  0.6 12.8 %collective-permute-start.3 = (bf16[352,16,128]{2,1,0:T(8,128)(2,1)}, bf16[352,16,128]{2,1,0:T(8,128)(2,1)S(1)}, u32[]{:S(2)}, u32[]{:S(2)}) collective-permute-start(bf16[352,16,128]{2,1,0:T(8,128)(2,1)} %bitcast.7), channel_id=1, source_target_pairs={{0,1},{1,0},{2,3},{3,2},{4,5},{5,4},{6,7},{7,6},{8,9},{9,8},{10,11... | collective-permute-start | bytes 4325384 | tf_op jit(solution)/shard_map/ppermute | solution.py:435
  4.0 9.5 %collective-permute-start = (bf16[736,128]{1,0:T(8,128)(2,1)}, bf16[736,128]{1,0:T(8,128)(2,1)S(1)}, u32[]{:S(2)}, u32[]{:S(2)}) collective-permute-start(bf16[736,128]{1,0:T(8,128)(2,1)} %get-tuple-element.18.refs_0_), channel_id=1, source_target_pairs={{0,8},{8,0},{16,24},{24,16},{1,9},{9,1},{17,25},{25,17},{2,10},{10... | collective-permute-start | bytes 565256 | tf_op jit(solution)/shard_map/ppermute | solution.py:432
  6.6 13.7 %collective-permute-start.2 = (bf16[736,128]{1,0:T(8,128)(2,1)}, bf16[736,128]{1,0:T(8,128)(2,1)S(1)}, u32[]{:S(2)}, u32[]{:S(2)}) collective-permute-start(bf16[736,128]{1,0:T(8,128)(2,1)} %get-tuple-element.18.refs_0_), channel_id=1, source_target_pairs={{0,24},{8,16},{16,8},{24,0},{1,25},{9,17},{17,9},{25,1},{2,26},{10... | collective-permute-start | bytes 565256 | tf_op jit(solution)/shard_map/ppermute | solution.py:432
  9.1 17.6 %collective-permute-start.1 = (bf16[736,128]{1,0:T(8,128)(2,1)}, bf16[736,128]{1,0:T(8,128)(2,1)S(1)}, u32[]{:S(2)}, u32[]{:S(2)}) collective-permute-start(bf16[736,128]{1,0:T(8,128)(2,1)} %get-tuple-element.18.refs_0_), channel_id=1, source_target_pairs={{0,16},{8,24},{16,0},{24,8},{1,17},{9,25},{17,1},{25,9},{2,18},{10... | collective-permute-start | bytes 565256 | tf_op jit(solution)/shard_map/ppermute | solution.py:432
  9.2 4.3 %copy-start = (bf16[736,128]{1,0:T(8,128)(2,1)S(1)}, bf16[736,128]{1,0:T(8,128)(2,1)}, u32[]{:S(2)}) copy-start(bf16[736,128]{1,0:T(8,128)(2,1)} %get-tuple-element.18.refs_0_) | copy-start | bytes 565252
  9.2 4.3 %copy-start.1 = (bf16[32,176,128]{2,1,0:T(8,128)(2,1)S(1)}, bf16[32,176,128]{2,1,0:T(8,128)(2,1)}, u32[]{:S(2)}) copy-start(bf16[32,176,128]{2,1,0:T(8,128)(2,1)} %param.9) | copy-start | bytes 4325380
  9.2 4.3 %copy-start.2 = (s32[401]{0:T(512)S(1)}, s32[401]{0:T(512)}, u32[]{:S(2)}) copy-start(s32[401]{0:T(512)} %get-tuple-element.19.refs_2_.refs_4_) | copy-start | bytes 4816
  9.2 4.2 %collective-permute-start.4 = (s32[401]{0:T(512)}, s32[401]{0:T(512)S(1)}, u32[]{:S(2)}, u32[]{:S(2)}) collective-permute-start(s32[401]{0:T(512)} %get-tuple-element.19.refs_2_.refs_4_), channel_id=1, source_target_pairs={{0,1},{1,0},{2,3},{3,2},{4,5},{5,4},{6,7},{7,6},{8,9},{9,8},{10,11... | collective-permute-start | bytes 4820 | tf_op jit(solution)/shard_map/ppermute | solution.py:435
  13.5 0.7 %copy-start.3 = (f32[32,128]{1,0:T(8,128)S(1)}, f32[32,128]{1,0:T(8,128)}, u32[]{:S(2)}) copy-start(f32[32,128]{1,0:T(8,128)} %shard_map.95.refs_6_.refs_7_) | copy-start | bytes 49156
  14.2 12.6 %copy-start.4 = (f32[32,128]{1,0:T(8,128)S(1)}, f32[32,128]{1,0:T(8,128)}, u32[]{:S(2)}) copy-start(f32[32,128]{1,0:T(8,128)} %shard_map.95.refs_6_.refs_7_) | copy-start | bytes 49156
  57.7 6.8 %collective-permute-start.9 = (bf16[4,4,224,128]{3,2,1,0:T(8,128)(2,1)S(1)}, bf16[4,4,224,128]{3,2,1,0:T(8,128)(2,1)S(1)}, u32[]{:S(2)}, u32[]{:S(2)}) collective-permute-start(bf16[4,4,224,128]{3,2,1,0:T(8,128)(2,1)S(1)} %all_to_all.11.mine_ref), channel_id=1, source_target_pairs={{0,1},{1,0},{2,3},{3,2},{4,5},{5,4},{6,7},{7,6},{8,9},{9,8},{10,11... | collective-permute-start | bytes 2752520 | tf_op jit(solution)/shard_map/ppermute | solution.py:435
  57.7 5.8 %collective-permute-start.7 = (f32[4,32,128]{2,1,0:T(8,128)S(1)}, f32[4,32,128]{2,1,0:T(8,128)S(1)}, u32[]{:S(2)}, u32[]{:S(2)}) collective-permute-start(f32[4,32,128]{2,1,0:T(8,128)S(1)} %all_to_all.10.refs_0_), channel_id=1, source_target_pairs={{0,6},{1,7},{2,4},{3,5},{4,2},{5,3},{6,0},{7,1},{8,14},{9,15},{10,... | collective-permute-start | bytes 196616 | tf_op jit(solution)/shard_map/ppermute | solution.py:435
  58.6 5.6 %collective-permute-start.6 = (f32[4,32,128]{2,1,0:T(8,128)S(1)}, f32[4,32,128]{2,1,0:T(8,128)S(1)}, u32[]{:S(2)}, u32[]{:S(2)}) collective-permute-start(f32[4,32,128]{2,1,0:T(8,128)S(1)} %all_to_all.10.refs_0_), channel_id=1, source_target_pairs={{0,4},{1,5},{2,6},{3,7},{4,0},{5,1},{6,2},{7,3},{8,12},{9,13},{10,... | collective-permute-start | bytes 196616 | tf_op jit(solution)/shard_map/ppermute | solution.py:435
  60.1 4.3 %collective-permute-start.5 = (f32[4,32,128]{2,1,0:T(8,128)S(1)}, f32[4,32,128]{2,1,0:T(8,128)S(1)}, u32[]{:S(2)}, u32[]{:S(2)}) collective-permute-start(f32[4,32,128]{2,1,0:T(8,128)S(1)} %all_to_all.10.refs_0_), channel_id=1, source_target_pairs={{0,2},{1,3},{2,0},{3,1},{4,6},{5,7},{6,4},{7,5},{8,10},{9,11},{10,... | collective-permute-start | bytes 196616 | tf_op jit(solution)/shard_map/ppermute | solution.py:435
  64.4 1.6 %collective-permute-start.8 = (f32[4,4,32,128]{3,2,1,0:T(8,128)S(1)}, f32[4,4,32,128]{3,2,1,0:T(8,128)S(1)}, u32[]{:S(2)}, u32[]{:S(2)}) collective-permute-start(f32[4,4,32,128]{3,2,1,0:T(8,128)S(1)} %bitcast.5), channel_id=1, source_target_pairs={{0,1},{1,0},{2,3},{3,2},{4,5},{5,4},{6,7},{7,6},{8,9},{9,8},{10,11... | collective-permute-start | bytes 786440 | tf_op jit(solution)/shard_map/ppermute | solution.py:435

commit v3 on v1

--- a/solution.py
+++ b/solution.py
@@ -44,7 +44,7 @@
 
 
 def prepare_kernel(
-    slots, per, tokens_ref, lives_ref, lengths_ref, sq_ref, sp_ref, pos_ref, sent_ref, blocks_ref
+    slots, tokens_ref, lives_ref, sq_ref, sp_ref, pos_ref, sent_ref
 ):
     c = lax.axis_index("col")
     half = tokens_ref.shape[0] // 2
@@ -59,19 +59,6 @@
             values.append(jnp.where(slot < lives_ref[at], value, 0.0))
         flipped = jnp.concatenate(values, axis=0).T
         sent_ref[j * width : (j + 1) * width, :] = flipped.astype(jnp.bfloat16)
-    passages = lengths_ref.shape[0]
-
-    def entries(p, at):
-        for b in range(per):
-            live = jnp.minimum(lengths_ref[p] - b * TILE, TILE) - 1
-            blocks_ref[at + b] = p * TILE * TILE + b * TILE + live
-        return at + lax.shift_right_logical(lengths_ref[p] + TILE - 1, 4)
-
-    count = lax.fori_loop(0, passages, entries, 0)
-    final = blocks_ref[count - 1]
-    for i in range(GROUP):
-        blocks_ref[count + i] = final
-    blocks_ref[blocks_ref.shape[0] - 1] = count
     block, wide = sq_ref.shape
     base = half // some * width
     depth = sp_ref.shape[0]
@@ -88,20 +75,42 @@
     sent_ref[base + depth :] = vectors
 
 
-def prepare(tokens, lives, cells, lengths, sq, sp, pos):
-    per = cells.shape[0] // lengths.shape[0]
+def prepare(tokens, lives, sq, sp, pos):
     block, slots, width = tokens.shape
     base = block // 2 * slots // LANES * width
     return pl.pallas_call(
-        functools.partial(prepare_kernel, slots, per),
-        out_shape=(
-            jax.ShapeDtypeStruct((base + sp.shape[0] + block, LANES), jnp.bfloat16),
-            jax.ShapeDtypeStruct((cells.shape[0] + TILE + GROUP + 1,), jnp.int32),
-        ),
-        in_specs=[vmem(), smem(), smem(), vmem(), vmem(), smem()],
-        out_specs=(vmem(), smem()),
+        functools.partial(prepare_kernel, slots),
+        out_shape=jax.ShapeDtypeStruct((base + sp.shape[0] + block, LANES), jnp.bfloat16),
+        in_specs=[vmem(), smem(), vmem(), vmem(), smem()],
+        out_specs=vmem(),
         compiler_params=params(56),
-    )(tokens, lives, lengths, sq, sp, pos)
+    )(tokens, lives, sq, sp, pos)
+
+
+def blocks_kernel(per, lengths_ref, after_ref, blocks_ref):
+    passages = lengths_ref.shape[0]
+
+    def entries(p, at):
+        for b in range(per):
+            live = jnp.minimum(lengths_ref[p] - b * TILE, TILE) - 1
+            blocks_ref[at + b] = p * TILE * TILE + b * TILE + live
+        return at + lax.shift_right_logical(lengths_ref[p] + TILE - 1, 4)
+
+    count = lax.fori_loop(0, passages, entries, 0)
+    final = blocks_ref[count - 1]
+    for i in range(GROUP):
+        blocks_ref[count + i] = final
+    blocks_ref[blocks_ref.shape[0] - 1] = count
+
+
+def live_blocks(lengths, per, after):
+    return pl.pallas_call(
+        functools.partial(blocks_kernel, per),
+        out_shape=jax.ShapeDtypeStruct((lengths.shape[0] * per + TILE + GROUP + 1,), jnp.int32),
+        in_specs=[smem(), place()],
+        out_specs=smem(),
+        compiler_params=params(56),
+    )(lengths, after)
 
 
 def teacher_kernel(slots, tasks, shifts, sides, priors, *refs):
@@ -429,32 +438,37 @@
     def over_col(x, k):
         return lax.ppermute(x, "col", [(i, i ^ k) for i in range(C)])
 
-    def spread(stack, after):
-        parts = [stack] + [over_col(stack, k) for k in range(2, C, 2)]
-        mine, _ = pack("col", parts, 0, stack.shape[0], after)
-        return mine, over_col(mine, 1)
-
     cells = passage_tokens.reshape(local * count // TILE, TILE, width)
     tokens = [cells, over_col(cells, 1)]
-    sent, blocks = prepare(
-        query_tokens, query_lengths, cells, passage_lengths, student_queries, student_passages.T, positives
-    )
+    sent = prepare(query_tokens, query_lengths, student_queries, student_passages.T, positives)
+    near = [sent] + [over_row(sent, k) for k in range(1, R)]
+    blocks = live_blocks(passage_lengths, count // TILE, sent)
     lists = [blocks, over_col(blocks, 1)]
-    near = [sent] + [over_row(sent, k) for k in range(1, R)]
-    common = dict(near=near, tokens=tokens, lists=lists, queries=queries, passages=local)
-    begun = teacher(slots, ((0, (0,)),), megabytes=56, **common)
-    score = teacher(slots, ((1, (0, 1)), (0, (1,))), after=(begun,), **common)
+    common = dict(tokens=tokens, lists=lists, queries=queries, passages=local)
+    begun = teacher(slots, ((0, (0,)),), near=near, megabytes=56, **common)
+    near[1], begun = lax.optimization_barrier((near[1], begun))
+    common["near"] = near
+    score = teacher(slots, ((1, (0, 1)), (0, (1,))), **common)
     base = sent.shape[0] - student_passages.shape[1] - block
     vectors, token = pack("row", near, base, sent.shape[0] - base, (score,))
+    parts = {0: vectors}
+    for k in range(2, C, 2):
+        if k & (k - 1) == 0:
+            parts[k] = over_col(vectors, k)
     priors = (score, begun)
     for k in range(2, R, 2):
         score = teacher(slots, ((0, (k, k + 1)), (1, (k, k + 1))), priors=priors, after=(token,), **common)
         priors = (score,)
-    scores = [score] + [over_row(score, k) for k in range(1, R)]
-    stack, token = pack("row", scores, 0, local, ())
-    mine, other = spread(vectors, (token,))
+    parts, score = lax.optimization_barrier((parts, score))
+    for k in range(2, C, 2):
+        if k not in parts:
+            parts[k] = over_col(parts[k & (k - 1)], k & -k)
+    stack, token = pack("row", [score] + [over_row(score, k) for k in range(1, R)], 0, local, ())
+    mine, _ = pack("col", [parts[k] for k in range(0, C, 2)], 0, R, (token,))
+    other = over_col(mine, 1)
+    t_mine, token = pack("col", [stack] + [over_col(stack, k) for k in range(2, C, 2)], 0, R, ())
+    t_other = over_col(t_mine, 1)
     s, slope, vectors, stats = student_scores(mine, other, token, queries, wide)
-    t_mine, t_other = spread(stack, ())
     query_grads, passage_grads, loss = finish(t_mine, t_other, s, slope, mine, other, vectors, stats, wide)
     return (query_grads, passage_grads.T, loss[0, 0])
 

time: 58.8 us -> 55.1 us (0.937)
  waiting for transfers between devices: 16.9 us -> 11.2 us
  starting transfers between devices: 15.8 us -> 17.4 us
  Pallas kernels: 24.2 us -> 25.4 us
  local copies, waits for them, and re-layouts: 0.73 us -> 0.02 us
    ppermute x6, waiting for transfers between devices: 12.7 us -> 7.24 us  [over_row(): return lax.ppermute(x, 'row', [(i, i ^ k) for i in range(R)])]
    ppermute x6, starting transfers between devices: 8.23 us -> 9.57 us  [over_row(): return lax.ppermute(x, 'row', [(i, i ^ k) for i in range(R)])]
    pallas_call x1 -> x2, Pallas kernels: 2.8 us -> 4.02 us  [the longest x1 2.24 us: live_blocks(): pl.pallas_call(functools.partial(blocks_kernel, per), out_shape=jax.Shape...]
    unnamed x10 -> x8, local copies, waits for them, and re-layouts: 0.73 us -> 0.02 us
    pallas_call x3, Pallas kernels: 17.4 us -> 18 us  [teacher(): pl.pallas_call(functools.partial(teacher_kernel, slots, tasks, shifts, si...]
  transfers between devices with their start and end apart: 16 -> 16, of which waited for: 8 -> 7; matrix products, arithmetic and copies ran while one was open for 0% -> 0% of each run, Pallas kernels for 37% -> 42%
where the time goes in v3:
time: 55.1 us; the launch traced here: 54.8 us
  Pallas kernels  25.4 us (46%)
  starting transfers between devices  17.4 us (32%)
  waiting for transfers between devices  11.2 us (20%)
  between operations  0.8 us (1%)
    pallas_call x3, Pallas kernels, teacher(): pl.pallas_call(functools.partial(teacher_kernel, slots, tasks, shifts, si...  18 us
    ppermute x6, starting transfers between devices, over_row(): return lax.ppermute(x, 'row', [(i, i ^ k) for i in range(R)])  9.57 us
    ppermute x10, starting transfers between devices, over_col(): return lax.ppermute(x, 'col', [(i, i ^ k) for i in range(C)])  7.84 us
    ppermute x6, waiting for transfers between devices, over_row(): return lax.ppermute(x, 'row', [(i, i ^ k) for i in range(R)])  7.24 us
    ppermute x10, waiting for transfers between devices, over_col(): return lax.ppermute(x, 'col', [(i, i ^ k) for i in range(C)])  3.91 us
    pallas_call x1, Pallas kernels, live_blocks(): pl.pallas_call(functools.partial(blocks_kernel, per), out_shape=jax.Shape...  2.24 us
    pallas_call x1, Pallas kernels, prepare(): pl.pallas_call(functools.partial(prepare_kernel, slots), out_shape=jax.Sh...  1.78 us
    pallas_call x1, Pallas kernels, finish(): pl.pallas_call(functools.partial(finish_kernel, wide), out_shape=(jax.Sha...  1.62 us
  transfers between devices with their start and end apart: 16, of which 7 were waited for; matrix products, arithmetic and copies ran while one was open for 0% of the time, Pallas kernels for 42%

profile of v3, /device:TPU:0, one launch (start us, length us, event | category | flops | bytes accessed | tf_op | source)
XLA Modules:
  0.0 54.8 jit_solution(17370703889338215652)
XLA Ops:
  0.6 0.5 collective-permute-start.3
  1.1 1.8 %shard_map.94.after_ref.refs_0_ = bf16[736,128]{1,0:T(8,128)(2,1)} custom-call(bf16[32,32,128]{2,1,0:T(8,128)(2,1)} %tokens_ref.1, s32[32]{0:T(128)} %lives_ref.1, bf16[32,96]{1,0:T(8,128)(2,1)} %sq_ref.1, bf16[192,128]{1,0:T(8,128)(2,1)} %bitcast.8, s32[32]{0:T(128)} %pos_ref.1), custom_call_target="tpu_custom_call" | custom-call | tf_op jit(solution)/shard_map/pallas_call | solution.py:81
  2.9 2.6 %collective-permute-start = (bf16[736,128]{1,0:T(8,128)(2,1)}, bf16[736,128]{1,0:T(8,128)(2,1)S(1)}, u32[]{:S(2)}, u32[]{:S(2)}) collective-permute-start(bf16[736,128]{1,0:T(8,128)(2,1)} %shard_map.94.after_ref.refs_0_), channel_id=1, source_target_pairs={{0,8},{8,0},{16,24},{24,16},{1,9},{9,1},{17,25},{25,17},{2,10},{10... | collective-permute-start | bytes 565256 | tf_op jit(solution)/shard_map/ppermute | solution.py:436
  5.5 2.5 %collective-permute-start.2 = (bf16[736,128]{1,0:T(8,128)(2,1)}, bf16[736,128]{1,0:T(8,128)(2,1)S(1)}, u32[]{:S(2)}, u32[]{:S(2)}) collective-permute-start(bf16[736,128]{1,0:T(8,128)(2,1)} %shard_map.94.after_ref.refs_0_), channel_id=1, source_target_pairs={{0,24},{8,16},{16,8},{24,0},{1,25},{9,17},{17,9},{25,1},{2,26},{10... | collective-permute-start | bytes 565256 | tf_op jit(solution)/shard_map/ppermute | solution.py:436
  8.0 0.1 collective-permute-start.1
  8.1 2.2 %shard_map.95.refs_2_.refs_4_ = s32[401]{0:T(512)} custom-call(s32[32]{0:T(128)} %lengths_ref.1, bf16[736,128]{1,0:T(8,128)(2,1)} %shard_map.94.after_ref.refs_0_), custom_call_target="tpu_custom_call" | custom-call | tf_op jit(solution)/shard_map/pallas_call | solution.py:107
  10.4 0.0 copy-start
  10.4 0.0 copy-start.1
  10.4 0.0 copy-start.2
  10.4 0.1 collective-permute-start.4
  10.5 4.4 %shard_map.96.refs_7_ = f32[32,128]{1,0:T(8,128)} custom-call(bf16[736,128]{1,0:T(8,128)(2,1)} %shard_map.94.after_ref.refs_0_, bf16[352,16,128]{2,1,0:T(8,128)(2,1)} %bitcast.5, s32[401]{0:T(512)} %shard_map.95.refs_2_.refs_4_), custom_call_target="tpu_custom_call" | custom-call | flops 1476395008 | bytes 1441792 | tf_op jit(solution)/shard_map/pallas_call | solution.py:193
  14.9 0.0 copy-start.3
  14.9 0.0 collective-permute-done.refs_1_
  14.9 0.0 collective-permute-done.4.refs_5_
  14.9 0.0 collective-permute-done.3.refs_3_
  14.9 0.0 copy-done
  14.9 0.0 copy-done.1
  14.9 0.0 copy-done.2
  14.9 6.2 %shard_map.97.refs_4_.refs_6_ = f32[32,128]{1,0:T(8,128)S(1)} custom-call(bf16[736,128]{1,0:T(8,128)(2,1)S(1)} %copy-done, bf16[736,128]{1,0:T(8,128)(2,1)S(1)} %collective-permute-done.refs_1_, bf16[352,16,128]{2,1,0:T(8,128)(2,1)S(1)} %bitcast.6, bf16[352,16,128]{2,1,0:T(8,128)(2,1)S(1)} %collective-permute-done.3.refs_3_, s32[401]{0:T(512)S(1)} %copy-done.1, ...), custom_call_target="tpu_custom_call" | custom-call | flops 4429185024 | bytes 2883584 | tf_op jit(solution)/shard_map/pallas_call | solution.py:193
  21.2 0.0 collective-permute-done.2.refs_3_.refs_1_
  21.2 4.4 %collective-permute-done.1.refs_2_.refs_0_ = bf16[736,128]{1,0:T(8,128)(2,1)S(1)} collective-permute-done((bf16[736,128]{1,0:T(8,128)(2,1)}, bf16[736,128]{1,0:T(8,128)(2,1)S(1)}, u32[]{:S(2)}, u32[]{:S(2)}) %collective-permute-start.1) | collective-permute-done | bytes 188448 | tf_op jit(solution)/shard_map/ppermute | solution.py:436
  25.6 1.6 %collective-permute-start.6 = (bf16[4,224,128]{2,1,0:T(8,128)(2,1)S(1)}, bf16[4,224,128]{2,1,0:T(8,128)(2,1)S(1)}, u32[]{:S(2)}, u32[]{:S(2)}) collective-permute-start(bf16[4,224,128]{2,1,0:T(8,128)(2,1)S(1)} %get-tuple-element.30.refs_0_), channel_id=1, source_target_pairs={{0,4},{1,5},{2,6},{3,7},{4,0},{5,1},{6,2},{7,3},{8,12},{9,13},{10,... | collective-permute-start | bytes 688136 | tf_op jit(solution)/shard_map/ppermute | solution.py:439
  27.2 1.5 %collective-permute-start.5 = (bf16[4,224,128]{2,1,0:T(8,128)(2,1)S(1)}, bf16[4,224,128]{2,1,0:T(8,128)(2,1)S(1)}, u32[]{:S(2)}, u32[]{:S(2)}) collective-permute-start(bf16[4,224,128]{2,1,0:T(8,128)(2,1)S(1)} %get-tuple-element.30.refs_0_), channel_id=1, source_target_pairs={{0,2},{1,3},{2,0},{3,1},{4,6},{5,7},{6,4},{7,5},{8,10},{9,11},{10,... | collective-permute-start | bytes 688136 | tf_op jit(solution)/shard_map/ppermute | solution.py:439
  28.7 0.0 copy-done.3
  28.7 7.4 %shard_map.99.refs_0_ = f32[32,128]{1,0:T(8,128)S(1)} custom-call(bf16[736,128]{1,0:T(8,128)(2,1)S(1)} %collective-permute-done.1.refs_2_.refs_0_, bf16[736,128]{1,0:T(8,128)(2,1)S(1)} %collective-permute-done.2.refs_3_.refs_1_, bf16[352,16,128]{2,1,0:T(8,128)(2,1)S(1)} %bitcast.7, bf16[352,16,128]{2,1,0:T(8,128)(2,1)S(1)} %collective-permute-done.3.refs_3_, ...), custom_call_target="tpu_custom_call" | custom-call | flops 5905580032 | bytes 2883584 | tf_op jit(solution)/shard_map/pallas_call | solution.py:193
  36.1 0.0 collective-permute-done.6.refs_2_
  36.1 0.0 collective-permute-done.5.refs_1_
  36.1 0.6 %collective-permute-start.14 = (bf16[4,224,128]{2,1,0:T(8,128)(2,1)S(1)}, bf16[4,224,128]{2,1,0:T(8,128)(2,1)S(1)}, u32[]{:S(2)}, u32[]{:S(2)}) collective-permute-start(bf16[4,224,128]{2,1,0:T(8,128)(2,1)S(1)} %collective-permute-done.6.refs_2_), channel_id=1, source_target_pairs={{0,2},{1,3},{2,0},{3,1},{4,6},{5,7},{6,4},{7,5},{8,10},{9,11},{10,... | collective-permute-start | bytes 688136 | tf_op jit(solution)/shard_map/ppermute | solution.py:439
  36.7 2.6 %collective-permute-start.9 = (f32[32,128]{1,0:T(8,128)S(1)}, f32[32,128]{1,0:T(8,128)S(1)}, u32[]{:S(2)}, u32[]{:S(2)}) collective-permute-start(f32[32,128]{1,0:T(8,128)S(1)} %shard_map.99.refs_0_), channel_id=1, source_target_pairs={{0,24},{8,16},{16,8},{24,0},{1,25},{9,17},{17,9},{25,1},{2,26},{10... | collective-permute-start | bytes 49160 | tf_op jit(solution)/shard_map/ppermute | solution.py:436
  39.3 0.0 collective-permute-start.8
  39.3 1.8 %collective-permute-start.7 = (f32[32,128]{1,0:T(8,128)S(1)}, f32[32,128]{1,0:T(8,128)S(1)}, u32[]{:S(2)}, u32[]{:S(2)}) collective-permute-start(f32[32,128]{1,0:T(8,128)S(1)} %shard_map.99.refs_0_), channel_id=1, source_target_pairs={{0,8},{8,0},{16,24},{24,16},{1,9},{9,1},{17,25},{25,17},{2,10},{10... | collective-permute-start | bytes 49160 | tf_op jit(solution)/shard_map/ppermute | solution.py:436
  41.1 1.1 %collective-permute-done.9.refs_3_ = f32[32,128]{1,0:T(8,128)S(1)} collective-permute-done((f32[32,128]{1,0:T(8,128)S(1)}, f32[32,128]{1,0:T(8,128)S(1)}, u32[]{:S(2)}, u32[]{:S(2)}) %collective-permute-start.9) | collective-permute-done | bytes 16416 | tf_op jit(solution)/shard_map/ppermute | solution.py:436
  42.2 1.7 %collective-permute-done.8.refs_2_ = f32[32,128]{1,0:T(8,128)S(1)} collective-permute-done((f32[32,128]{1,0:T(8,128)S(1)}, f32[32,128]{1,0:T(8,128)S(1)}, u32[]{:S(2)}, u32[]{:S(2)}) %collective-permute-start.8) | collective-permute-done | bytes 16416 | tf_op jit(solution)/shard_map/ppermute | solution.py:436
  43.9 0.0 collective-permute-done.7.refs_1_
  44.0 0.0 collective-permute-done.14.refs_3_
  44.0 0.7 %shard_map.102 = (bf16[4,4,224,128]{3,2,1,0:T(8,128)(2,1)S(1)}, f32[8,128]{1,0:T(8,128)}) custom-call(bf16[4,224,128]{2,1,0:T(8,128)(2,1)S(1)} %get-tuple-element.30.refs_0_, bf16[4,224,128]{2,1,0:T(8,128)(2,1)S(1)} %collective-permute-done.5.refs_1_, bf16[4,224,128]{2,1,0:T(8,128)(2,1)S(1)} %collective-permute-done.6.refs_2_, ...), custom_call_target="tpu_custom_call" | custom-call | tf_op jit(solution)/shard_map/pallas_call | solution.py:218
  44.6 0.0 collective-permute-start.15
  44.7 1.1 %collective-permute-start.12 = (f32[4,32,128]{2,1,0:T(8,128)S(1)}, f32[4,32,128]{2,1,0:T(8,128)S(1)}, u32[]{:S(2)}, u32[]{:S(2)}) collective-permute-start(f32[4,32,128]{2,1,0:T(8,128)S(1)} %get-tuple-element.28.refs_0_), channel_id=1, source_target_pairs={{0,6},{1,7},{2,4},{3,5},{4,2},{5,3},{6,0},{7,1},{8,14},{9,15},{10,... | collective-permute-start | bytes 196616 | tf_op jit(solution)/shard_map/ppermute | solution.py:439
  45.8 1.5 %collective-permute-start.11 = (f32[4,32,128]{2,1,0:T(8,128)S(1)}, f32[4,32,128]{2,1,0:T(8,128)S(1)}, u32[]{:S(2)}, u32[]{:S(2)}) collective-permute-start(f32[4,32,128]{2,1,0:T(8,128)S(1)} %get-tuple-element.28.refs_0_), channel_id=1, source_target_pairs={{0,4},{1,5},{2,6},{3,7},{4,0},{5,1},{6,2},{7,3},{8,12},{9,13},{10,... | collective-permute-start | bytes 196616 | tf_op jit(solution)/shard_map/ppermute | solution.py:439
  47.3 0.8 %collective-permute-start.10 = (f32[4,32,128]{2,1,0:T(8,128)S(1)}, f32[4,32,128]{2,1,0:T(8,128)S(1)}, u32[]{:S(2)}, u32[]{:S(2)}) collective-permute-start(f32[4,32,128]{2,1,0:T(8,128)S(1)} %get-tuple-element.28.refs_0_), channel_id=1, source_target_pairs={{0,2},{1,3},{2,0},{3,1},{4,6},{5,7},{6,4},{7,5},{8,10},{9,11},{10,... | collective-permute-start | bytes 196616 | tf_op jit(solution)/shard_map/ppermute | solution.py:439
  48.1 2.3 %collective-permute-done.12.refs_3_ = f32[4,32,128]{2,1,0:T(8,128)S(1)} collective-permute-done((f32[4,32,128]{2,1,0:T(8,128)S(1)}, f32[4,32,128]{2,1,0:T(8,128)S(1)}, u32[]{:S(2)}, u32[]{:S(2)}) %collective-permute-start.12) | collective-permute-done | bytes 65568 | tf_op jit(solution)/shard_map/ppermute | solution.py:439
  50.5 0.9 %collective-permute-done.11.refs_2_ = f32[4,32,128]{2,1,0:T(8,128)S(1)} collective-permute-done((f32[4,32,128]{2,1,0:T(8,128)S(1)}, f32[4,32,128]{2,1,0:T(8,128)S(1)}, u32[]{:S(2)}, u32[]{:S(2)}) %collective-permute-start.11) | collective-permute-done | bytes 65568 | tf_op jit(solution)/shard_map/ppermute | solution.py:439
  51.4 0.2 collective-permute-done.10.refs_1_
  51.6 0.1 collective-permute-start.13
  51.7 0.0 collective-permute-done.15.other_ref
  51.7 1.0 %shard_map.103 = (f32[8,128,128]{2,1,0:T(8,128)S(1)}, f32[8,128,128]{2,1,0:T(8,128)S(1)}, bf16[128,192]{1,0:T(8,128)(2,1)S(1)}, f32[8,128]{1,0:T(8,128)S(1)}) custom-call(bf16[4,4,224,128]{3,2,1,0:T(8,128)(2,1)S(1)} %get-tuple-element.34.mine_ref, bf16[4,4,224,128]{3,2,1,0:T(8,128)(2,1)S(1)} %collective-permute-done.15.other_ref, ...), custom_call_target="tpu_custom_call" | custom-call | tf_op jit(solution)/shard_map/pallas_call | solution.py:314
  52.8 0.5 collective-permute-done.13.t_other
  53.2 1.6 %shard_map.104 = (f32[32,96]{1,0:T(8,128)}, f32[192,128]{1,0:T(8,128)}, f32[1,1]{1,0:T(1,128)}) custom-call(f32[4,4,32,128]{3,2,1,0:T(8,128)S(1)} %get-tuple-element.29.t_mine, f32[4,4,32,128]{3,2,1,0:T(8,128)S(1)} %collective-permute-done.13.t_other, f32[8,128,128]{2,1,0:T(8,128)S(1)} %get-tuple-element.36.s_ref, ...), custom_call_target="tpu_custom_call" | custom-call | tf_op jit(solution)/shard_map/pallas_call | solution.py:414
  (3 shorter events, 0.1 us)
Async XLA Ops:
  0.6 14.3 %collective-permute-start.3 = (bf16[352,16,128]{2,1,0:T(8,128)(2,1)}, bf16[352,16,128]{2,1,0:T(8,128)(2,1)S(1)}, u32[]{:S(2)}, u32[]{:S(2)}) collective-permute-start(bf16[352,16,128]{2,1,0:T(8,128)(2,1)} %bitcast.4), channel_id=1, source_target_pairs={{0,1},{1,0},{2,3},{3,2},{4,5},{5,4},{6,7},{7,6},{8,9},{9,8},{10,11... | collective-permute-start | bytes 4325384 | tf_op jit(solution)/shard_map/ppermute | solution.py:439
  2.9 12.0 %collective-permute-start = (bf16[736,128]{1,0:T(8,128)(2,1)}, bf16[736,128]{1,0:T(8,128)(2,1)S(1)}, u32[]{:S(2)}, u32[]{:S(2)}) collective-permute-start(bf16[736,128]{1,0:T(8,128)(2,1)} %shard_map.94.after_ref.refs_0_), channel_id=1, source_target_pairs={{0,8},{8,0},{16,24},{24,16},{1,9},{9,1},{17,25},{25,17},{2,10},{10... | collective-permute-start | bytes 565256 | tf_op jit(solution)/shard_map/ppermute | solution.py:436
  5.5 15.7 %collective-permute-start.2 = (bf16[736,128]{1,0:T(8,128)(2,1)}, bf16[736,128]{1,0:T(8,128)(2,1)S(1)}, u32[]{:S(2)}, u32[]{:S(2)}) collective-permute-start(bf16[736,128]{1,0:T(8,128)(2,1)} %shard_map.94.after_ref.refs_0_), channel_id=1, source_target_pairs={{0,24},{8,16},{16,8},{24,0},{1,25},{9,17},{17,9},{25,1},{2,26},{10... | collective-permute-start | bytes 565256 | tf_op jit(solution)/shard_map/ppermute | solution.py:436
  8.0 17.6 %collective-permute-start.1 = (bf16[736,128]{1,0:T(8,128)(2,1)}, bf16[736,128]{1,0:T(8,128)(2,1)S(1)}, u32[]{:S(2)}, u32[]{:S(2)}) collective-permute-start(bf16[736,128]{1,0:T(8,128)(2,1)} %shard_map.94.after_ref.refs_0_), channel_id=1, source_target_pairs={{0,16},{8,24},{16,0},{24,8},{1,17},{9,25},{17,1},{25,9},{2,18},{10... | collective-permute-start | bytes 565256 | tf_op jit(solution)/shard_map/ppermute | solution.py:436
  10.4 4.5 %copy-start = (bf16[736,128]{1,0:T(8,128)(2,1)S(1)}, bf16[736,128]{1,0:T(8,128)(2,1)}, u32[]{:S(2)}) copy-start(bf16[736,128]{1,0:T(8,128)(2,1)} %shard_map.94.after_ref.refs_0_) | copy-start | bytes 565252
  10.4 4.5 %copy-start.1 = (s32[401]{0:T(512)S(1)}, s32[401]{0:T(512)}, u32[]{:S(2)}) copy-start(s32[401]{0:T(512)} %shard_map.95.refs_2_.refs_4_) | copy-start | bytes 4816
  10.4 4.5 %copy-start.2 = (bf16[32,176,128]{2,1,0:T(8,128)(2,1)S(1)}, bf16[32,176,128]{2,1,0:T(8,128)(2,1)}, u32[]{:S(2)}) copy-start(bf16[32,176,128]{2,1,0:T(8,128)(2,1)} %param.9) | copy-start | bytes 4325380
  10.4 4.5 %collective-permute-start.4 = (s32[401]{0:T(512)}, s32[401]{0:T(512)S(1)}, u32[]{:S(2)}, u32[]{:S(2)}) collective-permute-start(s32[401]{0:T(512)} %shard_map.95.refs_2_.refs_4_), channel_id=1, source_target_pairs={{0,1},{1,0},{2,3},{3,2},{4,5},{5,4},{6,7},{7,6},{8,9},{9,8},{10,11... | collective-permute-start | bytes 4820 | tf_op jit(solution)/shard_map/ppermute | solution.py:439
  14.9 13.8 %copy-start.3 = (f32[32,128]{1,0:T(8,128)S(1)}, f32[32,128]{1,0:T(8,128)}, u32[]{:S(2)}) copy-start(f32[32,128]{1,0:T(8,128)} %shard_map.96.refs_7_) | copy-start | bytes 49156
  25.6 10.5 %collective-permute-start.6 = (bf16[4,224,128]{2,1,0:T(8,128)(2,1)S(1)}, bf16[4,224,128]{2,1,0:T(8,128)(2,1)S(1)}, u32[]{:S(2)}, u32[]{:S(2)}) collective-permute-start(bf16[4,224,128]{2,1,0:T(8,128)(2,1)S(1)} %get-tuple-element.30.refs_0_), channel_id=1, source_target_pairs={{0,4},{1,5},{2,6},{3,7},{4,0},{5,1},{6,2},{7,3},{8,12},{9,13},{10,... | collective-permute-start | bytes 688136 | tf_op jit(solution)/shard_map/ppermute | solution.py:439
  27.2 8.9 %collective-permute-start.5 = (bf16[4,224,128]{2,1,0:T(8,128)(2,1)S(1)}, bf16[4,224,128]{2,1,0:T(8,128)(2,1)S(1)}, u32[]{:S(2)}, u32[]{:S(2)}) collective-permute-start(bf16[4,224,128]{2,1,0:T(8,128)(2,1)S(1)} %get-tuple-element.30.refs_0_), channel_id=1, source_target_pairs={{0,2},{1,3},{2,0},{3,1},{4,6},{5,7},{6,4},{7,5},{8,10},{9,11},{10,... | collective-permute-start | bytes 688136 | tf_op jit(solution)/shard_map/ppermute | solution.py:439
  36.1 7.9 %collective-permute-start.14 = (bf16[4,224,128]{2,1,0:T(8,128)(2,1)S(1)}, bf16[4,224,128]{2,1,0:T(8,128)(2,1)S(1)}, u32[]{:S(2)}, u32[]{:S(2)}) collective-permute-start(bf16[4,224,128]{2,1,0:T(8,128)(2,1)S(1)} %collective-permute-done.6.refs_2_), channel_id=1, source_target_pairs={{0,2},{1,3},{2,0},{3,1},{4,6},{5,7},{6,4},{7,5},{8,10},{9,11},{10,... | collective-permute-start | bytes 688136 | tf_op jit(solution)/shard_map/ppermute | solution.py:439
  36.7 5.5 %collective-permute-start.9 = (f32[32,128]{1,0:T(8,128)S(1)}, f32[32,128]{1,0:T(8,128)S(1)}, u32[]{:S(2)}, u32[]{:S(2)}) collective-permute-start(f32[32,128]{1,0:T(8,128)S(1)} %shard_map.99.refs_0_), channel_id=1, source_target_pairs={{0,24},{8,16},{16,8},{24,0},{1,25},{9,17},{17,9},{25,1},{2,26},{10... | collective-permute-start | bytes 49160 | tf_op jit(solution)/shard_map/ppermute | solution.py:436
  39.3 4.6 %collective-permute-start.8 = (f32[32,128]{1,0:T(8,128)S(1)}, f32[32,128]{1,0:T(8,128)S(1)}, u32[]{:S(2)}, u32[]{:S(2)}) collective-permute-start(f32[32,128]{1,0:T(8,128)S(1)} %shard_map.99.refs_0_), channel_id=1, source_target_pairs={{0,16},{8,24},{16,0},{24,8},{1,17},{9,25},{17,1},{25,9},{2,18},{10... | collective-permute-start | bytes 49160 | tf_op jit(solution)/shard_map/ppermute | solution.py:436
  39.3 4.6 %collective-permute-start.7 = (f32[32,128]{1,0:T(8,128)S(1)}, f32[32,128]{1,0:T(8,128)S(1)}, u32[]{:S(2)}, u32[]{:S(2)}) collective-permute-start(f32[32,128]{1,0:T(8,128)S(1)} %shard_map.99.refs_0_), channel_id=1, source_target_pairs={{0,8},{8,0},{16,24},{24,16},{1,9},{9,1},{17,25},{25,17},{2,10},{10... | collective-permute-start | bytes 49160 | tf_op jit(solution)/shard_map/ppermute | solution.py:436
  44.6 7.0 %collective-permute-start.15 = (bf16[4,4,224,128]{3,2,1,0:T(8,128)(2,1)S(1)}, bf16[4,4,224,128]{3,2,1,0:T(8,128)(2,1)S(1)}, u32[]{:S(2)}, u32[]{:S(2)}) collective-permute-start(bf16[4,4,224,128]{3,2,1,0:T(8,128)(2,1)S(1)} %get-tuple-element.34.mine_ref), channel_id=1, source_target_pairs={{0,1},{1,0},{2,3},{3,2},{4,5},{5,4},{6,7},{7,6},{8,9},{9,8},{10,11... | collective-permute-start | bytes 2752520 | tf_op jit(solution)/shard_map/ppermute | solution.py:439
  44.7 5.8 %collective-permute-start.12 = (f32[4,32,128]{2,1,0:T(8,128)S(1)}, f32[4,32,128]{2,1,0:T(8,128)S(1)}, u32[]{:S(2)}, u32[]{:S(2)}) collective-permute-start(f32[4,32,128]{2,1,0:T(8,128)S(1)} %get-tuple-element.28.refs_0_), channel_id=1, source_target_pairs={{0,6},{1,7},{2,4},{3,5},{4,2},{5,3},{6,0},{7,1},{8,14},{9,15},{10,... | collective-permute-start | bytes 196616 | tf_op jit(solution)/shard_map/ppermute | solution.py:439
  45.8 5.6 %collective-permute-start.11 = (f32[4,32,128]{2,1,0:T(8,128)S(1)}, f32[4,32,128]{2,1,0:T(8,128)S(1)}, u32[]{:S(2)}, u32[]{:S(2)}) collective-permute-start(f32[4,32,128]{2,1,0:T(8,128)S(1)} %get-tuple-element.28.refs_0_), channel_id=1, source_target_pairs={{0,4},{1,5},{2,6},{3,7},{4,0},{5,1},{6,2},{7,3},{8,12},{9,13},{10,... | collective-permute-start | bytes 196616 | tf_op jit(solution)/shard_map/ppermute | solution.py:439
  47.3 4.3 %collective-permute-start.10 = (f32[4,32,128]{2,1,0:T(8,128)S(1)}, f32[4,32,128]{2,1,0:T(8,128)S(1)}, u32[]{:S(2)}, u32[]{:S(2)}) collective-permute-start(f32[4,32,128]{2,1,0:T(8,128)S(1)} %get-tuple-element.28.refs_0_), channel_id=1, source_target_pairs={{0,2},{1,3},{2,0},{3,1},{4,6},{5,7},{6,4},{7,5},{8,10},{9,11},{10,... | collective-permute-start | bytes 196616 | tf_op jit(solution)/shard_map/ppermute | solution.py:439
  51.6 1.6 %collective-permute-start.13 = (f32[4,4,32,128]{3,2,1,0:T(8,128)S(1)}, f32[4,4,32,128]{3,2,1,0:T(8,128)S(1)}, u32[]{:S(2)}, u32[]{:S(2)}) collective-permute-start(f32[4,4,32,128]{3,2,1,0:T(8,128)S(1)} %get-tuple-element.29.t_mine), channel_id=1, source_target_pairs={{0,1},{1,0},{2,3},{3,2},{4,5},{5,4},{6,7},{7,6},{8,9},{9,8},{10,11... | collective-permute-start | bytes 786440 | tf_op jit(solution)/shard_map/ppermute | solution.py:439

commit v4 on v3

--- a/solution.py
+++ b/solution.py
@@ -91,10 +91,13 @@
     passages = lengths_ref.shape[0]
 
     def entries(p, at):
+        length = lengths_ref[p]
+        whole = p * TILE * TILE + TILE - 1
         for b in range(per):
-            live = jnp.minimum(lengths_ref[p] - b * TILE, TILE) - 1
-            blocks_ref[at + b] = p * TILE * TILE + b * TILE + live
-        return at + lax.shift_right_logical(lengths_ref[p] + TILE - 1, 4)
+            blocks_ref[at + b] = whole + b * TILE
+        after = at + lax.shift_right_logical(length + TILE - 1, 4)
+        blocks_ref[after - 1] = p * TILE * TILE + length - 1
+        return after
 
     count = lax.fori_loop(0, passages, entries, 0)
     final = blocks_ref[count - 1]
@@ -441,7 +444,9 @@
     cells = passage_tokens.reshape(local * count // TILE, TILE, width)
     tokens = [cells, over_col(cells, 1)]
     sent = prepare(query_tokens, query_lengths, student_queries, student_passages.T, positives)
-    near = [sent] + [over_row(sent, k) for k in range(1, R)]
+    near = [sent]
+    for k in range(1, R):
+        near.append(over_row(near[k & (k - 1)], k & -k))
     blocks = live_blocks(passage_lengths, count // TILE, sent)
     lists = [blocks, over_col(blocks, 1)]
     common = dict(tokens=tokens, lists=lists, queries=queries, passages=local)

time: 55.1 us -> 53.7 us (0.975)
  waiting for transfers between devices: 11.2 us -> 10.1 us
    ppermute x6, waiting for transfers between devices: 7.24 us -> 5.63 us  [over_row(): return lax.ppermute(x, 'row', [(i, i ^ k) for i in range(R)])]
    ppermute x10, waiting for transfers between devices: 3.91 us -> 4.51 us  [over_col(): return lax.ppermute(x, 'col', [(i, i ^ k) for i in range(C)])]
  transfers between devices with their start and end apart: 16 -> 16, of which waited for: 7 -> 8; matrix products, arithmetic and copies ran while one was open for 0% -> 0% of each run, Pallas kernels for 42% -> 42%
where the time goes in v4:
time: 53.7 us; the launch traced here: 53.6 us
  Pallas kernels  25 us (47%)
  starting transfers between devices  17.6 us (33%)
  waiting for transfers between devices  10.1 us (19%)
  between operations  0.79 us (1%)
    pallas_call x3, Pallas kernels, teacher(): pl.pallas_call(functools.partial(teacher_kernel, slots, tasks, shifts, si...  18 us
    ppermute x6, starting transfers between devices, over_row(): return lax.ppermute(x, 'row', [(i, i ^ k) for i in range(R)])  10 us
    ppermute x10, starting transfers between devices, over_col(): return lax.ppermute(x, 'col', [(i, i ^ k) for i in range(C)])  7.65 us
    ppermute x6, waiting for transfers between devices, over_row(): return lax.ppermute(x, 'row', [(i, i ^ k) for i in range(R)])  5.63 us
    ppermute x10, waiting for transfers between devices, over_col(): return lax.ppermute(x, 'col', [(i, i ^ k) for i in range(C)])  4.51 us
    pallas_call x1, Pallas kernels, prepare(): pl.pallas_call(functools.partial(prepare_kernel, slots), out_shape=jax.Sh...  1.78 us
    pallas_call x1, Pallas kernels, live_blocks(): pl.pallas_call(functools.partial(blocks_kernel, per), out_shape=jax.Shape...  1.77 us
    pallas_call x1, Pallas kernels, finish(): pl.pallas_call(functools.partial(finish_kernel, wide), out_shape=(jax.Sha...  1.63 us
  transfers between devices with their start and end apart: 16, of which 8 were waited for; matrix products, arithmetic and copies ran while one was open for 0% of the time, Pallas kernels for 42%

profile of v4, /device:TPU:0, one launch (start us, length us, event | category | flops | bytes accessed | tf_op | source)
XLA Modules:
  0.0 53.6 jit_solution(13583503487107284871)
XLA Ops:
  0.6 0.5 collective-permute-start.3
  1.1 1.8 %shard_map.94.after_ref.refs_0_ = bf16[736,128]{1,0:T(8,128)(2,1)} custom-call(bf16[32,32,128]{2,1,0:T(8,128)(2,1)} %tokens_ref.1, s32[32]{0:T(128)} %lives_ref.1, bf16[32,96]{1,0:T(8,128)(2,1)} %sq_ref.1, bf16[192,128]{1,0:T(8,128)(2,1)} %bitcast.8, s32[32]{0:T(128)} %pos_ref.1), custom_call_target="tpu_custom_call" | custom-call | tf_op jit(solution)/shard_map/pallas_call | solution.py:81
  2.9 2.6 %collective-permute-start = (bf16[736,128]{1,0:T(8,128)(2,1)}, bf16[736,128]{1,0:T(8,128)(2,1)S(1)}, u32[]{:S(2)}, u32[]{:S(2)}) collective-permute-start(bf16[736,128]{1,0:T(8,128)(2,1)} %shard_map.94.after_ref.refs_0_), channel_id=1, source_target_pairs={{0,8},{8,0},{16,24},{24,16},{1,9},{9,1},{17,25},{25,17},{2,10},{10... | collective-permute-start | bytes 565256 | tf_op jit(solution)/shard_map/ppermute | solution.py:439
  5.5 2.6 %collective-permute-start.1 = (bf16[736,128]{1,0:T(8,128)(2,1)}, bf16[736,128]{1,0:T(8,128)(2,1)S(1)}, u32[]{:S(2)}, u32[]{:S(2)}) collective-permute-start(bf16[736,128]{1,0:T(8,128)(2,1)} %shard_map.94.after_ref.refs_0_), channel_id=1, source_target_pairs={{0,16},{8,24},{16,0},{24,8},{1,17},{9,25},{17,1},{25,9},{2,18},{10... | collective-permute-start | bytes 565256 | tf_op jit(solution)/shard_map/ppermute | solution.py:439
  8.1 1.8 %shard_map.95.refs_2_.refs_4_ = s32[401]{0:T(512)} custom-call(s32[32]{0:T(128)} %lengths_ref.1, bf16[736,128]{1,0:T(8,128)(2,1)} %shard_map.94.after_ref.refs_0_), custom_call_target="tpu_custom_call" | custom-call | tf_op jit(solution)/shard_map/pallas_call | solution.py:110
  9.9 0.0 copy-start
  9.9 0.0 copy-start.1
  9.9 0.0 copy-start.2
  9.9 0.1 collective-permute-start.4
  10.0 4.4 %shard_map.96.refs_7_ = f32[32,128]{1,0:T(8,128)} custom-call(bf16[736,128]{1,0:T(8,128)(2,1)} %shard_map.94.after_ref.refs_0_, bf16[352,16,128]{2,1,0:T(8,128)(2,1)} %bitcast.5, s32[401]{0:T(512)} %shard_map.95.refs_2_.refs_4_), custom_call_target="tpu_custom_call" | custom-call | flops 1476395008 | bytes 1441792 | tf_op jit(solution)/shard_map/pallas_call | solution.py:196
  14.4 0.0 copy-start.3
  14.4 0.6 %collective-permute-done.refs_1_ = bf16[736,128]{1,0:T(8,128)(2,1)S(1)} collective-permute-done((bf16[736,128]{1,0:T(8,128)(2,1)}, bf16[736,128]{1,0:T(8,128)(2,1)S(1)}, u32[]{:S(2)}, u32[]{:S(2)}) %collective-permute-start) | collective-permute-done | bytes 188448 | tf_op jit(solution)/shard_map/ppermute | solution.py:439
  15.0 2.6 %collective-permute-done.1.refs_2_.refs_0_ = bf16[736,128]{1,0:T(8,128)(2,1)S(1)} collective-permute-done((bf16[736,128]{1,0:T(8,128)(2,1)}, bf16[736,128]{1,0:T(8,128)(2,1)S(1)}, u32[]{:S(2)}, u32[]{:S(2)}) %collective-permute-start.1) | collective-permute-done | bytes 188448 | tf_op jit(solution)/shard_map/ppermute | solution.py:439
  17.6 0.4 collective-permute-start.2
  18.0 0.0 collective-permute-done.4.refs_5_
  18.0 0.0 collective-permute-done.3.refs_3_
  18.0 0.0 copy-done
  18.0 0.0 copy-done.1
  18.0 0.0 copy-done.2
  18.0 6.2 %shard_map.97.refs_4_.refs_6_ = f32[32,128]{1,0:T(8,128)S(1)} custom-call(bf16[736,128]{1,0:T(8,128)(2,1)S(1)} %copy-done, bf16[736,128]{1,0:T(8,128)(2,1)S(1)} %collective-permute-done.refs_1_, bf16[352,16,128]{2,1,0:T(8,128)(2,1)S(1)} %bitcast.6, bf16[352,16,128]{2,1,0:T(8,128)(2,1)S(1)} %collective-permute-done.3.refs_3_, s32[401]{0:T(512)S(1)} %copy-done.1, ...), custom_call_target="tpu_custom_call" | custom-call | flops 4429185024 | bytes 2883584 | tf_op jit(solution)/shard_map/pallas_call | solution.py:196
  24.3 0.0 collective-permute-done.2.refs_3_.refs_1_
  24.3 1.4 %collective-permute-start.6 = (bf16[4,224,128]{2,1,0:T(8,128)(2,1)S(1)}, bf16[4,224,128]{2,1,0:T(8,128)(2,1)S(1)}, u32[]{:S(2)}, u32[]{:S(2)}) collective-permute-start(bf16[4,224,128]{2,1,0:T(8,128)(2,1)S(1)} %get-tuple-element.30.refs_0_), channel_id=1, source_target_pairs={{0,4},{1,5},{2,6},{3,7},{4,0},{5,1},{6,2},{7,3},{8,12},{9,13},{10,... | collective-permute-start | bytes 688136 | tf_op jit(solution)/shard_map/ppermute | solution.py:442
  25.7 1.7 %collective-permute-start.5 = (bf16[4,224,128]{2,1,0:T(8,128)(2,1)S(1)}, bf16[4,224,128]{2,1,0:T(8,128)(2,1)S(1)}, u32[]{:S(2)}, u32[]{:S(2)}) collective-permute-start(bf16[4,224,128]{2,1,0:T(8,128)(2,1)S(1)} %get-tuple-element.30.refs_0_), channel_id=1, source_target_pairs={{0,2},{1,3},{2,0},{3,1},{4,6},{5,7},{6,4},{7,5},{8,10},{9,11},{10,... | collective-permute-start | bytes 688136 | tf_op jit(solution)/shard_map/ppermute | solution.py:442
  27.4 0.0 copy-done.3
  27.4 7.4 %shard_map.99.refs_0_ = f32[32,128]{1,0:T(8,128)S(1)} custom-call(bf16[736,128]{1,0:T(8,128)(2,1)S(1)} %collective-permute-done.1.refs_2_.refs_0_, bf16[736,128]{1,0:T(8,128)(2,1)S(1)} %collective-permute-done.2.refs_3_.refs_1_, bf16[352,16,128]{2,1,0:T(8,128)(2,1)S(1)} %bitcast.7, bf16[352,16,128]{2,1,0:T(8,128)(2,1)S(1)} %collective-permute-done.3.refs_3_, ...), custom_call_target="tpu_custom_call" | custom-call | flops 5905580032 | bytes 2883584 | tf_op jit(solution)/shard_map/pallas_call | solution.py:196
  34.8 0.0 collective-permute-done.6.refs_2_
  34.8 0.0 collective-permute-done.5.refs_1_
  34.8 0.4 collective-permute-start.14
  35.3 2.2 %collective-permute-start.9 = (f32[32,128]{1,0:T(8,128)S(1)}, f32[32,128]{1,0:T(8,128)S(1)}, u32[]{:S(2)}, u32[]{:S(2)}) collective-permute-start(f32[32,128]{1,0:T(8,128)S(1)} %shard_map.99.refs_0_), channel_id=1, source_target_pairs={{0,24},{8,16},{16,8},{24,0},{1,25},{9,17},{17,9},{25,1},{2,26},{10... | collective-permute-start | bytes 49160 | tf_op jit(solution)/shard_map/ppermute | solution.py:439
  37.5 0.7 %collective-permute-start.8 = (f32[32,128]{1,0:T(8,128)S(1)}, f32[32,128]{1,0:T(8,128)S(1)}, u32[]{:S(2)}, u32[]{:S(2)}) collective-permute-start(f32[32,128]{1,0:T(8,128)S(1)} %shard_map.99.refs_0_), channel_id=1, source_target_pairs={{0,16},{8,24},{16,0},{24,8},{1,17},{9,25},{17,1},{25,9},{2,18},{10... | collective-permute-start | bytes 49160 | tf_op jit(solution)/shard_map/ppermute | solution.py:439
  38.2 1.5 %collective-permute-start.7 = (f32[32,128]{1,0:T(8,128)S(1)}, f32[32,128]{1,0:T(8,128)S(1)}, u32[]{:S(2)}, u32[]{:S(2)}) collective-permute-start(f32[32,128]{1,0:T(8,128)S(1)} %shard_map.99.refs_0_), channel_id=1, source_target_pairs={{0,8},{8,0},{16,24},{24,16},{1,9},{9,1},{17,25},{25,17},{2,10},{10... | collective-permute-start | bytes 49160 | tf_op jit(solution)/shard_map/ppermute | solution.py:439
  39.6 1.1 %collective-permute-done.9.refs_3_ = f32[32,128]{1,0:T(8,128)S(1)} collective-permute-done((f32[32,128]{1,0:T(8,128)S(1)}, f32[32,128]{1,0:T(8,128)S(1)}, u32[]{:S(2)}, u32[]{:S(2)}) %collective-permute-start.9) | collective-permute-done | bytes 16416 | tf_op jit(solution)/shard_map/ppermute | solution.py:439
  40.8 1.3 %collective-permute-done.8.refs_2_ = f32[32,128]{1,0:T(8,128)S(1)} collective-permute-done((f32[32,128]{1,0:T(8,128)S(1)}, f32[32,128]{1,0:T(8,128)S(1)}, u32[]{:S(2)}, u32[]{:S(2)}) %collective-permute-start.8) | collective-permute-done | bytes 16416 | tf_op jit(solution)/shard_map/ppermute | solution.py:439
  42.1 0.0 collective-permute-done.7.refs_1_
  42.1 0.0 collective-permute-done.14.refs_3_
  42.1 0.7 %shard_map.102 = (bf16[4,4,224,128]{3,2,1,0:T(8,128)(2,1)S(1)}, f32[8,128]{1,0:T(8,128)}) custom-call(bf16[4,224,128]{2,1,0:T(8,128)(2,1)S(1)} %get-tuple-element.30.refs_0_, bf16[4,224,128]{2,1,0:T(8,128)(2,1)S(1)} %collective-permute-done.5.refs_1_, bf16[4,224,128]{2,1,0:T(8,128)(2,1)S(1)} %collective-permute-done.6.refs_2_, ...), custom_call_target="tpu_custom_call" | custom-call | tf_op jit(solution)/shard_map/pallas_call | solution.py:221
  42.8 0.0 collective-permute-start.15
  42.8 1.4 %collective-permute-start.12 = (f32[4,32,128]{2,1,0:T(8,128)S(1)}, f32[4,32,128]{2,1,0:T(8,128)S(1)}, u32[]{:S(2)}, u32[]{:S(2)}) collective-permute-start(f32[4,32,128]{2,1,0:T(8,128)S(1)} %get-tuple-element.28.refs_0_), channel_id=1, source_target_pairs={{0,6},{1,7},{2,4},{3,5},{4,2},{5,3},{6,0},{7,1},{8,14},{9,15},{10,... | collective-permute-start | bytes 196616 | tf_op jit(solution)/shard_map/ppermute | solution.py:442
  44.2 1.8 %collective-permute-start.11 = (f32[4,32,128]{2,1,0:T(8,128)S(1)}, f32[4,32,128]{2,1,0:T(8,128)S(1)}, u32[]{:S(2)}, u32[]{:S(2)}) collective-permute-start(f32[4,32,128]{2,1,0:T(8,128)S(1)} %get-tuple-element.28.refs_0_), channel_id=1, source_target_pairs={{0,4},{1,5},{2,6},{3,7},{4,0},{5,1},{6,2},{7,3},{8,12},{9,13},{10,... | collective-permute-start | bytes 196616 | tf_op jit(solution)/shard_map/ppermute | solution.py:442
  46.1 0.2 collective-permute-start.10
  46.3 2.0 %collective-permute-done.12.refs_3_ = f32[4,32,128]{2,1,0:T(8,128)S(1)} collective-permute-done((f32[4,32,128]{2,1,0:T(8,128)S(1)}, f32[4,32,128]{2,1,0:T(8,128)S(1)}, u32[]{:S(2)}, u32[]{:S(2)}) %collective-permute-start.12) | collective-permute-done | bytes 65568 | tf_op jit(solution)/shard_map/ppermute | solution.py:442
  48.3 1.3 %collective-permute-done.11.refs_2_ = f32[4,32,128]{2,1,0:T(8,128)S(1)} collective-permute-done((f32[4,32,128]{2,1,0:T(8,128)S(1)}, f32[4,32,128]{2,1,0:T(8,128)S(1)}, u32[]{:S(2)}, u32[]{:S(2)}) %collective-permute-start.11) | collective-permute-done | bytes 65568 | tf_op jit(solution)/shard_map/ppermute | solution.py:442
  49.6 0.7 %collective-permute-done.10.refs_1_ = f32[4,32,128]{2,1,0:T(8,128)S(1)} collective-permute-done((f32[4,32,128]{2,1,0:T(8,128)S(1)}, f32[4,32,128]{2,1,0:T(8,128)S(1)}, u32[]{:S(2)}, u32[]{:S(2)}) %collective-permute-start.10) | collective-permute-done | bytes 65568 | tf_op jit(solution)/shard_map/ppermute | solution.py:442
  50.4 0.1 collective-permute-start.13
  50.5 0.0 collective-permute-done.15.other_ref
  50.5 1.0 %shard_map.103 = (f32[8,128,128]{2,1,0:T(8,128)S(1)}, f32[8,128,128]{2,1,0:T(8,128)S(1)}, bf16[128,192]{1,0:T(8,128)(2,1)S(1)}, f32[8,128]{1,0:T(8,128)S(1)}) custom-call(bf16[4,4,224,128]{3,2,1,0:T(8,128)(2,1)S(1)} %get-tuple-element.34.mine_ref, bf16[4,4,224,128]{3,2,1,0:T(8,128)(2,1)S(1)} %collective-permute-done.15.other_ref, ...), custom_call_target="tpu_custom_call" | custom-call | tf_op jit(solution)/shard_map/pallas_call | solution.py:317
  51.5 0.5 collective-permute-done.13.t_other
  52.0 1.6 %shard_map.104 = (f32[32,96]{1,0:T(8,128)}, f32[192,128]{1,0:T(8,128)}, f32[1,1]{1,0:T(1,128)}) custom-call(f32[4,4,32,128]{3,2,1,0:T(8,128)S(1)} %get-tuple-element.29.t_mine, f32[4,4,32,128]{3,2,1,0:T(8,128)S(1)} %collective-permute-done.13.t_other, f32[8,128,128]{2,1,0:T(8,128)S(1)} %get-tuple-element.36.s_ref, ...), custom_call_target="tpu_custom_call" | custom-call | tf_op jit(solution)/shard_map/pallas_call | solution.py:417
  (3 shorter events, 0.1 us)
Async XLA Ops:
  0.6 17.4 %collective-permute-start.3 = (bf16[352,16,128]{2,1,0:T(8,128)(2,1)}, bf16[352,16,128]{2,1,0:T(8,128)(2,1)S(1)}, u32[]{:S(2)}, u32[]{:S(2)}) collective-permute-start(bf16[352,16,128]{2,1,0:T(8,128)(2,1)} %bitcast.4), channel_id=1, source_target_pairs={{0,1},{1,0},{2,3},{3,2},{4,5},{5,4},{6,7},{7,6},{8,9},{9,8},{10,11... | collective-permute-start | bytes 4325384 | tf_op jit(solution)/shard_map/ppermute | solution.py:442
  2.9 12.1 %collective-permute-start = (bf16[736,128]{1,0:T(8,128)(2,1)}, bf16[736,128]{1,0:T(8,128)(2,1)S(1)}, u32[]{:S(2)}, u32[]{:S(2)}) collective-permute-start(bf16[736,128]{1,0:T(8,128)(2,1)} %shard_map.94.after_ref.refs_0_), channel_id=1, source_target_pairs={{0,8},{8,0},{16,24},{24,16},{1,9},{9,1},{17,25},{25,17},{2,10},{10... | collective-permute-start | bytes 565256 | tf_op jit(solution)/shard_map/ppermute | solution.py:439
  5.5 12.1 %collective-permute-start.1 = (bf16[736,128]{1,0:T(8,128)(2,1)}, bf16[736,128]{1,0:T(8,128)(2,1)S(1)}, u32[]{:S(2)}, u32[]{:S(2)}) collective-permute-start(bf16[736,128]{1,0:T(8,128)(2,1)} %shard_map.94.after_ref.refs_0_), channel_id=1, source_target_pairs={{0,16},{8,24},{16,0},{24,8},{1,17},{9,25},{17,1},{25,9},{2,18},{10... | collective-permute-start | bytes 565256 | tf_op jit(solution)/shard_map/ppermute | solution.py:439
  9.9 8.1 %copy-start = (bf16[736,128]{1,0:T(8,128)(2,1)S(1)}, bf16[736,128]{1,0:T(8,128)(2,1)}, u32[]{:S(2)}) copy-start(bf16[736,128]{1,0:T(8,128)(2,1)} %shard_map.94.after_ref.refs_0_) | copy-start | bytes 565252
  9.9 8.1 %copy-start.1 = (s32[401]{0:T(512)S(1)}, s32[401]{0:T(512)}, u32[]{:S(2)}) copy-start(s32[401]{0:T(512)} %shard_map.95.refs_2_.refs_4_) | copy-start | bytes 4816
  9.9 8.1 %copy-start.2 = (bf16[32,176,128]{2,1,0:T(8,128)(2,1)S(1)}, bf16[32,176,128]{2,1,0:T(8,128)(2,1)}, u32[]{:S(2)}) copy-start(bf16[32,176,128]{2,1,0:T(8,128)(2,1)} %param.9) | copy-start | bytes 4325380
  9.9 8.1 %collective-permute-start.4 = (s32[401]{0:T(512)}, s32[401]{0:T(512)S(1)}, u32[]{:S(2)}, u32[]{:S(2)}) collective-permute-start(s32[401]{0:T(512)} %shard_map.95.refs_2_.refs_4_), channel_id=1, source_target_pairs={{0,1},{1,0},{2,3},{3,2},{4,5},{5,4},{6,7},{7,6},{8,9},{9,8},{10,11... | collective-permute-start | bytes 4820 | tf_op jit(solution)/shard_map/ppermute | solution.py:442
  14.4 13.0 %copy-start.3 = (f32[32,128]{1,0:T(8,128)S(1)}, f32[32,128]{1,0:T(8,128)}, u32[]{:S(2)}) copy-start(f32[32,128]{1,0:T(8,128)} %shard_map.96.refs_7_) | copy-start | bytes 49156
  17.6 6.7 %collective-permute-start.2 = (bf16[736,128]{1,0:T(8,128)(2,1)S(1)}, bf16[736,128]{1,0:T(8,128)(2,1)S(1)}, u32[]{:S(2)}, u32[]{:S(2)}) collective-permute-start(bf16[736,128]{1,0:T(8,128)(2,1)S(1)} %collective-permute-done.1.refs_2_.refs_0_), channel_id=1, source_target_pairs={{0,8},{8,0},{16,24},{24,16},{1,9},{9,1},{17,25},{25,17},{2,10},{10... | collective-permute-start | bytes 565256 | tf_op jit(solution)/shard_map/ppermute | solution.py:439
  24.3 10.5 %collective-permute-start.6 = (bf16[4,224,128]{2,1,0:T(8,128)(2,1)S(1)}, bf16[4,224,128]{2,1,0:T(8,128)(2,1)S(1)}, u32[]{:S(2)}, u32[]{:S(2)}) collective-permute-start(bf16[4,224,128]{2,1,0:T(8,128)(2,1)S(1)} %get-tuple-element.30.refs_0_), channel_id=1, source_target_pairs={{0,4},{1,5},{2,6},{3,7},{4,0},{5,1},{6,2},{7,3},{8,12},{9,13},{10,... | collective-permute-start | bytes 688136 | tf_op jit(solution)/shard_map/ppermute | solution.py:442
  25.7 9.1 %collective-permute-start.5 = (bf16[4,224,128]{2,1,0:T(8,128)(2,1)S(1)}, bf16[4,224,128]{2,1,0:T(8,128)(2,1)S(1)}, u32[]{:S(2)}, u32[]{:S(2)}) collective-permute-start(bf16[4,224,128]{2,1,0:T(8,128)(2,1)S(1)} %get-tuple-element.30.refs_0_), channel_id=1, source_target_pairs={{0,2},{1,3},{2,0},{3,1},{4,6},{5,7},{6,4},{7,5},{8,10},{9,11},{10,... | collective-permute-start | bytes 688136 | tf_op jit(solution)/shard_map/ppermute | solution.py:442
  34.8 7.3 %collective-permute-start.14 = (bf16[4,224,128]{2,1,0:T(8,128)(2,1)S(1)}, bf16[4,224,128]{2,1,0:T(8,128)(2,1)S(1)}, u32[]{:S(2)}, u32[]{:S(2)}) collective-permute-start(bf16[4,224,128]{2,1,0:T(8,128)(2,1)S(1)} %collective-permute-done.6.refs_2_), channel_id=1, source_target_pairs={{0,2},{1,3},{2,0},{3,1},{4,6},{5,7},{6,4},{7,5},{8,10},{9,11},{10,... | collective-permute-start | bytes 688136 | tf_op jit(solution)/shard_map/ppermute | solution.py:442
  35.3 5.5 %collective-permute-start.9 = (f32[32,128]{1,0:T(8,128)S(1)}, f32[32,128]{1,0:T(8,128)S(1)}, u32[]{:S(2)}, u32[]{:S(2)}) collective-permute-start(f32[32,128]{1,0:T(8,128)S(1)} %shard_map.99.refs_0_), channel_id=1, source_target_pairs={{0,24},{8,16},{16,8},{24,0},{1,25},{9,17},{17,9},{25,1},{2,26},{10... | collective-permute-start | bytes 49160 | tf_op jit(solution)/shard_map/ppermute | solution.py:439
  37.5 4.6 %collective-permute-start.8 = (f32[32,128]{1,0:T(8,128)S(1)}, f32[32,128]{1,0:T(8,128)S(1)}, u32[]{:S(2)}, u32[]{:S(2)}) collective-permute-start(f32[32,128]{1,0:T(8,128)S(1)} %shard_map.99.refs_0_), channel_id=1, source_target_pairs={{0,16},{8,24},{16,0},{24,8},{1,17},{9,25},{17,1},{25,9},{2,18},{10... | collective-permute-start | bytes 49160 | tf_op jit(solution)/shard_map/ppermute | solution.py:439
  38.2 3.9 %collective-permute-start.7 = (f32[32,128]{1,0:T(8,128)S(1)}, f32[32,128]{1,0:T(8,128)S(1)}, u32[]{:S(2)}, u32[]{:S(2)}) collective-permute-start(f32[32,128]{1,0:T(8,128)S(1)} %shard_map.99.refs_0_), channel_id=1, source_target_pairs={{0,8},{8,0},{16,24},{24,16},{1,9},{9,1},{17,25},{25,17},{2,10},{10... | collective-permute-start | bytes 49160 | tf_op jit(solution)/shard_map/ppermute | solution.py:439
  42.8 7.7 %collective-permute-start.15 = (bf16[4,4,224,128]{3,2,1,0:T(8,128)(2,1)S(1)}, bf16[4,4,224,128]{3,2,1,0:T(8,128)(2,1)S(1)}, u32[]{:S(2)}, u32[]{:S(2)}) collective-permute-start(bf16[4,4,224,128]{3,2,1,0:T(8,128)(2,1)S(1)} %get-tuple-element.34.mine_ref), channel_id=1, source_target_pairs={{0,1},{1,0},{2,3},{3,2},{4,5},{5,4},{6,7},{7,6},{8,9},{9,8},{10,11... | collective-permute-start | bytes 2752520 | tf_op jit(solution)/shard_map/ppermute | solution.py:442
  42.8 5.5 %collective-permute-start.12 = (f32[4,32,128]{2,1,0:T(8,128)S(1)}, f32[4,32,128]{2,1,0:T(8,128)S(1)}, u32[]{:S(2)}, u32[]{:S(2)}) collective-permute-start(f32[4,32,128]{2,1,0:T(8,128)S(1)} %get-tuple-element.28.refs_0_), channel_id=1, source_target_pairs={{0,6},{1,7},{2,4},{3,5},{4,2},{5,3},{6,0},{7,1},{8,14},{9,15},{10,... | collective-permute-start | bytes 196616 | tf_op jit(solution)/shard_map/ppermute | solution.py:442
  44.2 5.4 %collective-permute-start.11 = (f32[4,32,128]{2,1,0:T(8,128)S(1)}, f32[4,32,128]{2,1,0:T(8,128)S(1)}, u32[]{:S(2)}, u32[]{:S(2)}) collective-permute-start(f32[4,32,128]{2,1,0:T(8,128)S(1)} %get-tuple-element.28.refs_0_), channel_id=1, source_target_pairs={{0,4},{1,5},{2,6},{3,7},{4,0},{5,1},{6,2},{7,3},{8,12},{9,13},{10,... | collective-permute-start | bytes 196616 | tf_op jit(solution)/shard_map/ppermute | solution.py:442
  46.1 4.3 %collective-permute-start.10 = (f32[4,32,128]{2,1,0:T(8,128)S(1)}, f32[4,32,128]{2,1,0:T(8,128)S(1)}, u32[]{:S(2)}, u32[]{:S(2)}) collective-permute-start(f32[4,32,128]{2,1,0:T(8,128)S(1)} %get-tuple-element.28.refs_0_), channel_id=1, source_target_pairs={{0,2},{1,3},{2,0},{3,1},{4,6},{5,7},{6,4},{7,5},{8,10},{9,11},{10,... | collective-permute-start | bytes 196616 | tf_op jit(solution)/shard_map/ppermute | solution.py:442
  50.4 1.6 %collective-permute-start.13 = (f32[4,4,32,128]{3,2,1,0:T(8,128)S(1)}, f32[4,4,32,128]{3,2,1,0:T(8,128)S(1)}, u32[]{:S(2)}, u32[]{:S(2)}) collective-permute-start(f32[4,4,32,128]{3,2,1,0:T(8,128)S(1)} %get-tuple-element.29.t_mine), channel_id=1, source_target_pairs={{0,1},{1,0},{2,3},{3,2},{4,5},{5,4},{6,7},{7,6},{8,9},{9,8},{10,11... | collective-permute-start | bytes 786440 | tf_op jit(solution)/shard_map/ppermute | solution.py:442

commit v5 on v4

--- a/solution.py
+++ b/solution.py
@@ -227,6 +227,26 @@
     )(*pieces, *after)
 
 
+def join_kernel(placed, first_ref, second_ref, out_ref, token_ref):
+    me = lax.axis_index("row") if placed else 0
+    count = first_ref.shape[0]
+    for i in range(count):
+        out_ref[me ^ i] = first_ref[i]
+        out_ref[me ^ (count + i)] = second_ref[i]
+    token_ref[...] = jnp.zeros(token_ref.shape, jnp.float32)
+
+
+def join(first, second, placed):
+    shape = (2 * first.shape[0],) + first.shape[1:]
+    return pl.pallas_call(
+        functools.partial(join_kernel, placed),
+        out_shape=(jax.ShapeDtypeStruct(shape, first.dtype), jax.ShapeDtypeStruct((8, LANES), jnp.float32)),
+        in_specs=[vmem()] * 2,
+        out_specs=(vmem(), vmem()),
+        compiler_params=params(24),
+    )(first, second)
+
+
 def loop(count, body, init):
     if count > 4:
         return lax.fori_loop(0, count, body, init)
@@ -451,9 +471,11 @@
     lists = [blocks, over_col(blocks, 1)]
     common = dict(tokens=tokens, lists=lists, queries=queries, passages=local)
     begun = teacher(slots, ((0, (0,)),), near=near, megabytes=56, **common)
-    near[1], begun = lax.optimization_barrier((near[1], begun))
+    tokens[1], begun = lax.optimization_barrier((tokens[1], begun))
     common["near"] = near
-    score = teacher(slots, ((1, (0, 1)), (0, (1,))), **common)
+    more = teacher(slots, ((1, (0,)),), **common)
+    near[1], more = lax.optimization_barrier((near[1], more))
+    score = teacher(slots, ((1, (1,)), (0, (1,))), priors=(more,), **common)
     base = sent.shape[0] - student_passages.shape[1] - block
     vectors, token = pack("row", near, base, sent.shape[0] - base, (score,))
     parts = {0: vectors}
@@ -468,7 +490,10 @@
     for k in range(2, C, 2):
         if k not in parts:
             parts[k] = over_col(parts[k & (k - 1)], k & -k)
-    stack, token = pack("row", [score] + [over_row(score, k) for k in range(1, R)], 0, local, ())
+    stack, bit = score[None], 1
+    while bit < R:
+        stack, token = join(stack, over_row(stack, bit), 2 * bit == R)
+        bit *= 2
     mine, _ = pack("col", [parts[k] for k in range(0, C, 2)], 0, R, (token,))
     other = over_col(mine, 1)
     t_mine, token = pack("col", [stack] + [over_col(stack, k) for k in range(2, C, 2)], 0, R, ())

time: 53.7 us -> 56.7 us (1.056)
  Pallas kernels: 25 us -> 27.1 us
  waiting for transfers between devices: 10.1 us -> 11.1 us
    ppermute x6 -> x5, waiting for transfers between devices: 5.63 us -> 7.33 us  [over_row(): return lax.ppermute(x, 'row', [(i, i ^ k) for i in range(R)])]
    pallas_call x3 -> x4, Pallas kernels: 18 us -> 19.5 us  [teacher(): pl.pallas_call(functools.partial(teacher_kernel, slots, tasks, shifts, si...]
    ppermute x10, waiting for transfers between devices: 4.51 us -> 3.72 us  [over_col(): return lax.ppermute(x, 'col', [(i, i ^ k) for i in range(C)])]
    pallas_call x0 -> x2, Pallas kernels: none -> 0.6 us  [join(): pl.pallas_call(functools.partial(join_kernel, placed), out_shape=(jax.Sha...]
    ppermute x6 -> x5, starting transfers between devices: 10 us -> 9.46 us  [over_row(): return lax.ppermute(x, 'row', [(i, i ^ k) for i in range(R)])]
  transfers between devices with their start and end apart: 16 -> 15, of which waited for: 8 -> 6; matrix products, arithmetic and copies ran while one was open for 0% -> 0% of each run, Pallas kernels for 42% -> 44%
where the time goes in v5:
time: 56.7 us; the launch traced here: 56.3 us
  Pallas kernels  27.1 us (48%)
  starting transfers between devices  17.3 us (31%)
  waiting for transfers between devices  11.1 us (20%)
  between operations  0.8 us (1%)
    pallas_call x4, Pallas kernels, teacher(): pl.pallas_call(functools.partial(teacher_kernel, slots, tasks, shifts, si...  19.5 us
    ppermute x5, starting transfers between devices, over_row(): return lax.ppermute(x, 'row', [(i, i ^ k) for i in range(R)])  9.46 us
    ppermute x10, starting transfers between devices, over_col(): return lax.ppermute(x, 'col', [(i, i ^ k) for i in range(C)])  7.81 us
    ppermute x5, waiting for transfers between devices, over_row(): return lax.ppermute(x, 'row', [(i, i ^ k) for i in range(R)])  7.33 us
    ppermute x10, waiting for transfers between devices, over_col(): return lax.ppermute(x, 'col', [(i, i ^ k) for i in range(C)])  3.72 us
    pallas_call x1, Pallas kernels, prepare(): pl.pallas_call(functools.partial(prepare_kernel, slots), out_shape=jax.Sh...  1.78 us
    pallas_call x1, Pallas kernels, live_blocks(): pl.pallas_call(functools.partial(blocks_kernel, per), out_shape=jax.Shape...  1.77 us
    pallas_call x1, Pallas kernels, finish(): pl.pallas_call(functools.partial(finish_kernel, wide), out_shape=(jax.Sha...  1.63 us
  transfers between devices with their start and end apart: 15, of which 6 were waited for; matrix products, arithmetic and copies ran while one was open for 0% of the time, Pallas kernels for 44%

profile of v5, /device:TPU:0, one launch (start us, length us, event | category | flops | bytes accessed | tf_op | source)
XLA Modules:
  0.0 56.3 jit_solution(4031646081467012241)
XLA Ops:
  0.6 0.5 collective-permute-start.1
  1.1 1.8 %shard_map.94.after_ref.refs_0_ = bf16[736,128]{1,0:T(8,128)(2,1)} custom-call(bf16[32,32,128]{2,1,0:T(8,128)(2,1)} %tokens_ref.1, s32[32]{0:T(128)} %lives_ref.1, bf16[32,96]{1,0:T(8,128)(2,1)} %sq_ref.1, bf16[192,128]{1,0:T(8,128)(2,1)} %bitcast.11, s32[32]{0:T(128)} %pos_ref.1), custom_call_target="tpu_custom_call" | custom-call | tf_op jit(solution)/shard_map/pallas_call | solution.py:81
  2.9 3.6 %collective-permute-start.3 = (bf16[736,128]{1,0:T(8,128)(2,1)}, bf16[736,128]{1,0:T(8,128)(2,1)S(1)}, u32[]{:S(2)}, u32[]{:S(2)}) collective-permute-start(bf16[736,128]{1,0:T(8,128)(2,1)} %shard_map.94.after_ref.refs_0_), channel_id=1, source_target_pairs={{0,16},{8,24},{16,0},{24,8},{1,17},{9,25},{17,1},{25,9},{2,18},{10... | collective-permute-start | bytes 565256 | tf_op jit(solution)/shard_map/ppermute | solution.py:459
  6.5 1.6 %collective-permute-start = (bf16[736,128]{1,0:T(8,128)(2,1)}, bf16[736,128]{1,0:T(8,128)(2,1)S(1)}, u32[]{:S(2)}, u32[]{:S(2)}) collective-permute-start(bf16[736,128]{1,0:T(8,128)(2,1)} %shard_map.94.after_ref.refs_0_), channel_id=1, source_target_pairs={{0,8},{8,0},{16,24},{24,16},{1,9},{9,1},{17,25},{25,17},{2,10},{10... | collective-permute-start | bytes 565256 | tf_op jit(solution)/shard_map/ppermute | solution.py:459
  8.1 1.8 %shard_map.95.refs_2_.refs_3_.refs_4_ = s32[401]{0:T(512)} custom-call(s32[32]{0:T(128)} %lengths_ref.1, bf16[736,128]{1,0:T(8,128)(2,1)} %shard_map.94.after_ref.refs_0_), custom_call_target="tpu_custom_call" | custom-call | tf_op jit(solution)/shard_map/pallas_call | solution.py:110
  9.9 0.0 copy-start
  9.9 0.1 collective-permute-start.2
  10.0 4.3 %shard_map.96.refs_7_ = f32[32,128]{1,0:T(8,128)} custom-call(bf16[736,128]{1,0:T(8,128)(2,1)} %shard_map.94.after_ref.refs_0_, bf16[352,16,128]{2,1,0:T(8,128)(2,1)} %bitcast.8, s32[401]{0:T(512)} %shard_map.95.refs_2_.refs_3_.refs_4_), custom_call_target="tpu_custom_call" | custom-call | flops 1476395008 | bytes 1441792 | tf_op jit(solution)/shard_map/pallas_call | solution.py:196
  14.3 0.0 copy-start.1
  14.3 0.0 copy-start.2
  14.3 2.0 %collective-permute-done.3.refs_2_.refs_0_ = bf16[736,128]{1,0:T(8,128)(2,1)S(1)} collective-permute-done((bf16[736,128]{1,0:T(8,128)(2,1)}, bf16[736,128]{1,0:T(8,128)(2,1)S(1)}, u32[]{:S(2)}, u32[]{:S(2)}) %collective-permute-start.3) | collective-permute-done | bytes 188448 | tf_op jit(solution)/shard_map/ppermute | solution.py:459
  16.3 0.7 %collective-permute-start.4 = (bf16[736,128]{1,0:T(8,128)(2,1)S(1)}, bf16[736,128]{1,0:T(8,128)(2,1)S(1)}, u32[]{:S(2)}, u32[]{:S(2)}) collective-permute-start(bf16[736,128]{1,0:T(8,128)(2,1)S(1)} %collective-permute-done.3.refs_2_.refs_0_), channel_id=1, source_target_pairs={{0,8},{8,0},{16,24},{24,16},{1,9},{9,1},{17,25},{25,17},{2,10},{10... | collective-permute-start | bytes 565256 | tf_op jit(solution)/shard_map/ppermute | solution.py:459
  17.0 0.0 collective-permute-done.1.refs_1_.refs_2_.refs_3_
  17.0 0.0 collective-permute-done.2.refs_2_.refs_4_.refs_5_
  17.0 0.0 copy-done
  17.0 2.8 %shard_map.97.refs_5_ = f32[32,128]{1,0:T(8,128)S(1)} custom-call(bf16[736,128]{1,0:T(8,128)(2,1)S(1)} %copy-done, bf16[352,16,128]{2,1,0:T(8,128)(2,1)S(1)} %collective-permute-done.1.refs_1_.refs_2_.refs_3_, s32[401]{0:T(512)S(1)} %collective-permute-done.2.refs_2_.refs_4_.refs_5_), custom_call_target="tpu_custom_call" | custom-call | flops 1476395008 | bytes 1441792 | tf_op jit(solution)/shard_map/pallas_call | solution.py:196
  19.8 0.0 copy-start.3
  19.8 0.0 collective-permute-done.refs_0_.refs_1_
  19.8 0.0 copy-done.1
  19.8 0.0 copy-done.2
  19.8 5.0 %shard_map.98.refs_4_.refs_6_ = f32[32,128]{1,0:T(8,128)S(1)} custom-call(bf16[736,128]{1,0:T(8,128)(2,1)S(1)} %collective-permute-done.refs_0_.refs_1_, bf16[352,16,128]{2,1,0:T(8,128)(2,1)S(1)} %bitcast.9, bf16[352,16,128]{2,1,0:T(8,128)(2,1)S(1)} %collective-permute-done.1.refs_1_.refs_2_.refs_3_, s32[401]{0:T(512)S(1)} %copy-done.1, ...), custom_call_target="tpu_custom_call" | custom-call | flops 2952790016 | bytes 2883584 | tf_op jit(solution)/shard_map/pallas_call | solution.py:196
  24.9 0.0 collective-permute-done.4.refs_3_.refs_1_
  24.9 1.6 %collective-permute-start.6 = (bf16[4,224,128]{2,1,0:T(8,128)(2,1)S(1)}, bf16[4,224,128]{2,1,0:T(8,128)(2,1)S(1)}, u32[]{:S(2)}, u32[]{:S(2)}) collective-permute-start(bf16[4,224,128]{2,1,0:T(8,128)(2,1)S(1)} %get-tuple-element.36.refs_0_), channel_id=1, source_target_pairs={{0,4},{1,5},{2,6},{3,7},{4,0},{5,1},{6,2},{7,3},{8,12},{9,13},{10,... | collective-permute-start | bytes 688136 | tf_op jit(solution)/shard_map/ppermute | solution.py:462
  26.5 1.3 %collective-permute-start.5 = (bf16[4,224,128]{2,1,0:T(8,128)(2,1)S(1)}, bf16[4,224,128]{2,1,0:T(8,128)(2,1)S(1)}, u32[]{:S(2)}, u32[]{:S(2)}) collective-permute-start(bf16[4,224,128]{2,1,0:T(8,128)(2,1)S(1)} %get-tuple-element.36.refs_0_), channel_id=1, source_target_pairs={{0,2},{1,3},{2,0},{3,1},{4,6},{5,7},{6,4},{7,5},{8,10},{9,11},{10,... | collective-permute-start | bytes 688136 | tf_op jit(solution)/shard_map/ppermute | solution.py:462
  27.8 0.0 copy-done.3
  27.9 7.4 %shard_map.100 = f32[32,128]{1,0:T(8,128)S(1)} custom-call(bf16[736,128]{1,0:T(8,128)(2,1)S(1)} %collective-permute-done.3.refs_2_.refs_0_, bf16[736,128]{1,0:T(8,128)(2,1)S(1)} %collective-permute-done.4.refs_3_.refs_1_, bf16[352,16,128]{2,1,0:T(8,128)(2,1)S(1)} %bitcast.10, bf16[352,16,128]{2,1,0:T(8,128)(2,1)S(1)} %collective-permute-done.1.refs_1_.refs_2_.refs_3_, ...), custom_call_target="tpu_custom_call" | custom-call | flops 5905580032 | bytes 2883584 | tf_op jit(solution)/shard_map/pallas_call | solution.py:196
  35.3 0.0 collective-permute-done.6.refs_2_
  35.3 0.0 collective-permute-done.5.refs_1_
  35.3 0.7 %collective-permute-start.13 = (bf16[4,224,128]{2,1,0:T(8,128)(2,1)S(1)}, bf16[4,224,128]{2,1,0:T(8,128)(2,1)S(1)}, u32[]{:S(2)}, u32[]{:S(2)}) collective-permute-start(bf16[4,224,128]{2,1,0:T(8,128)(2,1)S(1)} %collective-permute-done.6.refs_2_), channel_id=1, source_target_pairs={{0,2},{1,3},{2,0},{3,1},{4,6},{5,7},{6,4},{7,5},{8,10},{9,11},{10,... | collective-permute-start | bytes 688136 | tf_op jit(solution)/shard_map/ppermute | solution.py:462
  36.0 0.8 %collective-permute-start.7 = (f32[1,32,128]{2,1,0:T(8,128)S(1)}, f32[1,32,128]{2,1,0:T(8,128)S(1)}, u32[]{:S(2)}, u32[]{:S(2)}) collective-permute-start(f32[1,32,128]{2,1,0:T(8,128)S(1)} %bitcast.5), channel_id=1, source_target_pairs={{0,8},{8,0},{16,24},{24,16},{1,9},{9,1},{17,25},{25,17},{2,10},{10... | collective-permute-start | bytes 49160 | tf_op jit(solution)/shard_map/ppermute | solution.py:459
  36.8 3.0 %collective-permute-done.7.second_ref = f32[1,32,128]{2,1,0:T(8,128)S(1)} collective-permute-done((f32[1,32,128]{2,1,0:T(8,128)S(1)}, f32[1,32,128]{2,1,0:T(8,128)S(1)}, u32[]{:S(2)}, u32[]{:S(2)}) %collective-permute-start.7) | collective-permute-done | bytes 16416 | tf_op jit(solution)/shard_map/ppermute | solution.py:459
  39.8 0.6 %shard_map.101 = (f32[2,32,128]{2,1,0:T(8,128)S(1)}, f32[8,128]{1,0:T(8,128)}) custom-call(f32[1,32,128]{2,1,0:T(8,128)S(1)} %bitcast.6, f32[1,32,128]{2,1,0:T(8,128)S(1)} %collective-permute-done.7.second_ref), custom_call_target="tpu_custom_call" | custom-call | tf_op jit(solution)/shard_map/pallas_call | solution.py:241
  40.4 2.8 %collective-permute-start.8 = (f32[2,32,128]{2,1,0:T(8,128)S(1)}, f32[2,32,128]{2,1,0:T(8,128)S(1)}, u32[]{:S(2)}, u32[]{:S(2)}) collective-permute-start(f32[2,32,128]{2,1,0:T(8,128)S(1)} %get-tuple-element.33.first_ref), channel_id=1, source_target_pairs={{0,16},{8,24},{16,0},{24,8},{1,17},{9,25},{17,1},{25,9},{2,18},{10... | collective-permute-start | bytes 98312 | tf_op jit(solution)/shard_map/ppermute | solution.py:459
  43.2 2.4 %collective-permute-done.8.second_ref = f32[2,32,128]{2,1,0:T(8,128)S(1)} collective-permute-done((f32[2,32,128]{2,1,0:T(8,128)S(1)}, f32[2,32,128]{2,1,0:T(8,128)S(1)}, u32[]{:S(2)}, u32[]{:S(2)}) %collective-permute-start.8) | collective-permute-done | bytes 32800 | tf_op jit(solution)/shard_map/ppermute | solution.py:459
  45.5 0.0 collective-permute-done.13.refs_3_
  45.6 0.7 %shard_map.104 = (bf16[4,4,224,128]{3,2,1,0:T(8,128)(2,1)S(1)}, f32[8,128]{1,0:T(8,128)}) custom-call(bf16[4,224,128]{2,1,0:T(8,128)(2,1)S(1)} %get-tuple-element.36.refs_0_, bf16[4,224,128]{2,1,0:T(8,128)(2,1)S(1)} %collective-permute-done.5.refs_1_, bf16[4,224,128]{2,1,0:T(8,128)(2,1)S(1)} %collective-permute-done.6.refs_2_, ...), custom_call_target="tpu_custom_call" | custom-call | tf_op jit(solution)/shard_map/pallas_call | solution.py:221
  46.2 0.0 collective-permute-start.14
  46.2 1.1 %collective-permute-start.11 = (f32[4,32,128]{2,1,0:T(8,128)S(1)}, f32[4,32,128]{2,1,0:T(8,128)S(1)}, u32[]{:S(2)}, u32[]{:S(2)}) collective-permute-start(f32[4,32,128]{2,1,0:T(8,128)S(1)} %get-tuple-element.34.refs_0_), channel_id=1, source_target_pairs={{0,6},{1,7},{2,4},{3,5},{4,2},{5,3},{6,0},{7,1},{8,14},{9,15},{10,... | collective-permute-start | bytes 196616 | tf_op jit(solution)/shard_map/ppermute | solution.py:462
  47.4 1.3 %collective-permute-start.10 = (f32[4,32,128]{2,1,0:T(8,128)S(1)}, f32[4,32,128]{2,1,0:T(8,128)S(1)}, u32[]{:S(2)}, u32[]{:S(2)}) collective-permute-start(f32[4,32,128]{2,1,0:T(8,128)S(1)} %get-tuple-element.34.refs_0_), channel_id=1, source_target_pairs={{0,4},{1,5},{2,6},{3,7},{4,0},{5,1},{6,2},{7,3},{8,12},{9,13},{10,... | collective-permute-start | bytes 196616 | tf_op jit(solution)/shard_map/ppermute | solution.py:462
  48.7 1.0 %collective-permute-start.9 = (f32[4,32,128]{2,1,0:T(8,128)S(1)}, f32[4,32,128]{2,1,0:T(8,128)S(1)}, u32[]{:S(2)}, u32[]{:S(2)}) collective-permute-start(f32[4,32,128]{2,1,0:T(8,128)S(1)} %get-tuple-element.34.refs_0_), channel_id=1, source_target_pairs={{0,2},{1,3},{2,0},{3,1},{4,6},{5,7},{6,4},{7,5},{8,10},{9,11},{10,... | collective-permute-start | bytes 196616 | tf_op jit(solution)/shard_map/ppermute | solution.py:462
  49.7 2.3 %collective-permute-done.11.refs_3_ = f32[4,32,128]{2,1,0:T(8,128)S(1)} collective-permute-done((f32[4,32,128]{2,1,0:T(8,128)S(1)}, f32[4,32,128]{2,1,0:T(8,128)S(1)}, u32[]{:S(2)}, u32[]{:S(2)}) %collective-permute-start.11) | collective-permute-done | bytes 65568 | tf_op jit(solution)/shard_map/ppermute | solution.py:462
  52.1 0.9 %collective-permute-done.10.refs_2_ = f32[4,32,128]{2,1,0:T(8,128)S(1)} collective-permute-done((f32[4,32,128]{2,1,0:T(8,128)S(1)}, f32[4,32,128]{2,1,0:T(8,128)S(1)}, u32[]{:S(2)}, u32[]{:S(2)}) %collective-permute-start.10) | collective-permute-done | bytes 65568 | tf_op jit(solution)/shard_map/ppermute | solution.py:462
  53.0 0.0 collective-permute-done.9.refs_1_
  53.0 0.1 collective-permute-start.12
  53.1 0.0 collective-permute-done.14.other_ref
  53.1 1.1 %shard_map.105 = (f32[8,128,128]{2,1,0:T(8,128)S(1)}, f32[8,128,128]{2,1,0:T(8,128)S(1)}, bf16[128,192]{1,0:T(8,128)(2,1)S(1)}, f32[8,128]{1,0:T(8,128)S(1)}) custom-call(bf16[4,4,224,128]{3,2,1,0:T(8,128)(2,1)S(1)} %get-tuple-element.40.mine_ref, bf16[4,4,224,128]{3,2,1,0:T(8,128)(2,1)S(1)} %collective-permute-done.14.other_ref, ...), custom_call_target="tpu_custom_call" | custom-call | tf_op jit(solution)/shard_map/pallas_call | solution.py:337
  54.2 0.4 collective-permute-done.12.t_other
  54.6 1.6 %shard_map.106 = (f32[32,96]{1,0:T(8,128)}, f32[192,128]{1,0:T(8,128)}, f32[1,1]{1,0:T(1,128)}) custom-call(f32[4,4,32,128]{3,2,1,0:T(8,128)S(1)} %get-tuple-element.35.t_mine, f32[4,4,32,128]{3,2,1,0:T(8,128)S(1)} %collective-permute-done.12.t_other, f32[8,128,128]{2,1,0:T(8,128)S(1)} %get-tuple-element.42.s_ref, ...), custom_call_target="tpu_custom_call" | custom-call | tf_op jit(solution)/shard_map/pallas_call | solution.py:437
  (3 shorter events, 0.1 us)
Async XLA Ops:
  0.6 16.4 %collective-permute-start.1 = (bf16[352,16,128]{2,1,0:T(8,128)(2,1)}, bf16[352,16,128]{2,1,0:T(8,128)(2,1)S(1)}, u32[]{:S(2)}, u32[]{:S(2)}) collective-permute-start(bf16[352,16,128]{2,1,0:T(8,128)(2,1)} %bitcast.7), channel_id=1, source_target_pairs={{0,1},{1,0},{2,3},{3,2},{4,5},{5,4},{6,7},{7,6},{8,9},{9,8},{10,11... | collective-permute-start | bytes 4325384 | tf_op jit(solution)/shard_map/ppermute | solution.py:462
  2.9 13.3 %collective-permute-start.3 = (bf16[736,128]{1,0:T(8,128)(2,1)}, bf16[736,128]{1,0:T(8,128)(2,1)S(1)}, u32[]{:S(2)}, u32[]{:S(2)}) collective-permute-start(bf16[736,128]{1,0:T(8,128)(2,1)} %shard_map.94.after_ref.refs_0_), channel_id=1, source_target_pairs={{0,16},{8,24},{16,0},{24,8},{1,17},{9,25},{17,1},{25,9},{2,18},{10... | collective-permute-start | bytes 565256 | tf_op jit(solution)/shard_map/ppermute | solution.py:459
  6.5 13.3 %collective-permute-start = (bf16[736,128]{1,0:T(8,128)(2,1)}, bf16[736,128]{1,0:T(8,128)(2,1)S(1)}, u32[]{:S(2)}, u32[]{:S(2)}) collective-permute-start(bf16[736,128]{1,0:T(8,128)(2,1)} %shard_map.94.after_ref.refs_0_), channel_id=1, source_target_pairs={{0,8},{8,0},{16,24},{24,16},{1,9},{9,1},{17,25},{25,17},{2,10},{10... | collective-permute-start | bytes 565256 | tf_op jit(solution)/shard_map/ppermute | solution.py:459
  9.9 7.1 %copy-start = (bf16[736,128]{1,0:T(8,128)(2,1)S(1)}, bf16[736,128]{1,0:T(8,128)(2,1)}, u32[]{:S(2)}) copy-start(bf16[736,128]{1,0:T(8,128)(2,1)} %shard_map.94.after_ref.refs_0_) | copy-start | bytes 565252
  9.9 7.1 %collective-permute-start.2 = (s32[401]{0:T(512)}, s32[401]{0:T(512)S(1)}, u32[]{:S(2)}, u32[]{:S(2)}) collective-permute-start(s32[401]{0:T(512)} %shard_map.95.refs_2_.refs_3_.refs_4_), channel_id=1, source_target_pairs={{0,1},{1,0},{2,3},{3,2},{4,5},{5,4},{6,7},{7,6},{8,9},{9,8},{10,11... | collective-permute-start | bytes 4820 | tf_op jit(solution)/shard_map/ppermute | solution.py:462
  14.3 5.5 %copy-start.1 = (s32[401]{0:T(512)S(1)}, s32[401]{0:T(512)}, u32[]{:S(2)}) copy-start(s32[401]{0:T(512)} %shard_map.95.refs_2_.refs_3_.refs_4_) | copy-start | bytes 4816
  14.3 5.5 %copy-start.2 = (bf16[32,176,128]{2,1,0:T(8,128)(2,1)S(1)}, bf16[32,176,128]{2,1,0:T(8,128)(2,1)}, u32[]{:S(2)}) copy-start(bf16[32,176,128]{2,1,0:T(8,128)(2,1)} %param.9) | copy-start | bytes 4325380
  16.3 8.6 %collective-permute-start.4 = (bf16[736,128]{1,0:T(8,128)(2,1)S(1)}, bf16[736,128]{1,0:T(8,128)(2,1)S(1)}, u32[]{:S(2)}, u32[]{:S(2)}) collective-permute-start(bf16[736,128]{1,0:T(8,128)(2,1)S(1)} %collective-permute-done.3.refs_2_.refs_0_), channel_id=1, source_target_pairs={{0,8},{8,0},{16,24},{24,16},{1,9},{9,1},{17,25},{25,17},{2,10},{10... | collective-permute-start | bytes 565256 | tf_op jit(solution)/shard_map/ppermute | solution.py:459
  19.8 8.1 %copy-start.3 = (f32[32,128]{1,0:T(8,128)S(1)}, f32[32,128]{1,0:T(8,128)}, u32[]{:S(2)}) copy-start(f32[32,128]{1,0:T(8,128)} %shard_map.96.refs_7_) | copy-start | bytes 49156
  24.9 10.3 %collective-permute-start.6 = (bf16[4,224,128]{2,1,0:T(8,128)(2,1)S(1)}, bf16[4,224,128]{2,1,0:T(8,128)(2,1)S(1)}, u32[]{:S(2)}, u32[]{:S(2)}) collective-permute-start(bf16[4,224,128]{2,1,0:T(8,128)(2,1)S(1)} %get-tuple-element.36.refs_0_), channel_id=1, source_target_pairs={{0,4},{1,5},{2,6},{3,7},{4,0},{5,1},{6,2},{7,3},{8,12},{9,13},{10,... | collective-permute-start | bytes 688136 | tf_op jit(solution)/shard_map/ppermute | solution.py:462
  26.5 8.8 %collective-permute-start.5 = (bf16[4,224,128]{2,1,0:T(8,128)(2,1)S(1)}, bf16[4,224,128]{2,1,0:T(8,128)(2,1)S(1)}, u32[]{:S(2)}, u32[]{:S(2)}) collective-permute-start(bf16[4,224,128]{2,1,0:T(8,128)(2,1)S(1)} %get-tuple-element.36.refs_0_), channel_id=1, source_target_pairs={{0,2},{1,3},{2,0},{3,1},{4,6},{5,7},{6,4},{7,5},{8,10},{9,11},{10,... | collective-permute-start | bytes 688136 | tf_op jit(solution)/shard_map/ppermute | solution.py:462
  35.3 10.3 %collective-permute-start.13 = (bf16[4,224,128]{2,1,0:T(8,128)(2,1)S(1)}, bf16[4,224,128]{2,1,0:T(8,128)(2,1)S(1)}, u32[]{:S(2)}, u32[]{:S(2)}) collective-permute-start(bf16[4,224,128]{2,1,0:T(8,128)(2,1)S(1)} %collective-permute-done.6.refs_2_), channel_id=1, source_target_pairs={{0,2},{1,3},{2,0},{3,1},{4,6},{5,7},{6,4},{7,5},{8,10},{9,11},{10,... | collective-permute-start | bytes 688136 | tf_op jit(solution)/shard_map/ppermute | solution.py:462
  36.0 3.7 %collective-permute-start.7 = (f32[1,32,128]{2,1,0:T(8,128)S(1)}, f32[1,32,128]{2,1,0:T(8,128)S(1)}, u32[]{:S(2)}, u32[]{:S(2)}) collective-permute-start(f32[1,32,128]{2,1,0:T(8,128)S(1)} %bitcast.5), channel_id=1, source_target_pairs={{0,8},{8,0},{16,24},{24,16},{1,9},{9,1},{17,25},{25,17},{2,10},{10... | collective-permute-start | bytes 49160 | tf_op jit(solution)/shard_map/ppermute | solution.py:459
  40.4 5.2 %collective-permute-start.8 = (f32[2,32,128]{2,1,0:T(8,128)S(1)}, f32[2,32,128]{2,1,0:T(8,128)S(1)}, u32[]{:S(2)}, u32[]{:S(2)}) collective-permute-start(f32[2,32,128]{2,1,0:T(8,128)S(1)} %get-tuple-element.33.first_ref), channel_id=1, source_target_pairs={{0,16},{8,24},{16,0},{24,8},{1,17},{9,25},{17,1},{25,9},{2,18},{10... | collective-permute-start | bytes 98312 | tf_op jit(solution)/shard_map/ppermute | solution.py:459
  46.2 6.9 %collective-permute-start.14 = (bf16[4,4,224,128]{3,2,1,0:T(8,128)(2,1)S(1)}, bf16[4,4,224,128]{3,2,1,0:T(8,128)(2,1)S(1)}, u32[]{:S(2)}, u32[]{:S(2)}) collective-permute-start(bf16[4,4,224,128]{3,2,1,0:T(8,128)(2,1)S(1)} %get-tuple-element.40.mine_ref), channel_id=1, source_target_pairs={{0,1},{1,0},{2,3},{3,2},{4,5},{5,4},{6,7},{7,6},{8,9},{9,8},{10,11... | collective-permute-start | bytes 2752520 | tf_op jit(solution)/shard_map/ppermute | solution.py:462
  46.2 5.8 %collective-permute-start.11 = (f32[4,32,128]{2,1,0:T(8,128)S(1)}, f32[4,32,128]{2,1,0:T(8,128)S(1)}, u32[]{:S(2)}, u32[]{:S(2)}) collective-permute-start(f32[4,32,128]{2,1,0:T(8,128)S(1)} %get-tuple-element.34.refs_0_), channel_id=1, source_target_pairs={{0,6},{1,7},{2,4},{3,5},{4,2},{5,3},{6,0},{7,1},{8,14},{9,15},{10,... | collective-permute-start | bytes 196616 | tf_op jit(solution)/shard_map/ppermute | solution.py:462
  47.4 5.6 %collective-permute-start.10 = (f32[4,32,128]{2,1,0:T(8,128)S(1)}, f32[4,32,128]{2,1,0:T(8,128)S(1)}, u32[]{:S(2)}, u32[]{:S(2)}) collective-permute-start(f32[4,32,128]{2,1,0:T(8,128)S(1)} %get-tuple-element.34.refs_0_), channel_id=1, source_target_pairs={{0,4},{1,5},{2,6},{3,7},{4,0},{5,1},{6,2},{7,3},{8,12},{9,13},{10,... | collective-permute-start | bytes 196616 | tf_op jit(solution)/shard_map/ppermute | solution.py:462
  48.7 4.3 %collective-permute-start.9 = (f32[4,32,128]{2,1,0:T(8,128)S(1)}, f32[4,32,128]{2,1,0:T(8,128)S(1)}, u32[]{:S(2)}, u32[]{:S(2)}) collective-permute-start(f32[4,32,128]{2,1,0:T(8,128)S(1)} %get-tuple-element.34.refs_0_), channel_id=1, source_target_pairs={{0,2},{1,3},{2,0},{3,1},{4,6},{5,7},{6,4},{7,5},{8,10},{9,11},{10,... | collective-permute-start | bytes 196616 | tf_op jit(solution)/shard_map/ppermute | solution.py:462
  53.0 1.6 %collective-permute-start.12 = (f32[4,4,32,128]{3,2,1,0:T(8,128)S(1)}, f32[4,4,32,128]{3,2,1,0:T(8,128)S(1)}, u32[]{:S(2)}, u32[]{:S(2)}) collective-permute-start(f32[4,4,32,128]{3,2,1,0:T(8,128)S(1)} %get-tuple-element.35.t_mine), channel_id=1, source_target_pairs={{0,1},{1,0},{2,3},{3,2},{4,5},{5,4},{6,7},{7,6},{8,9},{9,8},{10,11... | collective-permute-start | bytes 786440 | tf_op jit(solution)/shard_map/ppermute | solution.py:462
